TPU v7x, 32 devices: a whole 2x2x4 slice. The times are simulated.
32 devices in a mesh: seq: 16 (over z, y, x), mp: 2 (over core).
Axes of the slice: x: 2, y: 2, z: 4, core: 2. Of those that a mesh axis runs over, the one named last changes fastest.
Arguments:
- tokens: bfloat16 [4, 4096, 512], P(None, 'seq'), may hold values from -6 to 6
- first_gain: float32 [512], replicated, may hold values from 0.5 to 1.5
- first_bias: float32 [512], replicated, may hold values from -3 to 3
- query_weight: bfloat16 [512, 512], P(None, 'mp'), may hold values from -0.25 to 0.25
- query_bias: float32 [512], P('mp'), may hold values from -3 to 3
- key_weight: bfloat16 [512, 512], P(None, 'mp'), may hold values from -0.25 to 0.25
- key_bias: float32 [512], P('mp'), may hold values from -3 to 3
- value_weight: bfloat16 [512, 512], P(None, 'mp'), may hold values from -0.25 to 0.25
- value_bias: float32 [512], P('mp'), may hold values from -3 to 3
- output_weight: bfloat16 [512, 512], P('mp'), may hold values from -1.5 to 1.5
- output_bias: float32 [512], replicated, may hold values from -3 to 3
- second_gain: float32 [512], replicated, may hold values from 0.5 to 1.5
- second_bias: float32 [512], replicated, may hold values from -3 to 3
- up_weight: bfloat16 [512, 2048], P(None, 'mp'), may hold values from -0.25 to 0.25
- up_bias: float32 [2048], P('mp'), may hold values from -3 to 3
- down_weight: bfloat16 [2048, 512], P('mp'), may hold values from -0.125 to 0.125
- down_bias: float32 [512], replicated, may hold values from -3 to 3
- cotangent: bfloat16 [4, 4096, 512], P(None, 'seq'), may hold values from -6 to 6
- doc_starts: int32 [4, 4096], P(None, 'seq'), may hold values from 0 to 1, as said below
- valid_mask: int32 [4, 4096], P(None, 'seq'), may hold values 0 or 1
Outputs:
- layer_out: bfloat16 [4, 4096, 512], P(None, 'seq')
- grad_tokens: float32 [4, 4096, 512], P(None, 'seq')
- lowest_norm: float32 [], replicated
- grad_first_gain: float32 [512], replicated
- grad_first_bias: float32 [512], replicated
- grad_query_weight: float32 [512, 512], P(None, 'mp')
- grad_query_bias: float32 [512], P('mp')
- grad_key_weight: float32 [512, 512], P(None, 'mp')
- grad_key_bias: float32 [512], P('mp')
- grad_value_weight: float32 [512, 512], P(None, 'mp')
- grad_value_bias: float32 [512], P('mp')
- grad_output_weight: float32 [512, 512], P('mp')
- grad_output_bias: float32 [512], replicated
- grad_second_gain: float32 [512], replicated
- grad_second_bias: float32 [512], replicated
- grad_up_weight: float32 [512, 2048], P(None, 'mp')
- grad_up_bias: float32 [2048], P('mp')
- grad_down_weight: float32 [2048, 512], P('mp')
- grad_down_bias: float32 [512], replicated
Inputs may be any that keep to these rules, and one draw needn't show every extreme that they name: `doc_starts`: the first entry of every row is 1; in one row, drawn from the seed, no other entry is 1.
All inputs are finite; a program needn't handle non-finite values. No bound on the sum of `valid_mask` on one device may be relied on, other than what follows from the above.
Results may differ from a plain program's by a relative error of at most 0.035.
The roundings to bfloat16 on the way count: a program that leaves them out, or rounds other values in their place, can miss the bound.
Values may be sent and summed in bfloat16 or wider, within the bound.
No kernel may reach another device: no remote copies, remote signals or barrier semaphores. Data moves between devices by JAX's collectives and lax.ppermute only.
A program may use at most 256 MiB of HBM per device.

v0:
```python
import jax
import jax.numpy as jnp
from jax import lax
from jax.sharding import PartitionSpec as P

HEAD_DIM = 64


EPSILON = 1e-05
LARGE_VALUE = 1e30


def entering(value, axis, join, neutral, backward):
    count, mine = (lax.axis_size(axis), lax.axis_index(axis))
    pieces = jax.tree.map(lambda part: lax.all_gather(part, axis), value)
    if backward:
        pieces = jax.tree.map(lambda part: part[::-1], pieces)
        mine = count - 1 - mine
    subtotal = jax.tree.map(
        lambda part, zero: jnp.full_like(part, 0) + jnp.asarray(zero, part.dtype), value, neutral
    )

    def lap(position, subtotal):
        longer = join(subtotal, jax.tree.map(lambda part: part[position], pieces))
        return jax.tree.map(lambda new, old: jnp.where(position < mine, new, old), longer, subtotal)

    return lax.fori_loop(0, count - 1, lap, subtotal)


def normalize(values):
    average = jnp.mean(values, axis=-1, keepdims=True)
    centred = values - average
    spread = jnp.mean(centred * centred, axis=-1, keepdims=True)
    inverse = lax.rsqrt(spread + EPSILON)
    return (centred * inverse, inverse)


def norm_backward(grad_out, normed, inverse, gain_row):
    grad_normed = grad_out * gain_row
    first_term = jnp.mean(grad_normed, axis=-1, keepdims=True)
    second_term = jnp.mean(grad_normed * normed, axis=-1, keepdims=True)
    return inverse * (grad_normed - first_term - normed * second_term)


def feature(values):
    return jax.nn.softplus(values)


def feature_slope(values):
    return jax.nn.sigmoid(values)


def gelu_slope(values):
    cumulative = 0.5 * (1.0 + lax.erf(values * 0.7071067811865476))
    density = 0.3989422804014327 * jnp.exp(-0.5 * values * values)
    return cumulative + values * density


def combine(earlier, following):
    kept_share = 1.0 - following[2]
    return (
        following[0] + kept_share[:, None, None, None] * earlier[0],
        following[1] + kept_share[:, None, None] * earlier[1],
        jnp.maximum(earlier[2], following[2]),
    )


def matmul(left_side, right_side):
    return jnp.dot(left_side, right_side, preferred_element_type=jnp.float32)


def contract_rows(left_side, right_side):
    return jnp.einsum("ta,tb->ab", left_side, right_side, preferred_element_type=jnp.float32)


def contract_cols(left_side, right_side):
    return jnp.einsum("ta,ba->tb", left_side, right_side, preferred_element_type=jnp.float32)


def run_layer(
    tokens,
    first_gain,
    first_bias,
    query_weight,
    query_bias,
    key_weight,
    key_bias,
    value_weight,
    value_bias,
    output_weight,
    output_bias,
    second_gain,
    second_bias,
    up_weight,
    up_bias,
    down_weight,
    down_bias,
    cotangent,
    doc_starts,
    valid_mask,
):
    row_count, block_len, model_width = tokens.shape
    local_width = query_weight.shape[1]
    local_heads = local_width // HEAD_DIM
    tok_count = row_count * block_len
    highest = lax.Precision.HIGHEST
    head_shape = (row_count, block_len, local_heads, HEAD_DIM)
    inputs = tokens.reshape(tok_count, model_width).astype(jnp.float32)
    normed_one, inverse_one = normalize(inputs)
    first_low = (normed_one * first_gain + first_bias).astype(jnp.bfloat16)
    query_pre = (matmul(first_low, query_weight) + query_bias).reshape(head_shape)
    key_pre = (matmul(first_low, key_weight) + key_bias).reshape(head_shape)
    value_low = (
        (matmul(first_low, value_weight) + value_bias).astype(jnp.bfloat16).reshape(head_shape)
    )
    query_feat = feature(query_pre).astype(jnp.bfloat16)
    key_feat = feature(key_pre).astype(jnp.bfloat16)
    segment = jnp.cumsum(doc_starts, axis=1)
    position = lax.broadcasted_iota(jnp.int32, (block_len, block_len), 0)
    earlier_pos = lax.broadcasted_iota(jnp.int32, (block_len, block_len), 1)
    valid_keys = valid_mask > 0
    key_mask = (
        (segment[:, :, None] == segment[:, None, :])
        & (position >= earlier_pos)[None]
        & valid_keys[:, None, :]
    ).astype(jnp.float32)[:, None]
    carried = (segment == 0).astype(jnp.float32)
    last_seg = ((segment == segment[:, -1:]) & valid_keys).astype(jnp.float32)
    restart = (segment[:, -1] > 0).astype(jnp.float32)
    raw_scores = (
        jnp.einsum("rthe,rshe->rhts", query_feat, key_feat, preferred_element_type=jnp.float32)
        * key_mask
    )
    weights_low = raw_scores.astype(jnp.bfloat16)
    within = jnp.einsum(
        "rhts,rshe->rthe", weights_low, value_low, preferred_element_type=jnp.float32
    )
    key_last = key_feat * last_seg[:, :, None, None].astype(jnp.bfloat16)
    state_local = jnp.einsum(
        "rshe,rshf->rhef", key_last, value_low, preferred_element_type=jnp.float32
    )
    total_local = jnp.sum(key_last.astype(jnp.float32), axis=1)
    identity = (jnp.zeros_like(state_local), jnp.zeros_like(total_local), jnp.zeros_like(restart))
    state_in, total_in, unused_flag = entering(
        (state_local, total_local, restart), "seq", combine, identity, False
    )
    query_wide = query_feat.astype(jnp.float32)
    across = (
        jnp.einsum("rthe,rhef->rthf", query_wide, state_in, precision=highest)
        * carried[:, :, None, None]
    )
    normaliser = (
        jnp.transpose(jnp.sum(raw_scores, axis=-1), (0, 2, 1))
        + jnp.einsum("rthe,rhe->rth", query_wide, total_in, precision=highest) * carried[:, :, None]
    )
    divisor = jnp.maximum(normaliser, 1.0)
    attended = (within + across) / divisor[..., None]
    attended_low = attended.reshape(tok_count, local_width).astype(jnp.bfloat16)
    local_min = jnp.min(jnp.where(valid_keys[:, :, None], normaliser, LARGE_VALUE))
    lowest_norm = lax.pmin(local_min, ("seq", "mp"))
    branch = matmul(attended_low, output_weight)
    middle = inputs + branch + output_bias
    normed_two, inverse_two = normalize(middle)
    second_low = (normed_two * second_gain + second_bias).astype(jnp.bfloat16)
    up_pre = matmul(second_low, up_weight) + up_bias
    active_low = jax.nn.gelu(up_pre, approximate=False).astype(jnp.bfloat16)
    ffn_out = matmul(active_low, down_weight)
    layer_out = (
        (middle + ffn_out + down_bias)
        .astype(jnp.bfloat16)
        .reshape(row_count, block_len, model_width)
    )
    grad_low = cotangent.reshape(tok_count, model_width)
    grad_out = grad_low.astype(jnp.float32)
    grad_down = contract_rows(active_low, grad_low)
    grad_down_bias = jnp.sum(grad_out, axis=0)
    grad_up_low = (contract_cols(grad_low, down_weight) * gelu_slope(up_pre)).astype(jnp.bfloat16)
    grad_up = contract_rows(second_low, grad_up_low)
    grad_up_bias = jnp.sum(grad_up_low.astype(jnp.float32), axis=0)
    grad_second = contract_cols(grad_up_low, up_weight)
    grad_second_gain = jnp.sum(grad_second * normed_two, axis=0)
    grad_second_bias = jnp.sum(grad_second, axis=0)
    grad_middle = grad_out + norm_backward(grad_second, normed_two, inverse_two, second_gain)
    grad_branch = grad_middle.astype(jnp.bfloat16)
    grad_output = contract_rows(attended_low, grad_branch)
    grad_output_bias = jnp.sum(grad_branch.astype(jnp.float32), axis=0)
    grad_attended = contract_cols(grad_branch, output_weight).reshape(head_shape)
    grad_num = grad_attended / divisor[..., None]
    grad_norm = jnp.where(
        normaliser > 1.0, -jnp.sum(grad_attended * attended, axis=-1) / divisor, 0.0
    )
    grad_within_low = grad_num.astype(jnp.bfloat16)
    grad_weights = jnp.einsum(
        "rthe,rshe->rhts", grad_within_low, value_low, preferred_element_type=jnp.float32
    )
    grad_values = jnp.einsum(
        "rhts,rthe->rshe", weights_low, grad_within_low, preferred_element_type=jnp.float32
    )
    grad_scores = (
        (grad_weights + jnp.transpose(grad_norm, (0, 2, 1))[..., None]) * key_mask
    ).astype(jnp.bfloat16)
    grad_query = jnp.einsum(
        "rhts,rshe->rthe", grad_scores, key_feat, preferred_element_type=jnp.float32
    )
    grad_key = jnp.einsum(
        "rhts,rthe->rshe", grad_scores, query_feat, preferred_element_type=jnp.float32
    )
    grad_across = grad_num * carried[:, :, None, None]
    grad_norm_carried = grad_norm * carried[:, :, None]
    grad_query = (
        grad_query
        + jnp.einsum("rthf,rhef->rthe", grad_across, state_in, precision=highest)
        + grad_norm_carried[..., None] * total_in[:, None]
    )
    grad_state_in = jnp.einsum("rthe,rthf->rhef", query_wide, grad_across, precision=highest)
    grad_total_in = jnp.einsum("rthe,rth->rhe", query_wide, grad_norm_carried, precision=highest)
    grad_state_loc, grad_total_loc, unused_back = entering(
        (grad_state_in, grad_total_in, restart), "seq", combine, identity, True
    )
    last_wide = last_seg[:, :, None, None]
    grad_key = grad_key + last_wide * (
        jnp.einsum(
            "rshf,rhef->rshe", value_low.astype(jnp.float32), grad_state_loc, precision=highest
        )
        + grad_total_loc[:, None]
    )
    grad_values = grad_values + last_wide * jnp.einsum(
        "rshe,rhef->rshf", key_feat.astype(jnp.float32), grad_state_loc, precision=highest
    )
    grad_query_low = (
        (grad_query * feature_slope(query_pre)).astype(jnp.bfloat16).reshape(tok_count, local_width)
    )
    grad_key_low = (
        (grad_key * feature_slope(key_pre)).astype(jnp.bfloat16).reshape(tok_count, local_width)
    )
    grad_value_low = grad_values.astype(jnp.bfloat16).reshape(tok_count, local_width)
    grad_first = (
        contract_cols(grad_query_low, query_weight)
        + contract_cols(grad_key_low, key_weight)
        + contract_cols(grad_value_low, value_weight)
    )
    grad_first_gain = jnp.sum(grad_first * normed_one, axis=0)
    grad_first_bias = jnp.sum(grad_first, axis=0)
    grad_tokens = (
        grad_middle + norm_backward(grad_first, normed_one, inverse_one, first_gain)
    ).reshape(row_count, block_len, model_width)
    grad_query_w = contract_rows(first_low, grad_query_low)
    grad_query_b = jnp.sum(grad_query_low.astype(jnp.float32), axis=0)
    grad_key_w = contract_rows(first_low, grad_key_low)
    grad_key_b = jnp.sum(grad_key_low.astype(jnp.float32), axis=0)
    grad_value_w = contract_rows(first_low, grad_value_low)
    grad_value_b = jnp.sum(grad_value_low.astype(jnp.float32), axis=0)
    weight_grads = (
        grad_first_gain,
        grad_first_bias,
        grad_query_w,
        grad_query_b,
        grad_key_w,
        grad_key_b,
        grad_value_w,
        grad_value_b,
        grad_output,
        grad_output_bias,
        grad_second_gain,
        grad_second_bias,
        grad_up,
        grad_up_bias,
        grad_down,
        grad_down_bias,
    )
    return (layer_out, grad_tokens, lowest_norm, weight_grads)


def per_device(
    tokens,
    first_gain,
    first_bias,
    query_weight,
    query_bias,
    key_weight,
    key_bias,
    value_weight,
    value_bias,
    output_weight,
    output_bias,
    second_gain,
    second_bias,
    up_weight,
    up_bias,
    down_weight,
    down_bias,
    cotangent,
    doc_starts,
    valid_mask,
):
    share_count = lax.axis_size("mp")
    share_index = lax.axis_index("mp")
    query_all, key_all, value_all, up_all = (
        lax.all_gather(query_weight, "mp", axis=1, tiled=True),
        lax.all_gather(key_weight, "mp", axis=1, tiled=True),
        lax.all_gather(value_weight, "mp", axis=1, tiled=True),
        lax.all_gather(up_weight, "mp", axis=1, tiled=True),
    )
    output_all, down_all = (
        lax.all_gather(output_weight, "mp", axis=0, tiled=True),
        lax.all_gather(down_weight, "mp", axis=0, tiled=True),
    )
    query_b_all, key_b_all, value_b_all, up_b_all = (
        lax.all_gather(query_bias, "mp", axis=0, tiled=True),
        lax.all_gather(key_bias, "mp", axis=0, tiled=True),
        lax.all_gather(value_bias, "mp", axis=0, tiled=True),
        lax.all_gather(up_bias, "mp", axis=0, tiled=True),
    )
    rows_here = tokens.shape[0] // share_count
    row_start = share_index * rows_here

    def own_rows(values):
        return lax.dynamic_slice_in_dim(values, row_start, rows_here, 0)

    layer_part, grad_part, lowest_norm, weight_grads = run_layer(
        own_rows(tokens),
        first_gain,
        first_bias,
        query_all,
        query_b_all,
        key_all,
        key_b_all,
        value_all,
        value_b_all,
        output_all,
        output_bias,
        second_gain,
        second_bias,
        up_all,
        up_b_all,
        down_all,
        down_bias,
        own_rows(cotangent),
        own_rows(doc_starts),
        own_rows(valid_mask),
    )
    layer_wide, grad_tokens = (
        lax.all_gather(layer_part.astype(jnp.float32), "mp", axis=0, tiled=True),
        lax.all_gather(grad_part, "mp", axis=0, tiled=True),
    )
    layer_out = layer_wide.astype(jnp.bfloat16)
    summed = lax.psum(
        (
            weight_grads[0],
            weight_grads[1],
            weight_grads[2],
            weight_grads[3],
            weight_grads[4],
            weight_grads[5],
            weight_grads[6],
            weight_grads[7],
            weight_grads[8],
            weight_grads[9],
            weight_grads[10],
            weight_grads[11],
            weight_grads[12],
            weight_grads[13],
            weight_grads[14],
            weight_grads[15],
        ),
        ("seq", "mp"),
    )
    attn_width = query_weight.shape[1]
    ff_width = up_weight.shape[1]

    def own_share(values, width, dim):
        return lax.dynamic_slice_in_dim(values, share_index * width, width, dim)

    weight_grads = (
        summed[0],
        summed[1],
        own_share(summed[2], attn_width, 1),
        own_share(summed[3], attn_width, 0),
        own_share(summed[4], attn_width, 1),
        own_share(summed[5], attn_width, 0),
        own_share(summed[6], attn_width, 1),
        own_share(summed[7], attn_width, 0),
        own_share(summed[8], attn_width, 0),
        summed[9],
        summed[10],
        summed[11],
        own_share(summed[12], ff_width, 1),
        own_share(summed[13], ff_width, 0),
        own_share(summed[14], ff_width, 0),
        summed[15],
    )
    return (layer_out, grad_tokens, lowest_norm) + tuple(weight_grads)


def solution(mesh):
    return jax.shard_map(
        per_device,
        mesh=mesh,
        in_specs=(
            P(None, "seq", None),
            P(),
            P(),
            P(None, "mp"),
            P("mp"),
            P(None, "mp"),
            P("mp"),
            P(None, "mp"),
            P("mp"),
            P("mp", None),
            P(),
            P(),
            P(),
            P(None, "mp"),
            P("mp"),
            P("mp", None),
            P(),
            P(None, "seq", None),
            P(None, "seq"),
            P(None, "seq"),
        ),
        out_specs=(
            P(None, "seq", None),
            P(None, "seq", None),
            P(),
            P(),
            P(),
            P(None, "mp"),
            P("mp"),
            P(None, "mp"),
            P("mp"),
            P(None, "mp"),
            P("mp"),
            P("mp", None),
            P(),
            P(),
            P(),
            P(None, "mp"),
            P("mp"),
            P("mp", None),
            P(),
        ),
        check_vma=False,
    )
```

profile of v0, /device:TPU:0, one launch (start us, length us, event | category | flops | bytes accessed | tf_op | source)
XLA Modules:
  0.0 638.2 jit_solution(2873309122931378106)
XLA Ops:
  7.3 2.1 all-gather.6
  17.8 2.4 all_gather.68
  20.2 2.4 all_gather.70
  22.6 2.4 all_gather.66
  29.9 2.9 reshape.328
  35.8 6.6 %convert_reduce_fusion.6 = (f32[2,8,64]{0,2,1:T(8,128)S(1)}, bf16[2,256,8,64]{1,0,3,2:T(2,128)(2,1)S(1)}, bf16[2,256,8,64]{1,0,3,2:T(2,128)(2,1)S(1)}, bf16[2,256,8,64]{1,0,3,2:T(2,128)(2,1)S(1)}) fusion(bf16[2,256]{1,0:T(2,128)(2,1)S(1)} %get-tuple-element.382, f32[2,256,8,64]{1,0,3,2:T(2,128)} %reshape.328, f32[2,256,8,64]{1,0,3,2:T(2,128)} %reshape.327), kind=kLoop, calls=%fused_computation.103 | loop fusion | flops 5241856 | bytes 3675136 | tf_op jit(solution)/shard_map/reduce_sum | solution.py:142
  47.9 44.0 %all-reduce = f32[32]{0:T(128)S(1)} all-reduce(f32[32]{0:T(128)S(1)} %dynamic-update-slice), channel_id=3, replica_groups=mesh['seq'=16,'mp'=2] {'seq'}, use_global_device_ids=true, to_apply=%add | all-reduce | flops 32 | bytes 256
  93.9 4.0 all_gather.77
  97.9 2.5 convert_reduce_fusion.1
  100.5 37.6 %all-gather.2 = f32[32,8,64]{2,1,0:T(8,128)S(1)} all-gather(f32[2,8,64]{2,1,0:T(8,128)S(1)} %copy.102), channel_id=4, replica_groups=mesh['seq'=16,'mp'=2] {'seq'}, dimensions={0}, use_global_device_ids=true | all-gather | bytes 69632 | tf_op jit(solution)/shard_map/all_gather | solution.py:15
  141.6 19.0 %all-gather.23.cloned.1.call-done = f32[32,8,64,64]{3,2,1,0:T(8,128)} async-done(((f32[2,8,64,64]{3,2,1,0:T(8,128)}), f32[32,8,64,64]{3,2,1,0:T(8,128)}) %all-gather.23.cloned.1.call-update) | async-done | bytes 4194320 | tf_op jit(solution)/shard_map/all_gather | solution.py:15
  160.7 19.6 %while.32 = (s32[]{:T(128)}, f32[2,8,64,64]{3,2,1,0:T(8,128)S(1)}, f32[2,8,64]{2,1,0:T(8,128)S(1)}, s32[]{:T(128)}, f32[16,2,8,64,64]{4,3,2,1,0:T(8,128)}, /*ind...) while((s32[]{:T(128)}, f32[2,8,64,64]{3,2,1,0:T(8,128)S(1)}, ...), condition=%wide.region_6.7_spmd.clone, body=%wide.region_5.6_spmd.clone.sunk | while | flops 266246 | bytes 798887 | solution.py:27
  184.5 13.2 %fusion.10 = (bf16[512,2048]{1,0:T(8,128)(2,1)}, f32[512,2048]{1,0:T(8,128)}) fusion(f32[2048]{0:T(1024)S(1)} %all_gather.79, bf16[512,2048]{1,0:T(8,128)(2,1)} %all-gather.15.cloned.1.call-done, f32[512,512]{1,0:T(8,128)S(1)} %get-tuple-element.395, f32[512]{0:T(512)S(1)} %copy-done.49, f32[512]{0:T(512)S(1)} %copy-done.48, f32[512]{0:T(512)S(1)} %add_rsqrt_fusion, ...), kind=kOutput, calls=%fused_computation.18 | convolution fusion | flops 1144258560 | bytes 9453568 | tf_op jit(solution)/shard_map/dot_general | solution.py:69
  197.8 5.0 convert_reduce_fusion
  202.8 2.1 multiply_reduce_fusion.1
  206.8 2.9 reshape.332
  209.7 2.8 fusion.52
  216.1 39.8 %all-gather.4 = f32[32,8,64]{2,1,0:T(8,128)S(1)} all-gather(f32[2,8,64]{2,1,0:T(8,128)S(1)} %bitcast.226), channel_id=6, replica_groups=mesh['seq'=16,'mp'=2] {'seq'}, dimensions={0}, use_global_device_ids=true | all-gather | bytes 69632 | tf_op jit(solution)/shard_map/all_gather | solution.py:15
  256.0 2.4 multiply_convert_fusion
  266.9 2.0 fusion.37
  269.0 56.1 %all-gather.25.cloned.1.call-done = f32[32,8,64,64]{3,2,1,0:T(8,128)} async-done(((f32[2,8,64,64]{3,2,1,0:T(8,128)}), f32[32,8,64,64]{3,2,1,0:T(8,128)}) %all-gather.25.cloned.1.call-update) | async-done | bytes 4194320 | tf_op jit(solution)/shard_map/all_gather | solution.py:15
  325.1 8.3 %rev.9 = f32[16,2,8,64,64]{4,3,2,1,0:T(8,128)} reverse(f32[16,2,8,64,64]{4,3,2,1,0:T(8,128)} %bitcast.189), dimensions={0} | reverse | bytes 8388608 | tf_op jit(solution)/shard_map/rev | solution.py:17
  333.5 19.5 %while.33 = (s32[]{:T(128)}, f32[2,8,64,64]{3,2,1,0:T(8,128)S(1)}, f32[2,8,64]{2,1,0:T(8,128)S(1)}, s32[]{:T(128)}, f32[16,2,8,64,64]{4,3,2,1,0:T(8,128)}, /*ind...) while((s32[]{:T(128)}, f32[2,8,64,64]{3,2,1,0:T(8,128)S(1)}, ...), condition=%wide.region_14.15_spmd.clone, body=%wide.region_13.14_spmd.clone.sunk | while | flops 266246 | bytes 798887 | solution.py:27
  353.0 2.1 convert_reduce_fusion.3
  361.3 2.7 fusion.97
  363.9 2.5 fusion.82
  366.5 3.2 fusion.100
  369.7 3.4 fusion.88
  376.1 40.2 %pmin.7 = f32[]{:T(128)} all-reduce(f32[]{:T(128)} %get-tuple-element.377), channel_id=1, replica_groups=mesh['seq'=16,'mp'=2] {'seq','mp'}, use_global_device_ids=true, to_apply=%region_18.19 | all-reduce | flops 1 | bytes 8 | tf_op jit(solution)/shard_map/pmin | solution.py:160
  416.5 42.7 %all-reduce.1 = (f32[512]{0:T(512)}, f32[512]{0:T(512)}, f32[512]{0:T(512)S(1)}, f32[512]{0:T(512)S(1)}, f32[512]{0:T(512)S(1)}, /*index=5*/f32[512]{0:T(512)}, ...) all-reduce(f32[512]{0:T(512)S(1)} %get-tuple-element.323, ...), channel_id=1, replica_groups=mesh['seq'=16,'mp'=2] {'seq','mp'}, use_global_device_ids=true, to_apply=%region_20.21 | all-reduce | flops 6656 | bytes 53248 | tf_op jit(solution)/shard_map/psum | solution.py:347
  461.7 155.5 %all-reduce.5.cloned.1.call-done = (f32[512,512]{1,0:T(8,128)}, f32[512,512]{1,0:T(8,128)}, f32[512,512]{1,0:T(8,128)}, f32[512,512]{1,0:T(8,128)}, f32[512,2048]{1,0:T(8,128)}, /*index=5*/f32[2048,512]{1,0:T(8,128)}) async-done(((f32[512,512]{1,0:T(8,128)}, f32[512,512]{1,0:T(8,128)}, f32[512,512]{1,0:T(8,128)}, f32[512,512]{1,0:T(8,128)}, f32[512,2048]{1,0:T(8,128)}, /*index=5*/f32[2048,512]{1,0:T(8,128)}), ...) | async-done | bytes 12582928 | tf_op jit(solution)/shard_map/psum | solution.py:347
  619.3 2.6 constant_dynamic-slice_fusion.6
  (343 shorter events, 105.3 us)
Async XLA Ops:
  7.2 6.2 copy-start
  7.2 153.4 %all-gather.23.cloned.1.call-start = ((), (), s32[]{:S(2)}) async-start(), calls=%async_computation.4 | async-start | bytes 8912896 | tf_op jit(solution)/shard_map/all_gather | solution.py:15
  17.8 10.3 %copy-start.51 = (f32[1,2,2,128]{3,1,2,0:T(2,128)}, f32[1,2,2,128]{3,1,2,0:T(2,128)S(1)}, u32[]{:S(2)}) copy-start(f32[1,2,2,128]{3,1,2,0:T(2,128)S(1)} %copy.140) | copy-start | bytes 6148
  20.2 12.5 %copy-start.20 = (bf16[512,512]{1,0:T(8,128)(2,1)}, bf16[512,512]{1,0:T(8,128)(2,1)S(1)}, u32[]{:S(2)}) copy-start(bf16[512,512]{1,0:T(8,128)(2,1)S(1)} %all_gather.68) | copy-start | bytes 1572868
  22.6 6.0 copy-start.18
  28.1 14.3 %copy-start.15 = (bf16[2,256,8,64]{1,3,2,0:T(8,128)(2,1)}, bf16[2,256,8,64]{1,3,2,0:T(8,128)(2,1)S(1)}, u32[]{:S(2)}) copy-start(bf16[2,256,8,64]{1,3,2,0:T(8,128)(2,1)S(1)} %copy.98) | copy-start | bytes 1572868
  29.9 5.3 copy-start.64
  35.2 10.2 %copy-start.4 = (bf16[4,256,512]{2,1,0:T(8,128)(2,1)S(1)}, bf16[4,256,512]{2,1,0:T(8,128)(2,1)}, u32[]{:S(2)}) copy-start(bf16[4,256,512]{2,1,0:T(8,128)(2,1)} %param.24) | copy-start | bytes 3145732
  35.8 178.7 %copy-start.55 = (f32[2,256]{1,0:T(2,128)}, f32[2,256]{1,0:T(2,128)S(1)}, u32[]{:S(2)}) copy-start(f32[2,256]{1,0:T(2,128)S(1)} %get-tuple-element.387) | copy-start | bytes 6148
  35.8 10.6 %copy-start.68 = (u32[32]{0:T(128)S(1)}, u32[32]{0:T(128)}, u32[]{:S(2)}) copy-start(u32[32]{0:T(128)} %constant.175) | copy-start | bytes 388
  35.8 56.2 %copy-start.61 = (f32[1024]{0:T(1024)S(1)}, f32[1024]{0:T(1024)}, u32[]{:S(2)}) copy-start(f32[1024]{0:T(1024)} %param.38) | copy-start | bytes 12292
  42.4 95.9 %copy-start.10 = (bf16[2,256,8,64]{1,0,3,2:T(2,128)(2,1)}, bf16[2,256,8,64]{1,0,3,2:T(2,128)(2,1)S(1)}, u32[]{:S(2)}) copy-start(bf16[2,256,8,64]{1,0,3,2:T(2,128)(2,1)S(1)} %get-tuple-element.381) | copy-start | bytes 1572868
  42.4 167.3 %copy-start.8 = (bf16[2,256,8,64]{1,0,3,2:T(2,128)(2,1)}, bf16[2,256,8,64]{1,0,3,2:T(2,128)(2,1)S(1)}, u32[]{:S(2)}) copy-start(bf16[2,256,8,64]{1,0,3,2:T(2,128)(2,1)S(1)} %get-tuple-element.408) | copy-start | bytes 1572868
  43.6 140.9 %all-gather.15.cloned.1.call-start = ((), (), s32[]{:S(2)}) async-start(), calls=%async_computation | async-start | bytes 3145728 | tf_op jit(solution)/shard_map/all_gather | solution.py:302
  44.3 153.4 %all-gather.17.cloned.1.call-start = ((), (), s32[]{:S(2)}) async-start(), calls=%async_computation.1 | async-start | bytes 3145728 | tf_op jit(solution)/shard_map/all_gather | solution.py:306
  45.0 280.1 %all-gather.25.cloned.1.call-start = ((), (), s32[]{:S(2)}) async-start(), calls=%async_computation.5 | async-start | bytes 8912896 | tf_op jit(solution)/shard_map/all_gather | solution.py:15
  93.9 47.2 %copy-start.16 = (bf16[2,256,8,64]{1,3,2,0:T(8,128)(2,1)S(1)}, bf16[2,256,8,64]{1,3,2,0:T(8,128)(2,1)}, u32[]{:S(2)}) copy-start(bf16[2,256,8,64]{1,3,2,0:T(8,128)(2,1)} %copy-done.15) | copy-start | bytes 1572868
  183.6 14.2 %copy-start.22 = (bf16[64,8,2,256]{3,1,2,0:T(8,128)(2,1)}, bf16[64,8,2,256]{3,1,2,0:T(8,128)(2,1)S(1)}, u32[]{:S(2)}) copy-start(bf16[64,8,2,256]{3,1,2,0:T(8,128)(2,1)S(1)} %copy.142) | copy-start | bytes 1572868
  184.4 13.3 %copy-start.25 = (bf16[2,256,512]{2,1,0:T(8,128)(2,1)S(1)}, bf16[2,256,512]{2,1,0:T(8,128)(2,1)}, u32[]{:S(2)}) copy-start(bf16[2,256,512]{2,1,0:T(8,128)(2,1)} %get-tuple-element.374) | copy-start | bytes 1572868
  197.8 5.0 copy-start.66
  212.5 203.9 %all-gather.19.cloned.1.call-start = ((), (), s32[]{:S(2)}) async-start(), calls=%async_computation.2 | async-start | bytes 1572864 | tf_op jit(solution)/shard_map/all_gather | solution.py:343
  269.0 192.8 %all-gather.21.cloned.1.call-start = ((), (), s32[]{:S(2)}) async-start(), calls=%async_computation.3 | async-start | bytes 3145728 | tf_op jit(solution)/shard_map/all_gather | solution.py:344
  333.5 19.5 %copy-start.12 = (bf16[2,256,8,64]{1,0,3,2:T(2,128)(2,1)S(1)}, bf16[2,256,8,64]{1,0,3,2:T(2,128)(2,1)}, u32[]{:S(2)}) copy-start(bf16[2,256,8,64]{1,0,3,2:T(2,128)(2,1)} %copy-done.10) | copy-start | bytes 1572868
  333.5 19.5 %copy-start.60 = (f32[2,256]{1,0:T(2,128)S(1)}, f32[2,256]{1,0:T(2,128)}, u32[]{:S(2)}) copy-start(f32[2,256]{1,0:T(2,128)} %get-tuple-element.383) | copy-start | bytes 6148
  360.6 256.6 %all-reduce.5.cloned.1.call-start = ((), (), s32[]{:S(2)}) async-start(), calls=%async_computation.6 | async-start | bytes 25165824 | tf_op jit(solution)/shard_map/psum | solution.py:347
  360.9 5.5 copy-start.27
  361.0 5.5 copy-start.36
  369.7 4.9 copy-start.30
  376.0 40.5 %copy-start.59 = (f32[512]{0:T(512)S(1)}, f32[512]{0:T(512)}, u32[]{:S(2)}) copy-start(f32[512]{0:T(512)} %get-tuple-element.373) | copy-start | bytes 6148
  376.1 40.5 %copy-start.63 = (f32[512]{0:T(512)S(1)}, f32[512]{0:T(512)}, u32[]{:S(2)}) copy-start(f32[512]{0:T(512)} %get-tuple-element.327) | copy-start | bytes 6148
  617.3 8.4 %copy-start.44 = (f32[512,2048]{1,0:T(8,128)S(1)}, f32[512,2048]{1,0:T(8,128)}, u32[]{:S(2)}) copy-start(f32[512,2048]{1,0:T(8,128)} %get-tuple-element.371) | copy-start | bytes 12582916
  617.3 9.8 %copy-start.43 = (f32[2048,512]{1,0:T(8,128)S(1)}, f32[2048,512]{1,0:T(8,128)}, u32[]{:S(2)}) copy-start(f32[2048,512]{1,0:T(8,128)} %get-tuple-element.372) | copy-start | bytes 12582916
  (44 other events, 113.4 us)
Sparse Core Ops, SparseCore 0:
  43.7 116.9 all-gather.22
  162.2 9.4 all-gather.14
  173.2 11.7 all-gather.16
  212.6 112.4 all-gather.24
  327.1 7.2 all-gather.18
  360.8 8.7 all-gather.20
  377.7 239.4 all-reduce.4
where the time goes:
time: 647 us; the launch traced here: 638 us
  waiting for transfers between devices  232 us (36%)
  blocking collectives  223 us (34%)
  matrix products  62.9 us (10%)
  other arithmetic  59.5 us (9%)
  local copies, waits for them, and re-layouts  42.2 us (7%)
  between operations  16.2 us (3%)
    psum x1, waiting for transfers between devices, per_device(): lax.psum((weight_grads[0], weight_grads[1], weight_grads[2], weight_grads...  156 us
    all_gather x2, blocking collectives, entering(): pieces = jax.tree.map(lambda part: lax.all_gather(part, axis), value)  77.4 us
    all_gather x2, waiting for transfers between devices, entering(): pieces = jax.tree.map(lambda part: lax.all_gather(part, axis), value)  75.1 us
    unnamed x1, blocking collectives  44 us
    psum x1, blocking collectives, per_device(): lax.psum((weight_grads[0], weight_grads[1], weight_grads[2], weight_grads...  42.7 us
    pmin x1, blocking collectives, run_layer(): lowest_norm = lax.pmin(local_min, ('seq', 'mp'))  40.2 us
    select_n x60, other arithmetic, lap(): jnp.where(position < mine, new, old)  37.7 us
    dot_general x6, matrix products, matmul(): return jnp.dot(left_side, right_side, preferred_element_type=jnp.float32)  17.1 us
  transfers between devices with their start and end apart: 7, of which 3 were waited for; matrix products, arithmetic and copies ran while one was open for 17% of the time, Pallas kernels for 0%

commit v1 on v0

v1 whole, which is shorter than its diff:
```python
import functools

import jax
import jax.numpy as jnp
from jax import lax
from jax.experimental import pallas as pl
from jax.experimental.pallas import tpu as pltpu
from jax.sharding import PartitionSpec as P

HEAD_DIM = 64
LANES = 128
EPSILON = 1e-05
LARGE_VALUE = 1e30
MEBI = 1024 * 1024

low = jnp.bfloat16
wide = jnp.float32


def dot(left, right):
    return jnp.dot(left, right, preferred_element_type=wide)


def dot_nt(left, right):
    return lax.dot_general(left, right, (((1,), (1,)), ((), ())), preferred_element_type=wide)


def dot_tn(left, right):
    return lax.dot_general(left, right, (((0,), (0,)), ((), ())), preferred_element_type=wide)


def iota(shape, dim):
    return lax.broadcasted_iota(jnp.int32, shape, dim)


def first_head(shape):
    return iota(shape, 1) < HEAD_DIM


def only_head(pair, head):
    keep = first_head(pair.shape) if head == 0 else jnp.logical_not(first_head(pair.shape))
    return jnp.where(keep, pair, jnp.zeros_like(pair))


def head_sums(pair):
    keep = first_head(pair.shape)
    one = jnp.sum(jnp.where(keep, pair, 0.0), axis=1, keepdims=True)
    two = jnp.sum(jnp.where(keep, 0.0, pair), axis=1, keepdims=True)
    return jnp.where(keep, one, two)


def spread_heads(columns):
    return jnp.where(first_head((columns.shape[0], LANES)), columns[:, 0:1], columns[:, 1:2])


def two_terms(value):
    high = value.astype(low)
    return high, (value - high.astype(wide)).astype(low)


def two_blocks(state):
    return jnp.concatenate([only_head(state, 0), only_head(state, 1)], axis=0)


def compact(product):
    return jnp.where(
        first_head((HEAD_DIM, LANES)), product[:HEAD_DIM], product[HEAD_DIM:]
    )


def normalize(values):
    average = jnp.mean(values, axis=1, keepdims=True)
    centred = values - average
    spread = jnp.mean(centred * centred, axis=1, keepdims=True)
    inverse = lax.rsqrt(spread + EPSILON)
    return (centred * inverse, inverse)


def norm_backward(grad_out, normed, inverse, gain_row):
    grad_normed = grad_out * gain_row
    first_term = jnp.mean(grad_normed, axis=1, keepdims=True)
    second_term = jnp.mean(grad_normed * normed, axis=1, keepdims=True)
    return inverse * (grad_normed - first_term - normed * second_term)


def column_sums(values):
    return jnp.sum(values, axis=0, keepdims=True)


TILE = 32


def tiles(count):
    return [slice(start, start + TILE) for start in range(0, count, TILE)]


def fold_rows(values):
    total = values[0:8]
    for start in range(8, values.shape[0], 8):
        total = total + values[start : start + 8]
    return total


class Sizes:
    def __init__(self, blocks, rows, block, width, attn, hidden):
        self.blocks, self.rows, self.block = blocks, rows, block
        self.width, self.attn, self.hidden = width, attn, hidden
        self.toks = rows * block
        self.pairs = 2 * attn // LANES
        self.group = blocks // (rows * self.pairs)
        self.slice = HEAD_DIM // self.group
        self.height = -(-(self.slice + 3) // 8) * 8

    def at(self, row, tile):
        return slice(row * self.block + tile.start, row * self.block + tile.stop)

    def span(self, row):
        return slice(row * self.block, (row + 1) * self.block)


def lanes_of(pair):
    return slice(pair * LANES, (pair + 1) * LANES)


def write_state(z, sent_ref, held_ref, row, pair, state, total, restart, extra):
    held_ref[...] = state
    for step in range(z.group):
        index = (row * z.pairs + pair) * z.group + step
        sent_ref[index, 0 : z.slice, :] = held_ref[step * z.slice : (step + 1) * z.slice, :]
        sent_ref[index, z.slice : z.slice + 1, :] = total
        sent_ref[index, z.slice + 1 : z.slice + 2, :] = jnp.broadcast_to(restart, (1, LANES))
        sent_ref[index, z.slice + 2 : z.slice + 3, :] = extra
        if z.height > z.slice + 3:
            sent_ref[index, z.slice + 3 : z.height, :] = jnp.zeros(
                (z.height - z.slice - 3, LANES), wide
            )


def read_state(z, got_ref, held_ref, row, pair):
    start = (row * z.pairs + pair) * z.group
    for step in range(z.group):
        held_ref[step * z.slice : (step + 1) * z.slice, :] = got_ref[start + step, 0 : z.slice, :]
    return held_ref[...], got_ref[start, z.slice : z.slice + 1, :]


def mask_of(z, cols_ref, segs_ref, row):
    here = cols_ref[z.span(row), 0:1]
    there = segs_ref[row * 8 : row * 8 + 1, :]
    shape = (z.block, z.block)
    return jnp.logical_and(here == there, iota(shape, 0) >= iota(shape, 1))


def project_kernel(
    z,
    mine_ref,
    tokens_ref,
    starts_ref,
    valid_ref,
    gain_ref,
    bias_ref,
    wk_ref,
    wk2_ref,
    bk_ref,
    wv_ref,
    wv2_ref,
    bv_ref,
    other_bias_ref,
    first_ref,
    kslope_ref,
    kfeat_ref,
    vlow_ref,
    cols_ref,
    segs_ref,
    sent_ref,
    held_ref,
    pre_ref,
):
    mine = mine_ref[0]
    for row in range(z.rows):
        for tile in tiles(z.block):
            x = tokens_ref[row, tile, :].astype(wide)
            normed, _ = normalize(x)
            first_ref[z.at(row, tile), :] = (normed * gain_ref[...] + bias_ref[...]).astype(low)
    a = z.attn
    first = first_ref[...]
    for part, (wk, wv, bk, bv) in enumerate(
        (
            (wk_ref, wv_ref, bk_ref[...], bv_ref[...]),
            (wk2_ref, wv2_ref, other_bias_ref[:, a : 2 * a], other_bias_ref[:, 2 * a : 3 * a]),
        )
    ):
        lanes = slice(part * a, (part + 1) * a)
        pre_ref[part] = dot(first, wk[...])
        vlow_ref[:, lanes] = (dot(first, wv[...]) + bv).astype(low)
        for tile in tiles(z.toks):
            key_pre = pre_ref[part, tile, :] + bk
            kslope_ref[tile, lanes] = jax.nn.sigmoid(key_pre).astype(low)
            kfeat_ref[tile, lanes] = softplus(key_pre).astype(low)
    square = (z.block, z.block)
    upto = iota(square, 0) <= iota(square, 1)
    upper = jnp.where(upto, 1.0, 0.0).astype(low)
    since = jnp.where(iota(square, 0) >= iota(square, 1), 1.0, 0.0).astype(low)
    same = jnp.where(iota(square, 0) == iota(square, 1), 1.0, 0.0).astype(low)
    for row in range(z.rows):
        other = z.rows + row

        def pick(ref):
            value = jnp.where(mine == 0, ref[row : row + 1, :], ref[other : other + 1, :])
            return jnp.broadcast_to(value.astype(wide), (8, z.block)).astype(low)

        starts, valid = pick(starts_ref), pick(valid_ref)
        seg_row = dot(starts, upper)
        seg_col = dot_nt(since, starts)[:, 0:1]
        valid_col = dot_nt(same, valid)[:, 0:1]
        seg_end = seg_row[0:1, z.block - 1 : z.block]
        segs_ref[row * 8 : (row + 1) * 8, :] = jnp.where(valid.astype(wide) > 0.0, seg_row, -1.0)
        carried = jnp.where(seg_col == 0.0, 1.0, 0.0)
        last = jnp.where(jnp.logical_and(seg_col == seg_end, valid_col > 0.0), 1.0, 0.0)
        restart = jnp.where(seg_end > 0.0, 1.0, 0.0)
        lane = iota((z.block, LANES), 1)
        cols = jnp.where(lane == 0, seg_col, 0.0)
        cols = jnp.where(lane == 1, carried, cols)
        cols = jnp.where(lane == 2, last, cols)
        cols = jnp.where(lane == 3, valid_col, cols)
        cols = jnp.where(lane == 4, restart, cols)
        cols_ref[z.span(row), :] = cols
        for pair in range(z.pairs):
            keys = kfeat_ref[z.span(row), lanes_of(pair)].astype(wide) * last
            product = dot_tn(keys.astype(low), vlow_ref[z.span(row), lanes_of(pair)])
            write_state(
                z,
                sent_ref,
                held_ref,
                row,
                pair,
                compact(product),
                column_sums(keys),
                restart,
                jnp.zeros((1, LANES), wide),
            )


def softplus(values):
    return jnp.maximum(values, 0.0) + jnp.log1p(jnp.exp(-jnp.abs(values)))


def scan_kernel(z, backward, held_ref, scanned_ref, lowest_ref):
    flag = z.slice + 1
    running = jnp.zeros((z.height, LANES), wide)
    least = jnp.full((1, LANES), LARGE_VALUE, wide)
    for step in range(z.blocks):
        block = z.blocks - 1 - step if backward else step
        scanned_ref[block] = running
        here = held_ref[block]
        running = here + (1.0 - here[flag : flag + 1, :]) * running
        least = jnp.minimum(least, here[flag + 1 : flag + 2, :])
    lowest_ref[...] = jnp.broadcast_to(least, (8, LANES))


def score_kernel(
    z,
    first_ref,
    wq_ref,
    wq2_ref,
    bq_ref,
    other_bias_ref,
    kfeat_ref,
    vlow_ref,
    cols_ref,
    segs_ref,
    qslope_ref,
    qfeat_ref,
    weights_ref,
    within_ref,
    sums_ref,
    pre_ref,
):
    a = z.attn
    for part, (wq, bq) in enumerate(((wq_ref, bq_ref[...]), (wq2_ref, other_bias_ref[:, 0:a]))):
        lanes = slice(part * a, (part + 1) * a)
        pre_ref[part] = dot(first_ref[...], wq[...])
        for tile in tiles(z.toks):
            query_pre = pre_ref[part, tile, :] + bq
            qslope_ref[tile, lanes] = jax.nn.sigmoid(query_pre).astype(low)
            qfeat_ref[tile, lanes] = softplus(query_pre).astype(low)
    for row in range(z.rows):
        mask = mask_of(z, cols_ref, segs_ref, row)
        table = jnp.zeros((z.block, LANES), wide)
        for pair in range(z.pairs):
            here = (z.span(row), lanes_of(pair))
            queries, keys, values = qfeat_ref[here], kfeat_ref[here], vlow_ref[here]
            within = jnp.zeros((z.block, LANES), wide)
            sums = []
            for head in range(2):
                scores = jnp.where(mask, dot_nt(only_head(queries, head), keys), 0.0)
                weights = scores.astype(low)
                weights_ref[(row * z.pairs + pair) * 2 + head] = weights
                within = within + dot(weights, only_head(values, head))
                sums.append(jnp.sum(scores, axis=1, keepdims=True))
            within_ref[here] = within
            lane = iota((z.block, LANES), 1)
            table = jnp.where(lane == 2 * pair, sums[0], table)
            table = jnp.where(lane == 2 * pair + 1, sums[1], table)
        sums_ref[z.span(row), :] = table


def middle_kernel(
    z,
    mine_ref,
    got_ref,
    qfeat_ref,
    within_ref,
    sums_ref,
    cols_ref,
    tokens_ref,
    cot_ref,
    wo_ref,
    wo2_ref,
    ob_ref,
    gain_ref,
    bias_ref,
    wup_ref,
    wup2_ref,
    bup_ref,
    bup2_ref,
    wd_ref,
    wd2_ref,
    db_ref,
    layer_ref,
    act_ref,
    act2_ref,
    gup_ref,
    gup2_ref,
    second_ref,
    gbr_ref,
    att_ref,
    att2_ref,
    gnum_ref,
    gnorm_ref,
    sent_ref,
    vec_ref,
    s_mid,
    s_n2,
    s_r2,
    s_ffn,
    s_gsec,
    s_att,
    s_norm,
    s_min,
    held_ref,
    s_up,
    s_gact,
):
    step = pl.program_id(0)
    a = z.attn

    @pl.when(step == 0)
    def _():
        least = jnp.full((1, 1), LARGE_VALUE, wide)
        for row in range(z.rows):
            carried = cols_ref[z.span(row), 1:2]
            valid = cols_ref[z.span(row), 3:4]
            for pair in range(z.pairs):
                here = (z.span(row), lanes_of(pair))
                state, total = read_state(z, got_ref, held_ref, row, pair)
                high, rest = two_terms(two_blocks(state))
                queries = qfeat_ref[here]
                across = dot(
                    jnp.concatenate([queries, queries], axis=1),
                    jnp.concatenate([high, rest], axis=0),
                )
                norm = spread_heads(sums_ref[z.span(row), 2 * pair : 2 * pair + 2])
                norm = norm + carried * head_sums(queries.astype(wide) * total)
                s_norm[here] = norm
                seen = jnp.where(valid > 0.0, norm, LARGE_VALUE)
                seen = jnp.min(jnp.min(seen, axis=0, keepdims=True), axis=1, keepdims=True)
                least = jnp.minimum(least, seen)
                attended = (within_ref[here] + across * carried) / jnp.maximum(norm, 1.0)
                s_att[here] = attended
        s_min[...] = jnp.broadcast_to(least, (8, LANES))
        att_ref[...] = s_att[:, 0:a].astype(low)
        att2_ref[...] = s_att[:, a : 2 * a].astype(low)
        s_mid[...] = dot(att_ref[...], wo_ref[...]) + dot(att2_ref[...], wo2_ref[...])
        for row in range(z.rows):
            for tile in tiles(z.block):
                here = z.at(row, tile)
                middle = tokens_ref[row, tile, :].astype(wide) + s_mid[here, :] + ob_ref[...]
                s_mid[here, :] = middle
                normed, inverse = normalize(middle)
                s_n2[here, :] = normed
                s_r2[here, :] = jnp.broadcast_to(inverse, (TILE, LANES))
                second_ref[here, :] = (normed * gain_ref[...] + bias_ref[...]).astype(low)
        s_ffn[...] = jnp.zeros_like(s_ffn)
        s_gsec[...] = jnp.zeros_like(s_gsec)
        vec_ref[...] = jnp.zeros_like(vec_ref)

    for part, (wup, bup, wd, act_out, gup_out) in enumerate(
        (
            (wup_ref, bup_ref, wd_ref, act_ref, gup_ref),
            (wup2_ref, bup2_ref, wd2_ref, act2_ref, gup2_ref),
        )
    ):
        sums = jnp.zeros((8, bup.shape[1]), wide)
        for row in range(z.rows):
            span = z.span(row)
            s_up[row] = dot(second_ref[span, :], wup[...])
            s_gact[row] = dot_nt(cot_ref[row], wd[...])
            for tile in tiles(z.block):
                up = s_up[row, tile, :] + bup[...]
                share = 0.5 * (1.0 + lax.erf(up * 0.7071067811865476))
                density = 0.3989422804014327 * jnp.exp(-0.5 * up * up)
                act_out[z.at(row, tile), :] = (up * share).astype(low)
                gup = (s_gact[row, tile, :] * (share + up * density)).astype(low)
                gup_out[z.at(row, tile), :] = gup
                sums = sums + fold_rows(gup.astype(wide))
            s_ffn[span, :] += dot(act_out[span, :], wd[...])
            s_gsec[span, :] += dot_nt(gup_out[span, :], wup[...])
        vec_ref[pl.ds(4 + part * pl.num_programs(0) + step, 1), :] = column_sums(sums)

    @pl.when(step == pl.num_programs(0) - 1)
    def _():
        sums = [jnp.zeros((8, z.width), wide) for _ in range(4)]
        for row in range(z.rows):
            for tile in tiles(z.block):
                here = z.at(row, tile)
                layer_ref[here, :] = (s_mid[here, :] + s_ffn[here, :] + db_ref[...]).astype(low)
                grad_out = cot_ref[row, tile, :].astype(wide)
                grad_second, normed = s_gsec[here, :], s_n2[here, :]
                inverse = s_r2[here, 0:1]
                grad_middle = grad_out + norm_backward(
                    grad_second, normed, inverse, gain_ref[...]
                )
                grad_branch = grad_middle.astype(low)
                gbr_ref[here, :] = grad_branch
                values = (grad_branch.astype(wide), grad_second * normed, grad_second, grad_out)
                sums = [total + fold_rows(value) for total, value in zip(sums, values)]
        for line, total in enumerate(sums):
            vec_ref[line : line + 1, :] = column_sums(total)
        grad_branch = gbr_ref[...]
        gnum_ref[:, 0:a] = dot_nt(grad_branch, wo_ref[...])
        gnum_ref[:, a : 2 * a] = dot_nt(grad_branch, wo2_ref[...])
        for row in range(z.rows):
            carried = cols_ref[z.span(row), 1:2]
            restart = cols_ref[row * z.block : row * z.block + 1, 4:5]
            table = jnp.zeros((z.block, LANES), wide)
            for pair in range(z.pairs):
                here = (z.span(row), lanes_of(pair))
                grad_att, norm = gnum_ref[here], s_norm[here]
                inverse = 1.0 / jnp.maximum(norm, 1.0)
                grad_num = grad_att * inverse
                gnum_ref[here] = grad_num
                along = head_sums(grad_att * s_att[here])
                grad_norm = jnp.where(norm > 1.0, -along * inverse, 0.0)
                lane = iota((z.block, LANES), 1)
                table = jnp.where(lane == 2 * pair, grad_norm[:, 0:1], table)
                table = jnp.where(
                    lane == 2 * pair + 1, grad_norm[:, HEAD_DIM : HEAD_DIM + 1], table
                )
                queries = qfeat_ref[here]
                high, rest = two_terms(grad_num * carried)
                product = dot_tn(queries, jnp.concatenate([high, rest], axis=1))
                product = product[:, 0:LANES] + product[:, LANES : 2 * LANES]
                total = column_sums(queries.astype(wide) * (grad_norm * carried))
                write_state(
                    z,
                    sent_ref,
                    held_ref,
                    row,
                    pair,
                    compact(product),
                    total,
                    restart,
                    s_min[0:1, :],
                )
            gnorm_ref[z.span(row), :] = table


def local_kernel(
    z,
    got_ref,
    weights_ref,
    qfeat_ref,
    kfeat_ref,
    vlow_ref,
    gnum_ref,
    gnorm_ref,
    qslope_ref,
    cols_ref,
    segs_ref,
    gq_ref,
    gq2_ref,
    gk_ref,
    gv_ref,
    vec_ref,
    held_ref,
):
    a = z.attn
    vec_ref[...] = jnp.zeros_like(vec_ref)
    half = z.pairs // 2
    for row in range(z.rows):
        mask = mask_of(z, cols_ref, segs_ref, row)
        carried = cols_ref[z.span(row), 1:2]
        for pair in range(z.pairs):
            here = (z.span(row), lanes_of(pair))
            queries, keys, values = qfeat_ref[here], kfeat_ref[here], vlow_ref[here]
            state, total = read_state(z, got_ref, held_ref, row, pair)
            high, rest = two_terms(two_blocks(state))
            grad_norm = spread_heads(gnorm_ref[z.span(row), 2 * pair : 2 * pair + 2])
            num_high, num_rest = two_terms(gnum_ref[here])
            grad_q = carried * (
                dot_nt(
                    jnp.concatenate([num_high, num_rest, num_high], axis=1),
                    jnp.concatenate([high, high, rest], axis=1),
                )
                + grad_norm * total
            )
            grad_k = jnp.zeros((z.block, LANES), wide)
            grad_v = jnp.zeros((z.block, LANES), wide)
            for head in range(2):
                grad_low = only_head(num_high, head)
                norm_col = grad_norm[:, head * HEAD_DIM : head * HEAD_DIM + 1]
                grad_scores = jnp.where(mask, dot_nt(grad_low, values) + norm_col, 0.0).astype(low)
                grad_q = grad_q + dot(grad_scores, only_head(keys, head))
                grad_k = grad_k + dot_tn(grad_scores, only_head(queries, head))
                weights = weights_ref[(row * z.pairs + pair) * 2 + head]
                grad_v = grad_v + dot_tn(weights, grad_low)
            gk_ref[here] = grad_k.astype(low)
            gv_ref[here] = grad_v.astype(low)
            grad_low = (grad_q * qslope_ref[here].astype(wide)).astype(low)
            out = gq_ref if pair < half else gq2_ref
            out[z.span(row), lanes_of(pair % half)] = grad_low
            vec_ref[0:1, lanes_of(pair)] += column_sums(grad_low.astype(wide))


def ffn_grad_kernel(
    z,
    mine_ref,
    act_ref,
    act2_ref,
    cot_ref,
    cot2_ref,
    second_ref,
    second2_ref,
    gup_ref,
    gup2_ref,
    down_keep_ref,
    down_give_ref,
    up_keep_ref,
    up_give_ref,
):
    c1 = cot_ref[...].reshape(z.toks, z.width)
    c2 = cot2_ref[...].reshape(z.toks, z.width)
    down = (dot_tn(act_ref[...], c1) + dot_tn(act2_ref[...], c2)).astype(low)
    up = dot_tn(second_ref[...], gup_ref[...]) + dot_tn(second2_ref[...], gup2_ref[...])
    up = up.astype(low)
    rows, fold = down.shape[0], z.width // up.shape[1]
    tall = z.width // fold
    for distance in range(4):
        down_out = down_give_ref if distance % 2 else down_keep_ref
        up_out = up_give_ref if distance // 2 else up_keep_ref

        @pl.when(pl.program_id(0) == distance)
        def _():
            start = (distance // 2) * rows
            down_out[start : start + rows, :] = down
            start = (distance % 2) * tall
            for i in range(fold):
                lanes = slice(i * up.shape[1], (i + 1) * up.shape[1])
                up_out[start : start + tall, lanes] = up[i * tall : (i + 1) * tall]


def added(kept, got):
    return (kept.astype(wide) + got.astype(wide)).astype(low)


def first_pair_kernel(down_ref, down_got, up_ref, up_got, dk_ref, dg_ref, uk_ref, ug_ref):
    half = dk_ref.shape[0]
    for kept, got, keep, give in (
        (down_ref, down_got, dk_ref, dg_ref),
        (up_ref, up_got, uk_ref, ug_ref),
    ):
        keep[...] = added(kept[0:half, :], got[0:half, :])
        give[...] = added(kept[half : 2 * half, :], got[half : 2 * half, :])


def second_pair_kernel(level, mine_ref, down_ref, down_got, up_ref, up_got, *outs):
    rows = outs[0].shape[0] // 2
    for distance, out_ref in enumerate(outs):
        start = jnp.bitwise_xor(mine_ref[1 + level.index], distance) * rows
        span = pl.ds(pl.multiple_of(start, rows), rows)
        out_ref[0:rows, :] = added(down_ref[span, :], down_got[span, :])
        out_ref[rows : 2 * rows, :] = added(up_ref[span, :], up_got[span, :])


def sum_kernel(level, mine_ref, *refs):
    pieces, outs = refs[: level.radix], refs[level.radix :]
    rows = outs[0].shape[0]
    place = mine_ref[1 + level.index + 1] if len(outs) > 1 else None
    for distance, out_ref in enumerate(outs):
        start = 0
        if place is not None:
            start = pl.multiple_of(jnp.bitwise_xor(place, distance) * rows, rows)
        total = pieces[0][pl.ds(start, rows), :].astype(wide)
        for piece in pieces[1:]:
            total = total + piece[pl.ds(start, rows), :].astype(wide)
        out_ref[...] = total.astype(low)


def join_kernel(level, mine_ref, *refs):
    pieces, outs = refs[: level.radix], refs[level.radix :]
    rows = pieces[0].shape[0] // len(outs)
    for distance, piece in enumerate(pieces):
        place = jnp.bitwise_xor(mine_ref[1 + level.index], distance)
        for i, out_ref in enumerate(outs):
            span = pl.ds(pl.multiple_of(place * rows, rows), rows)
            out_ref[span, :] = piece[i * rows : (i + 1) * rows, :]


def unpack_ffn_kernel(z, mine_ref, *refs):
    downs, ups, (down_ref, up_ref) = refs[:4], refs[4:8], refs[8:]
    rows = z.hidden // 4
    fold = z.width // rows
    tall = z.width // fold
    for distance in range(4):
        place = jnp.bitwise_xor(mine_ref[1], distance)
        span = pl.ds(pl.multiple_of(place * rows, rows), rows)
        down_ref[span, :] = downs[distance][...].astype(wide)
        for i in range(fold):
            lanes = slice(i * rows, (i + 1) * rows)
            up_ref[i * tall : (i + 1) * tall, span] = ups[distance][:, lanes].astype(wide)


def final_kernel(
    z,
    mine_ref,
    got_ref,
    kfeat_ref,
    vlow_ref,
    kslope_ref,
    gk_ref,
    gv_ref,
    cols_ref,
    gq_ref,
    gq2_ref,
    wq_ref,
    wq2_ref,
    wk_ref,
    wk2_ref,
    wv_ref,
    wv2_ref,
    tokens_ref,
    gain_ref,
    gbr_ref,
    vec_mid_ref,
    vec_loc_ref,
    gk1_ref,
    gk2_ref,
    gv1_ref,
    gv2_ref,
    gtok_ref,
    keep_ref,
    give_ref,
    held_ref,
    s_first,
):
    a = z.attn
    half = z.pairs // 2
    keep_ref[...] = jnp.zeros_like(keep_ref)
    give_ref[...] = jnp.zeros_like(give_ref)
    for row in range(z.rows):
        last = cols_ref[z.span(row), 2:3]
        for pair in range(z.pairs):
            here = (z.span(row), lanes_of(pair))
            keys, values = kfeat_ref[here], vlow_ref[here]
            state, total = read_state(z, got_ref, held_ref, row, pair)
            high, rest = two_terms(two_blocks(state))
            grad_k = gk_ref[here].astype(wide) + last * (
                dot_nt(
                    jnp.concatenate([values, values], axis=1),
                    jnp.concatenate([high, rest], axis=1),
                )
                + total
            )
            grad_v = gv_ref[here].astype(wide) + last * dot(
                jnp.concatenate([keys, keys], axis=1), jnp.concatenate([high, rest], axis=0)
            )
            grad_k = (grad_k * kslope_ref[here].astype(wide)).astype(low)
            grad_v = grad_v.astype(low)
            out_k, out_v = (gk1_ref, gv1_ref) if pair < half else (gk2_ref, gv2_ref)
            there = (z.span(row), lanes_of(pair % half))
            out_k[there] = grad_k
            out_v[there] = grad_v
    halves = (
        (keep_ref, gq_ref, gk1_ref, gv1_ref, wq_ref, wk_ref, wv_ref, 0),
        (give_ref, gq2_ref, gk2_ref, gv2_ref, wq2_ref, wk2_ref, wv2_ref, 1),
    )
    steps = z.hidden // z.width
    for out, gq, gk, gv, wq, wk, wv, part in halves:
        partial = dot_nt(gq[...], wq[...]) + dot_nt(gk[...], wk[...])
        partial = partial + dot_nt(gv[...], wv[...])
        if part == 0:
            s_first[...] = partial
        else:
            s_first[...] += partial
        out[2:6, :] = vec_mid_ref[0:4, :]
        out[6:7, 0:a] = vec_loc_ref[0:1, part * a : (part + 1) * a]
        out[6:7, a : 2 * a] = column_sums(gk[...].astype(wide))
        out[7:8, 0:a] = column_sums(gv[...].astype(wide))
        out[8 : 8 + steps, :] = vec_mid_ref[4 + part * steps : 4 + (part + 1) * steps, :]
    sums = [jnp.zeros((8, z.width), wide) for _ in range(2)]
    for row in range(z.rows):
        for tile in tiles(z.block):
            here = z.at(row, tile)
            normed, inverse = normalize(tokens_ref[row, tile, :].astype(wide))
            grad_first = s_first[here, :]
            grad_tokens = norm_backward(grad_first, normed, inverse, gain_ref[...])
            gtok_ref[here, :] = (gbr_ref[here, :].astype(wide) + grad_tokens).astype(low)
            values = (grad_first * normed, grad_first)
            sums = [total + fold_rows(value) for total, value in zip(sums, values)]
    for line, total in enumerate(sums):
        for out in (keep_ref, give_ref):
            out[line : line + 1, :] = column_sums(total)


def attn_grad_kernel(
    z,
    radix,
    mine_ref,
    first_ref,
    first2_ref,
    gq_ref,
    gq2_ref,
    gk_ref,
    gk2_ref,
    gv_ref,
    gv2_ref,
    att_ref,
    att2_ref,
    gbr_ref,
    gbr2_ref,
    keep_ref,
    got_ref,
    *outs,
):
    outs, out_ref = outs[:radix], outs[radix]
    a, w = z.attn, z.width
    first, first2 = first_ref[...], first2_ref[...]
    out_ref[0:w, 0:a] = (dot_tn(first, gq_ref[...]) + dot_tn(first2, gq2_ref[...])).astype(low)
    out_ref[0:w, a : 2 * a] = (dot_tn(first, gk_ref[...]) + dot_tn(first2, gk2_ref[...])).astype(
        low
    )
    grad_v = (dot_tn(first, gv_ref[...]) + dot_tn(first2, gv2_ref[...])).astype(low)
    half = w // 2
    out_ref[w : w + half, 0:a] = grad_v[0:half]
    out_ref[w : w + half, a : 2 * a] = grad_v[half:w]
    out_ref[w + half : w + half + a, :] = (
        dot_tn(att_ref[...], gbr_ref[...]) + dot_tn(att2_ref[...], gbr2_ref[...])
    ).astype(low)
    start = w + half + a
    out_ref[start:, :] = jnp.zeros((out_ref.shape[0] - start, w), low)
    out_ref[start : start + 16, :] = (keep_ref[...] + got_ref[...]).astype(low)
    for distance, out in enumerate(outs):
        rows = out.shape[0]
        first_row = jnp.bitwise_xor(mine_ref[1], distance) * rows
        out[...] = out_ref[pl.ds(pl.multiple_of(first_row, rows), rows), :]


def place_kernel(mine_ref, one_ref, one2_ref, two_ref, two2_ref, out_one_ref, out_two_ref):
    step = pl.program_id(0)

    @pl.when(step == 0)
    def _():
        out_one_ref[...] = one_ref[...].reshape(out_one_ref.shape)
        out_two_ref[...] = two_ref[...].reshape(out_two_ref.shape).astype(wide)

    @pl.when(step == 1)
    def _():
        out_one_ref[...] = one2_ref[...].reshape(out_one_ref.shape)
        out_two_ref[...] = two2_ref[...].reshape(out_two_ref.shape).astype(wide)


def unpack_attn_kernel(z, level, mine_ref, *refs):
    pieces, refs = refs[: level.radix], refs[level.radix :]
    lowest_ref, lowest2_ref, q_ref, k_ref, v_ref, o_ref = refs[:6]
    vecs, sums_ref = refs[6:17], refs[17]
    join_kernel(level, mine_ref, *pieces, sums_ref)
    a, w = z.attn, z.width
    half = w // 2
    q_ref[...] = sums_ref[0:w, 0:a].astype(wide)
    k_ref[...] = sums_ref[0:w, a : 2 * a].astype(wide)
    v_ref[0:half, :] = sums_ref[w : w + half, 0:a].astype(wide)
    v_ref[half:w, :] = sums_ref[w : w + half, a : 2 * a].astype(wide)
    o_ref[...] = sums_ref[w + half : w + half + a, :].astype(wide)
    start = w + half + a
    table = sums_ref[start : start + 16, :].astype(wide)
    g1, b1, ob, g2, b2, db, qb, kb, vb, upb, least = vecs
    for row, out in enumerate((g1, b1, ob, g2, b2, db)):
        out[...] = table[row : row + 1, :]
    qb[...] = table[6:7, 0:a]
    kb[...] = table[6:7, a : 2 * a]
    vb[...] = table[7:8, 0:a]
    for part in range(z.hidden // w):
        upb[:, part * w : (part + 1) * w] = table[8 + part : 9 + part, :]
    least[...] = jnp.minimum(lowest_ref[0:1, 0:1], lowest2_ref[0:1, 0:1])


def swap(value):
    return lax.ppermute(value, "mp", [(0, 1), (1, 0)])


def over_blocks(value):
    return lax.all_to_all(value, "seq", 0, 0)


class Level:
    def __init__(self, index, shift, radix):
        self.index, self.shift, self.radix = index, shift, radix

    def exchange(self, value, distance, count):
        other = distance << self.shift
        return lax.ppermute(value, "seq", [(i, i ^ other) for i in range(count)])


def levels_of(count):
    levels, shift = [], 0
    while (1 << shift) < count:
        radix = 4 if (4 << shift) <= count else 2
        levels.append(Level(len(levels), shift, radix))
        shift += 2 if radix == 4 else 1
    return levels


def shape(dims, kind):
    return jax.ShapeDtypeStruct(tuple(dims), kind)


HELD = pl.BlockSpec(memory_space=pltpu.VMEM)


def full(value):
    dims = tuple(value.shape)
    return pl.BlockSpec(dims, lambda *_: (0,) * len(dims))


def call(kernel, ins, outs, flops, mine=None, specs=None, out_specs=None, grid=(1,), scratch=(), limit=58, after=None, held=(), held_out=()):
    specs, out_specs = specs or {}, out_specs or {}
    in_list = [specs.get(i, full(value)) for i, value in enumerate(ins)]
    out_list = [out_specs.get(i, full(value)) for i, value in enumerate(outs)]
    in_list = [HELD if i in held else spec for i, spec in enumerate(in_list)]
    out_list = [HELD if i in held_out else spec for i, spec in enumerate(out_list)]
    moved = sum(v.size * v.dtype.itemsize for v in list(ins) + list(outs))
    head = 0 if mine is None else 1
    ins = list(ins)
    body = kernel
    if after is not None:
        spot = head + len(ins)
        in_list.append(pl.BlockSpec(memory_space=pl.ANY))
        ins.append(after)

        def body(*refs):
            kernel(*refs[:spot], *refs[spot + 1 :])

    return pl.pallas_call(
        body,
        grid_spec=pltpu.PrefetchScalarGridSpec(
            num_scalar_prefetch=head,
            grid=grid,
            in_specs=in_list,
            out_specs=out_list,
            scratch_shapes=list(scratch),
        ),
        out_shape=list(outs),
        compiler_params=pltpu.CompilerParams(vmem_limit_bytes=limit * MEBI),
        cost_estimate=pl.CostEstimate(flops=int(flops), bytes_accessed=int(moved), transcendentals=0),
    )(*(() if mine is None else (mine,)), *ins)


def per_device(
    tokens,
    first_gain,
    first_bias,
    query_weight,
    query_bias,
    key_weight,
    key_bias,
    value_weight,
    value_bias,
    output_weight,
    output_bias,
    second_gain,
    second_bias,
    up_weight,
    up_bias,
    down_weight,
    down_bias,
    cotangent,
    doc_starts,
    valid_mask,
):
    blocks = lax.axis_size("seq")
    shares = lax.axis_size("mp")
    all_rows, block, width = tokens.shape
    a, hidden = query_weight.shape[1], up_weight.shape[1]
    z = Sizes(blocks, all_rows // shares, block, width, a, hidden)
    t = z.toks
    levels = levels_of(blocks)
    me = lax.axis_index("seq")
    places = [(me >> level.shift) & (level.radix - 1) for level in levels]
    mine = jnp.stack([lax.axis_index("mp")] + places).astype(jnp.int32)

    def row(vector):
        return vector.reshape(1, vector.shape[0])

    g1, b1, g2, b2 = row(first_gain), row(first_bias), row(second_gain), row(second_bias)
    ob, db = row(output_bias), row(down_bias)
    wk2, wv2, wq2 = swap(key_weight), swap(value_weight), swap(query_weight)
    other_bias = swap(row(jnp.concatenate([query_bias, key_bias, value_bias, up_bias])))
    wo2, wup2, wd2 = swap(output_weight), swap(up_weight), swap(down_weight)

    def own_block(other=False):
        if other:
            return pl.BlockSpec((z.rows, block, width), lambda i, m: (1 - m[0], 0, 0))
        return pl.BlockSpec((z.rows, block, width), lambda i, m: (m[0], 0, 0))

    part = functools.partial
    sent_shape = shape((blocks, z.height, LANES), wide)
    state_scratch = pltpu.VMEM((HEAD_DIM, LANES), wide)
    thin = shape((t, LANES), wide)
    narrow, broad, half = shape((t, width), low), shape((t, width), wide), shape((t, a), low)

    first, kslope, kfeat, vlow, cols, segs, sent = call(
        part(project_kernel, z),
        (
            tokens,
            doc_starts,
            valid_mask,
            g1,
            b1,
            key_weight,
            wk2,
            row(key_bias),
            value_weight,
            wv2,
            row(value_bias),
            other_bias,
        ),
        (
            narrow,
            narrow,
            narrow,
            narrow,
            thin,
            shape((8 * z.rows, block), wide),
            sent_shape,
        ),
        4e9,
        mine,
        specs={0: own_block()},
        scratch=[state_scratch, pltpu.VMEM((2, t, a), wide)],
    )

    def scan(held, backward, after):
        return call(
            part(scan_kernel, z, backward),
            (held,),
            (sent_shape, shape((8, LANES), wide)),
            1e8,
            limit=8,
            after=after,
            held=(0,),
            held_out=(0, 1),
        )

    arriving = over_blocks(sent)
    qslope, qfeat, weights, within, sums = call(
        part(score_kernel, z),
        (first, query_weight, wq2, row(query_bias), other_bias, kfeat, vlow, cols, segs),
        (narrow, narrow, shape((z.rows * z.pairs * 2, block, block), low), broad, thin),
        4e9,
        scratch=[pltpu.VMEM((2, t, a), wide)],
    )
    entering, _ = scan(arriving, False, qfeat)
    entering = over_blocks(entering)
    steps = hidden // width
    up_block = pl.BlockSpec((width, width), lambda i, m: (0, i))
    down_block = pl.BlockSpec((width, width), lambda i, m: (i, 0))
    tok_block = pl.BlockSpec((t, width), lambda i, m: (0, i))
    bias_block = pl.BlockSpec((1, width), lambda i, m: (0, i))
    other_up = other_bias[:, 3 * a :]
    wider = shape((t, hidden), low)
    (
        layer,
        act,
        act2,
        gup,
        gup2,
        second,
        gbr,
        att,
        att2,
        gnum,
        gnorm,
        sent_back,
        vec_mid,
    ) = call(
        part(middle_kernel, z),
        (
            entering,
            qfeat,
            within,
            sums,
            cols,
            tokens,
            cotangent,
            output_weight,
            wo2,
            ob,
            g2,
            b2,
            up_weight,
            wup2,
            row(up_bias),
            other_up,
            down_weight,
            wd2,
            db,
        ),
        (
            narrow,
            wider,
            wider,
            wider,
            wider,
            narrow,
            narrow,
            half,
            half,
            broad,
            thin,
            sent_shape,
            shape((16, width), wide),
        ),
        12e9,
        mine,
        specs={
            5: own_block(),
            6: own_block(),
            12: up_block,
            13: up_block,
            14: bias_block,
            15: bias_block,
            16: down_block,
            17: down_block,
        },
        out_specs={1: tok_block, 2: tok_block, 3: tok_block, 4: tok_block},
        held=(0,),
        grid=(steps,),
        scratch=[
            pltpu.VMEM((t, width), wide),
            pltpu.VMEM((t, width), wide),
            pltpu.VMEM((t, LANES), wide),
            pltpu.VMEM((t, width), wide),
            pltpu.VMEM((t, width), wide),
            pltpu.VMEM((t, 2 * a), wide),
            pltpu.VMEM((t, 2 * a), wide),
            pltpu.VMEM((8, LANES), wide),
            state_scratch,
            pltpu.VMEM((z.rows, block, width), wide),
            pltpu.VMEM((z.rows, block, width), wide),
        ],
    )
    act_in, gup_in, second_in = swap(act2), swap(gup2), swap(second)
    leaving = over_blocks(sent_back)
    piece = hidden // 4
    act_block = pl.BlockSpec((t, piece), lambda i, m: (0, jnp.bitwise_xor(m[1], i)))
    two = shape((2 * piece, width), low)
    one = shape((piece, width), low)
    down_keep, down_give, up_keep, up_give = call(
        part(ffn_grad_kernel, z),
        (act, act_in, cotangent, cotangent, second, second_in, gup, gup_in),
        (two, two, two, two),
        4e9,
        mine,
        specs={
            0: act_block,
            1: act_block,
            2: own_block(),
            3: own_block(True),
            6: act_block,
            7: act_block,
        },
        grid=(4,),
    )

    def to(value, distance):
        return levels[0].exchange(value, distance, blocks)

    def spread(level, parts):
        return [parts[0]] + [level.exchange(p, d, blocks) for d, p in enumerate(parts) if d]

    def summed(number, parts, after):
        level = levels[number]
        following = levels[number + 1].radix if number + 1 < len(levels) else 1
        rows = parts[0].shape[0] // following
        return call(
            part(sum_kernel, level),
            parts,
            [shape((rows, width), low)] * following,
            1e6,
            mine,
            limit=8,
            after=after,
            held=range(len(parts)),
            held_out=range(following),
        )

    def joined(number, value, count, after):
        level = levels[number]
        rows = level.radix * value.shape[0] // count
        return call(
            part(join_kernel, level),
            spread(level, [value] * level.radix),
            [shape((rows, width), low)] * count,
            1e6,
            mine,
            limit=8,
            after=after,
            held=range(level.radix),
            held_out=range(count),
        )

    leaving, lowest = scan(leaving, True, down_keep)
    scanned = lowest
    leaving = over_blocks(leaving)
    down_got, up_got = to(down_give, 1), to(up_give, 2)
    gq, gq2, gk_local, gv_local, vec_loc = call(
        part(local_kernel, z),
        (entering, weights, qfeat, kfeat, vlow, gnum, gnorm, qslope, cols, segs),
        (half, half, narrow, narrow, shape((8, 2 * a), wide)),
        6e9,
        scratch=[state_scratch],
        after=scanned,
    )
    table = shape((16, width), wide)
    gk, gk2, gv, gv2, gtok, keep, give = call(
        part(final_kernel, z),
        (
            leaving,
            kfeat,
            vlow,
            kslope,
            gk_local,
            gv_local,
            cols,
            gq,
            gq2,
            query_weight,
            wq2,
            key_weight,
            wk2,
            value_weight,
            wv2,
            tokens,
            g1,
            gbr,
            vec_mid,
            vec_loc,
        ),
        (half, half, half, half, narrow, table, table),
        4e9,
        mine,
        specs={15: own_block()},
        scratch=[state_scratch, pltpu.VMEM((t, width), wide)],
        held=(0,),
    )
    down_keep, down_give, up_keep, up_give = call(
        first_pair_kernel,
        (down_keep, down_got, up_keep, up_got),
        (one, one, one, one),
        1e6,
        limit=8,
        after=keep,
        held=range(4),
        held_out=range(4),
    )
    down_got, up_got = to(down_give, 2), to(up_give, 1)
    unit = 16 * blocks
    height = -(-(2 * width + 16) // unit) * unit
    radix = levels[0].radix
    rest = call(
        part(attn_grad_kernel, z, radix),
        (
            first,
            swap(first),
            gq,
            swap(gq2),
            gk,
            swap(gk2),
            gv,
            swap(gv2),
            att,
            swap(att2),
            gbr,
            swap(gbr),
            keep,
            swap(give),
        ),
        [shape((height // radix, width), low)] * radix,
        2e9,
        mine,
        scratch=[pltpu.VMEM((height, width), low)],
        after=down_keep,
    )
    rest_done = rest[0]
    radix = levels[1].radix
    parts = call(
        part(second_pair_kernel, levels[1]),
        (down_keep, down_got, up_keep, up_got),
        [shape((2 * piece // radix, width), low)] * radix,
        1e6,
        mine,
        limit=8,
        after=rest_done,
        held=range(4),
        held_out=range(radix),
    )
    for number in range(1, len(levels)):
        parts = summed(number, spread(levels[number], parts), rest_done)
    (ffn,) = parts
    rest = summed(0, spread(levels[0], rest), ffn)
    for number in range(len(levels) - 1, 1, -1):
        (ffn,) = joined(number, ffn, 1, rest[0])
    down, up = joined(1, ffn, 2, rest[0])
    for number in range(1, len(levels)):
        rest = summed(number, spread(levels[number], rest), down)
    (rest,) = rest
    down_x, down_y, up_x, up_y = to(down, 1), to(down, 2), to(up, 1), to(up, 2)
    ffn_pieces = (down, down_x, down_y, to(down_y, 1), up, up_x, up_y, to(up_x, 2))
    placed = pl.BlockSpec(
        (z.rows, block, width), lambda i, m: (jnp.where(i == 0, m[0], 1 - m[0]), 0, 0)
    )
    layer_out, grad_tokens = call(
        place_kernel,
        (layer, swap(layer), gtok, swap(gtok)),
        (shape(tokens.shape, low), shape(tokens.shape, wide)),
        1e6,
        mine,
        out_specs={0: placed, 1: placed},
        grid=(2,),
        after=rest,
    )
    for number in range(len(levels) - 1, 0, -1):
        (rest,) = joined(number, rest, 1, grad_tokens)
    rest_pieces = spread(levels[0], [rest] * levels[0].radix)
    grad_down, grad_up = call(
        part(unpack_ffn_kernel, z),
        ffn_pieces,
        (shape((hidden, width), wide), shape((width, hidden), wide)),
        1e6,
        mine,
        after=rest,
    )
    (grad_q, grad_k, grad_v, grad_o, g1, b1, ob, g2, b2, db, qb, kb, vb, upb, least) = call(
        part(unpack_attn_kernel, z, levels[0]),
        (*rest_pieces, lowest, swap(lowest)),
        (
            shape((width, a), wide),
            shape((width, a), wide),
            shape((width, a), wide),
            shape((a, width), wide),
        )
        + tuple(shape((1, width), wide) for _ in range(6))
        + tuple(shape((1, a), wide) for _ in range(3))
        + (shape((1, hidden), wide), shape((1, 1), wide)),
        1e6,
        mine,
        scratch=[pltpu.VMEM((height, width), low)],
        after=grad_down,
    )

    def flat(table):
        return table.reshape(table.shape[1])

    return (
        layer_out,
        grad_tokens,
        least.reshape(()),
        flat(g1),
        flat(b1),
        grad_q,
        flat(qb),
        grad_k,
        flat(kb),
        grad_v,
        flat(vb),
        grad_o,
        flat(ob),
        flat(g2),
        flat(b2),
        grad_up,
        flat(upb),
        grad_down,
        flat(db),
    )


def solution(mesh):
    return jax.shard_map(
        per_device,
        mesh=mesh,
        in_specs=(
            P(None, "seq", None),
            P(),
            P(),
            P(None, "mp"),
            P("mp"),
            P(None, "mp"),
            P("mp"),
            P(None, "mp"),
            P("mp"),
            P("mp", None),
            P(),
            P(),
            P(),
            P(None, "mp"),
            P("mp"),
            P("mp", None),
            P(),
            P(None, "seq", None),
            P(None, "seq"),
            P(None, "seq"),
        ),
        out_specs=(
            P(None, "seq", None),
            P(None, "seq", None),
            P(),
            P(),
            P(),
            P(None, "mp"),
            P("mp"),
            P(None, "mp"),
            P("mp"),
            P(None, "mp"),
            P("mp"),
            P("mp", None),
            P(),
            P(),
            P(),
            P(None, "mp"),
            P("mp"),
            P("mp", None),
            P(),
        ),
        check_vma=False,
    )
```

time: 647 us -> 208 us (0.32); the launches traced: 638 us -> 207 us
  blocking collectives: 223 us -> 0 us
  waiting for transfers between devices: 232 us -> 54.6 us
  Pallas kernels: 0 us -> 73.6 us
  matrix products: 62.9 us -> 0 us
  starting transfers between devices: 0.75 us -> 59.6 us
  other arithmetic: 59.5 us -> 1.32 us
  local copies, waits for them, and re-layouts: 42.2 us -> 16.5 us
  between operations: 16.2 us -> 1.4 us
    psum x1 -> x0, waiting for transfers between devices: 156 us -> none  [per_device(): lax.psum((weight_grads[0], weight_grads[1], weight_grads[2], weight_grads...]
    all_gather x10 -> x0, blocking collectives: 96.5 us -> none  [the longest x2 77.4 us: entering(): pieces = jax.tree.map(lambda part: lax.all_gather(part, axis), value)]
    all_gather x6 -> x0, waiting for transfers between devices: 75.1 us -> none  [the longest x2 75.1 us: entering(): pieces = jax.tree.map(lambda part: lax.all_gather(part, axis), value)]
    pallas_call x0 -> x19, Pallas kernels: none -> 73.6 us  [call(): pl.pallas_call(body, grid_spec=pltpu.PrefetchScalarGridSpec(num_scalar_pr...]
    dot_general x32 -> x0, matrix products: 62.9 us -> none  [the longest x6 17.1 us: matmul(): return jnp.dot(left_side, right_side, preferred_element_type=jnp.float32)]
    unnamed x1 -> x0, blocking collectives: 44 us -> none
    psum x1 -> x0, blocking collectives: 42.7 us -> none  [per_device(): lax.psum((weight_grads[0], weight_grads[1], weight_grads[2], weight_grads...]
    pmin x1 -> x0, blocking collectives: 40.2 us -> none  [run_layer(): lowest_norm = lax.pmin(local_min, ('seq', 'mp'))]
  transfers between devices with their start and end apart: 7 -> 52, of which waited for: 3 -> 18; matrix products, arithmetic and copies ran while one was open for 17% -> 1% of each run, Pallas kernels for 0% -> 25%
where the time goes in v1:
time: 208 us; the launch traced here: 207 us
  Pallas kernels  73.6 us (35%)
  starting transfers between devices  59.6 us (29%)
  waiting for transfers between devices  54.6 us (26%)
  local copies, waits for them, and re-layouts  16.5 us (8%)
    pallas_call x19, Pallas kernels, call(): pl.pallas_call(body, grid_spec=pltpu.PrefetchScalarGridSpec(num_scalar_pr...  73.6 us
    ppermute x28, waiting for transfers between devices, exchange(): return lax.ppermute(value, 'seq', [(i, i ^ other) for i in range(count)])  36.6 us
    ppermute x28, starting transfers between devices, exchange(): return lax.ppermute(value, 'seq', [(i, i ^ other) for i in range(count)])  35.3 us
    all_to_all x4, starting transfers between devices, over_blocks(): return lax.all_to_all(value, 'seq', 0, 0)  20 us
    unnamed x110, local copies, waits for them, and re-layouts  15.9 us
    all_to_all x4, waiting for transfers between devices, over_blocks(): return lax.all_to_all(value, 'seq', 0, 0)  14.5 us
    ppermute x20, starting transfers between devices, swap(): return lax.ppermute(value, 'mp', [(0, 1), (1, 0)])  4.31 us
  transfers between devices with their start and end apart: 52, of which 18 were waited for; matrix products, arithmetic and copies ran while one was open for 1% of the time, Pallas kernels for 25%

profile of v1, /device:TPU:0, one launch (start us, length us, event | category | flops | bytes accessed | tf_op | source)
XLA Modules:
  0.0 207.0 jit_solution(12358580625308692846)
XLA Ops:
  4.1 5.3 %shard_map.339 = (bf16[512,512]{1,0:T(8,128)(2,1)}, bf16[512,512]{1,0:T(8,128)(2,1)}, bf16[512,512]{1,0:T(8,128)(2,1)}, bf16[512,512]{1,0:T(8,128)(2,1)}, f32[51...) custom-call(s32[3]{0:T(128)} %pad_add_fusion.mine_ref.refs_0_, bf16[4,256,512]{2,1,0:T(8,128)(2,1)} %tokens_ref.5, ...), custom_call_target="tpu_custom_call" | custom-call | flops 4000000000 | bytes 4822016 | tf_op jit(solution)/shard_map/pallas_call | solution.py:863
  9.4 8.2 %all-to-all-start = ((f32[16,40,128]{2,1,0:T(8,128)}), f32[16,40,128]{2,1,0:T(8,128)S(1)}, u32[]{:S(2)}, u32[]{:S(2)}) async-start(f32[16,40,128]{2,1,0:T(8,128)} %get-tuple-element.100), calls=%async_computation | async-start | bytes 655360 | tf_op jit(solution)/shard_map/all_to_all | solution.py:812
  18.2 6.0 %shard_map.340 = (bf16[512,512]{1,0:T(8,128)(2,1)}, bf16[512,512]{1,0:T(8,128)(2,1)}, bf16[16,256,256]{2,1,0:T(8,128)(2,1)}, f32[512,512]{1,0:T(8,128)}, f32[512,128]{1,0:T(8,128)}) custom-call(bf16[512,512]{1,0:T(8,128)(2,1)} %get-tuple-element.101.first_ref.refs_1_, bf16[512,256]{1,0:T(8,128)(2,1)} %wq_ref.3, ...), custom_call_target="tpu_custom_call" | custom-call | flops 4000000000 | bytes 6840320 | tf_op jit(solution)/shard_map/pallas_call | solution.py:863
  24.2 5.0 %all-to-all-done.refs_0_ = f32[16,40,128]{2,1,0:T(8,128)S(1)} async-done(((f32[16,40,128]{2,1,0:T(8,128)}), f32[16,40,128]{2,1,0:T(8,128)S(1)}, u32[]{:S(2)}, u32[]{:S(2)}) %all-to-all-start) | async-done | bytes 327712 | tf_op jit(solution)/shard_map/all_to_all | solution.py:812
  31.0 3.7 %all-to-all-start.1 = ((f32[16,40,128]{2,1,0:T(8,128)}), f32[16,40,128]{2,1,0:T(8,128)S(1)}, u32[]{:S(2)}, u32[]{:S(2)}) async-start(f32[16,40,128]{2,1,0:T(8,128)} %get-tuple-element.107), calls=%async_computation.1 | async-start | bytes 655360 | tf_op jit(solution)/shard_map/all_to_all | solution.py:812
  37.3 8.1 %all-to-all-done.1.got_ref.refs_0_ = f32[16,40,128]{2,1,0:T(8,128)S(1)} async-done(((f32[16,40,128]{2,1,0:T(8,128)}), f32[16,40,128]{2,1,0:T(8,128)S(1)}, u32[]{:S(2)}, u32[]{:S(2)}) %all-to-all-start.1) | async-done | bytes 327712 | tf_op jit(solution)/shard_map/all_to_all | solution.py:812
  46.1 17.7 %shard_map.342 = (bf16[512,512]{1,0:T(8,128)(2,1)}, bf16[512,1024]{1,0:T(8,128)(2,1)}, bf16[512,1024]{1,0:T(8,128)(2,1)}, bf16[512,1024]{1,0:T(8,128)(2,1)}, bf1...) custom-call(s32[3]{0:T(128)} %pad_add_fusion.mine_ref.refs_0_, ...), custom_call_target="tpu_custom_call" | custom-call | flops 12000000000 | bytes 17219584 | tf_op jit(solution)/shard_map/pallas_call | solution.py:863
  64.5 3.5 %all-to-all-start.2 = ((f32[16,40,128]{2,1,0:T(8,128)}), f32[16,40,128]{2,1,0:T(8,128)S(1)}, u32[]{:S(2)}, u32[]{:S(2)}) async-start(f32[16,40,128]{2,1,0:T(8,128)} %get-tuple-element.111), calls=%async_computation.2 | async-start | bytes 655360 | tf_op jit(solution)/shard_map/all_to_all | solution.py:812
  70.5 7.8 %shard_map.343 = (bf16[512,512]{1,0:T(8,128)(2,1)}, bf16[512,512]{1,0:T(8,128)(2,1)}, bf16[512,512]{1,0:T(8,128)(2,1)}, bf16[512,512]{1,0:T(8,128)(2,1)}) custom-call(s32[3]{0:T(128)} %pad_add_fusion.mine_ref.refs_0_, bf16[512,1024]{1,0:T(8,128)(2,1)} %get-tuple-element.112.act_ref, bf16[512,1024]{1,0:T(8,128)(2,1)} %copy-done.41, ...), custom_call_target="tpu_custom_call" | custom-call | flops 4000000000 | bytes 9437184 | tf_op jit(solution)/shard_map/pallas_call | solution.py:863
  82.2 4.5 %all-to-all-start.3 = ((f32[16,40,128]{2,1,0:T(8,128)}), f32[16,40,128]{2,1,0:T(8,128)S(1)}, u32[]{:S(2)}, u32[]{:S(2)}) async-start(f32[16,40,128]{2,1,0:T(8,128)} %get-tuple-element.118), calls=%async_computation.3 | async-start | bytes 655360 | tf_op jit(solution)/shard_map/all_to_all | solution.py:812
  87.4 1.9 collective-permute-start.19
  90.8 7.7 %shard_map.345 = (bf16[512,256]{1,0:T(8,128)(2,1)}, bf16[512,256]{1,0:T(8,128)(2,1)}, bf16[512,512]{1,0:T(8,128)(2,1)}, bf16[512,512]{1,0:T(8,128)(2,1)}, f32[8,512]{1,0:T(8,128)}) custom-call(f32[16,40,128]{2,1,0:T(8,128)} %copy-done.23, bf16[16,256,256]{2,1,0:T(8,128)(2,1)} %get-tuple-element.120.refs_1_, ...), custom_call_target="tpu_custom_call" | custom-call | flops 6000000000 | bytes 7700480 | tf_op jit(solution)/shard_map/pallas_call | solution.py:863
  99.4 6.4 %shard_map.346 = (bf16[512,256]{1,0:T(8,128)(2,1)}, bf16[512,256]{1,0:T(8,128)(2,1)}, bf16[512,256]{1,0:T(8,128)(2,1)}, bf16[512,256]{1,0:T(8,128)(2,1)}, bf16[5...) custom-call(s32[3]{0:T(128)} %pad_add_fusion.mine_ref.refs_0_, f32[16,40,128]{2,1,0:T(8,128)} %copy-done.24, ...), custom_call_target="tpu_custom_call" | custom-call | flops 4000000000 | bytes 8570880 | tf_op jit(solution)/shard_map/pallas_call | solution.py:863
  111.7 5.3 %shard_map.348 = (bf16[320,512]{1,0:T(8,128)(2,1)}, bf16[320,512]{1,0:T(8,128)(2,1)}, bf16[320,512]{1,0:T(8,128)(2,1)}, bf16[320,512]{1,0:T(8,128)(2,1)}) custom-call(s32[3]{0:T(128)} %pad_add_fusion.mine_ref.refs_0_, bf16[512,512]{1,0:T(8,128)(2,1)} %get-tuple-element.101.first_ref.refs_1_, bf16[512,512]{1,0:T(8,128)(2,1)} %copy-done.44, ...), custom_call_target="tpu_custom_call" | custom-call | flops 2000000000 | bytes 5570560 | tf_op jit(solution)/shard_map/pallas_call | solution.py:863
  120.3 2.3 %collective-permute-start.27 = (bf16[128,512]{1,0:T(8,128)(2,1)S(1)}, bf16[128,512]{1,0:T(8,128)(2,1)S(1)}, u32[]{:S(2)}, u32[]{:S(2)}) collective-permute-start(bf16[128,512]{1,0:T(8,128)(2,1)S(1)} %get-tuple-element.154), channel_id=1, source_target_pairs={{0,16},{2,18},{4,20},{6,22},{8,24},{10,26},{12,28},{14,30},{16,0},... | collective-permute-start | bytes 393224 | tf_op jit(solution)/shard_map/ppermute | solution.py:821
  126.4 1.9 collective-permute-start.23
  128.3 4.9 %collective-permute-done.27.refs_3_ = bf16[128,512]{1,0:T(8,128)(2,1)S(1)} collective-permute-done((bf16[128,512]{1,0:T(8,128)(2,1)S(1)}, bf16[128,512]{1,0:T(8,128)(2,1)S(1)}, u32[]{:S(2)}, u32[]{:S(2)}) %collective-permute-start.27) | collective-permute-done | bytes 131104 | tf_op jit(solution)/shard_map/ppermute | solution.py:821
  135.3 1.9 collective-permute-start.32
  137.2 3.1 %collective-permute-done.22.refs_3_ = bf16[320,512]{1,0:T(8,128)(2,1)S(1)} collective-permute-done((bf16[320,512]{1,0:T(8,128)(2,1)}, bf16[320,512]{1,0:T(8,128)(2,1)S(1)}, u32[]{:S(2)}, u32[]{:S(2)}) %collective-permute-start.22) | collective-permute-done | bytes 327712 | tf_op jit(solution)/shard_map/ppermute | solution.py:821
  141.6 1.8 collective-permute-start.34
  144.8 8.7 %collective-permute-done.33.refs_3_ = bf16[128,512]{1,0:T(8,128)(2,1)S(1)} collective-permute-done((bf16[128,512]{1,0:T(8,128)(2,1)S(1)}, bf16[128,512]{1,0:T(8,128)(2,1)S(1)}, u32[]{:S(2)}, u32[]{:S(2)}) %collective-permute-start.33) | collective-permute-done | bytes 131104 | tf_op jit(solution)/shard_map/ppermute | solution.py:821
  153.4 1.8 collective-permute-start.31
  157.0 1.7 collective-permute-done.30.refs_3_
  166.6 5.7 %collective-permute-done.36.refs_3_ = bf16[80,512]{1,0:T(8,128)(2,1)S(1)} collective-permute-done((bf16[80,512]{1,0:T(8,128)(2,1)S(1)}, bf16[80,512]{1,0:T(8,128)(2,1)S(1)}, u32[]{:S(2)}, u32[]{:S(2)}) %collective-permute-start.36) | collective-permute-done | bytes 81952 | tf_op jit(solution)/shard_map/ppermute | solution.py:821
  172.3 2.1 collective-permute-start.37
  174.4 4.0 %shard_map.354 = (bf16[4,256,512]{2,1,0:T(8,128)(2,1)}, f32[4,256,512]{2,1,0:T(8,128)}) custom-call(s32[3]{0:T(128)} %pad_add_fusion.mine_ref.refs_0_, bf16[512,512]{1,0:T(8,128)(2,1)} %get-tuple-element.110.refs_1_, bf16[512,512]{1,0:T(8,128)(2,1)} %copy-done.21, bf16[512,512]{1,0:T(8,128)(2,1)} %get-tuple-element.132.refs_3_, bf16[512,512]{1,0:T(8,128)(2,1)} %copy-done.22, ...), custom_call_target="tpu_custom_call" | custom-call | flops 1000000 | bytes 5242880 | tf_op jit(solution)/shard_map/pallas_call | solution.py:863
  178.6 1.6 copy-done.3
  182.4 1.9 collective-permute-start.39
  185.9 1.9 collective-permute-start.47
  187.7 8.9 %collective-permute-done.44.refs_4_ = bf16[256,512]{1,0:T(8,128)(2,1)S(1)} collective-permute-done((bf16[256,512]{1,0:T(8,128)(2,1)S(1)}, bf16[256,512]{1,0:T(8,128)(2,1)S(1)}, u32[]{:S(2)}, u32[]{:S(2)}) %collective-permute-start.44) | collective-permute-done | bytes 262176 | tf_op jit(solution)/shard_map/ppermute | solution.py:821
  198.0 4.4 %shard_map.356 = (f32[1024,512]{1,0:T(8,128)}, f32[512,1024]{1,0:T(8,128)}) custom-call(s32[3]{0:T(128)} %pad_add_fusion.mine_ref.refs_0_, bf16[256,512]{1,0:T(8,128)(2,1)} %copy-done.6, bf16[256,512]{1,0:T(8,128)(2,1)} %copy-done.30, bf16[256,512]{1,0:T(8,128)(2,1)} %copy-done.28, bf16[256,512]{1,0:T(8,128)(2,1)} %copy-done.32, ...), custom_call_target="tpu_custom_call" | custom-call | flops 1000000 | bytes 6291456 | tf_op jit(solution)/shard_map/pallas_call | solution.py:863
  203.4 3.4 %shard_map.357 = (f32[512,256]{1,0:T(8,128)}, f32[512,256]{1,0:T(8,128)}, f32[512,256]{1,0:T(8,128)}, f32[256,512]{1,0:T(8,128)}, f32[1,512]{1,0:T(1,128)}, /*in...) custom-call(s32[3]{0:T(128)} %pad_add_fusion.mine_ref.refs_0_, ...), custom_call_target="tpu_custom_call" | custom-call | flops 1000000 | bytes 3435524 | tf_op jit(solution)/shard_map/pallas_call | solution.py:863
  (205 shorter events, 52.5 us)
Async XLA Ops:
  2.5 15.7 %collective-permute-start.3 = (bf16[512,256]{1,0:T(8,128)(2,1)}, bf16[512,256]{1,0:T(8,128)(2,1)}, u32[]{:S(2)}, u32[]{:S(2)}) collective-permute-start(bf16[512,256]{1,0:T(8,128)(2,1)} %wq_ref.3), channel_id=1, source_target_pairs={{0,1},{1,0},{2,3},{3,2},{4,5},{5,4},{6,7},{7,6},{8,9},{9,8},{10,11... | collective-permute-start | bytes 786440 | tf_op jit(solution)/shard_map/ppermute | solution.py:808
  9.4 19.9 %all-to-all-start = ((f32[16,40,128]{2,1,0:T(8,128)}), f32[16,40,128]{2,1,0:T(8,128)S(1)}, u32[]{:S(2)}, u32[]{:S(2)}) async-start(f32[16,40,128]{2,1,0:T(8,128)} %get-tuple-element.100), calls=%async_computation | async-start | bytes 655360 | tf_op jit(solution)/shard_map/all_to_all | solution.py:812
  17.6 19.0 %collective-permute-start.5 = (bf16[512,1024]{1,0:T(8,128)(2,1)S(1)}, bf16[512,1024]{1,0:T(8,128)(2,1)S(1)}, u32[]{:S(2)}, u32[]{:S(2)}) collective-permute-start(bf16[512,1024]{1,0:T(8,128)(2,1)S(1)} %copy-done.37), channel_id=1, source_target_pairs={{0,1},{1,0},{2,3},{3,2},{4,5},{5,4},{6,7},{7,6},{8,9},{9,8},{10,11... | collective-permute-start | bytes 3145736 | tf_op jit(solution)/shard_map/ppermute | solution.py:808
  17.7 19.6 %collective-permute-start.6 = (bf16[1024,512]{1,0:T(8,128)(2,1)S(1)}, bf16[1024,512]{1,0:T(8,128)(2,1)}, u32[]{:S(2)}, u32[]{:S(2)}) collective-permute-start(bf16[1024,512]{1,0:T(8,128)(2,1)S(1)} %copy-done.38), channel_id=1, source_target_pairs={{0,1},{1,0},{2,3},{3,2},{4,5},{5,4},{6,7},{7,6},{8,9},{9,8},{10,11... | collective-permute-start | bytes 3145736 | tf_op jit(solution)/shard_map/ppermute | solution.py:808
  31.0 14.3 %all-to-all-start.1 = ((f32[16,40,128]{2,1,0:T(8,128)}), f32[16,40,128]{2,1,0:T(8,128)S(1)}, u32[]{:S(2)}, u32[]{:S(2)}) async-start(f32[16,40,128]{2,1,0:T(8,128)} %get-tuple-element.107), calls=%async_computation.1 | async-start | bytes 655360 | tf_op jit(solution)/shard_map/all_to_all | solution.py:812
  64.5 15.3 %all-to-all-start.2 = ((f32[16,40,128]{2,1,0:T(8,128)}), f32[16,40,128]{2,1,0:T(8,128)S(1)}, u32[]{:S(2)}, u32[]{:S(2)}) async-start(f32[16,40,128]{2,1,0:T(8,128)} %get-tuple-element.111), calls=%async_computation.2 | async-start | bytes 655360 | tf_op jit(solution)/shard_map/all_to_all | solution.py:812
  82.2 16.4 %all-to-all-start.3 = ((f32[16,40,128]{2,1,0:T(8,128)}), f32[16,40,128]{2,1,0:T(8,128)S(1)}, u32[]{:S(2)}, u32[]{:S(2)}) async-start(f32[16,40,128]{2,1,0:T(8,128)} %get-tuple-element.118), calls=%async_computation.3 | async-start | bytes 655360 | tf_op jit(solution)/shard_map/all_to_all | solution.py:812
  86.7 11.8 %collective-permute-start.12 = (bf16[512,512]{1,0:T(8,128)(2,1)S(1)}, bf16[512,512]{1,0:T(8,128)(2,1)S(1)}, u32[]{:S(2)}, u32[]{:S(2)}) collective-permute-start(bf16[512,512]{1,0:T(8,128)(2,1)S(1)} %copy-done.42), channel_id=1, source_target_pairs={{0,1},{1,0},{2,3},{3,2},{4,5},{5,4},{6,7},{7,6},{8,9},{9,8},{10,11... | collective-permute-start | bytes 1572872 | tf_op jit(solution)/shard_map/ppermute | solution.py:808
  86.8 22.0 %collective-permute-start.17 = (bf16[512,512]{1,0:T(8,128)(2,1)S(1)}, bf16[512,512]{1,0:T(8,128)(2,1)S(1)}, u32[]{:S(2)}, u32[]{:S(2)}) collective-permute-start(bf16[512,512]{1,0:T(8,128)(2,1)S(1)} %copy-done.43), channel_id=1, source_target_pairs={{0,1},{1,0},{2,3},{3,2},{4,5},{5,4},{6,7},{7,6},{8,9},{9,8},{10,11... | collective-permute-start | bytes 1572872 | tf_op jit(solution)/shard_map/ppermute | solution.py:808
  87.3 20.8 %collective-permute-start.16 = (bf16[512,256]{1,0:T(8,128)(2,1)}, bf16[512,256]{1,0:T(8,128)(2,1)}, u32[]{:S(2)}, u32[]{:S(2)}) collective-permute-start(bf16[512,256]{1,0:T(8,128)(2,1)} %get-tuple-element.138), channel_id=1, source_target_pairs={{0,1},{1,0},{2,3},{3,2},{4,5},{5,4},{6,7},{7,6},{8,9},{9,8},{10,11... | collective-permute-start | bytes 786440 | tf_op jit(solution)/shard_map/ppermute | solution.py:808
  87.4 18.4 %collective-permute-start.19 = (bf16[512,512]{1,0:T(8,128)(2,1)}, bf16[512,512]{1,0:T(8,128)(2,1)S(1)}, u32[]{:S(2)}, u32[]{:S(2)}) collective-permute-start(bf16[512,512]{1,0:T(8,128)(2,1)} %get-tuple-element.141), channel_id=1, source_target_pairs={{0,2},{2,0},{4,6},{6,4},{8,10},{10,8},{12,14},{14,12},{16,18},{18,... | collective-permute-start | bytes 1572872 | tf_op jit(solution)/shard_map/ppermute | solution.py:821
  89.3 17.0 %collective-permute-start.20 = (bf16[512,512]{1,0:T(8,128)(2,1)}, bf16[512,512]{1,0:T(8,128)(2,1)S(1)}, u32[]{:S(2)}, u32[]{:S(2)}) collective-permute-start(bf16[512,512]{1,0:T(8,128)(2,1)} %get-tuple-element.143), channel_id=1, source_target_pairs={{0,4},{2,6},{4,0},{6,2},{8,12},{10,14},{12,8},{14,10},{16,20},{18,... | collective-permute-start | bytes 1572872 | tf_op jit(solution)/shard_map/ppermute | solution.py:821
  98.5 11.1 %collective-permute-start.13 = (bf16[512,256]{1,0:T(8,128)(2,1)}, bf16[512,256]{1,0:T(8,128)(2,1)S(1)}, u32[]{:S(2)}, u32[]{:S(2)}) collective-permute-start(bf16[512,256]{1,0:T(8,128)(2,1)} %get-tuple-element.128.gq2_ref), channel_id=1, source_target_pairs={{0,1},{1,0},{2,3},{3,2},{4,5},{5,4},{6,7},{7,6},{8,9},{9,8},{10,11... | collective-permute-start | bytes 786440 | tf_op jit(solution)/shard_map/ppermute | solution.py:808
  120.3 12.9 %collective-permute-start.27 = (bf16[128,512]{1,0:T(8,128)(2,1)S(1)}, bf16[128,512]{1,0:T(8,128)(2,1)S(1)}, u32[]{:S(2)}, u32[]{:S(2)}) collective-permute-start(bf16[128,512]{1,0:T(8,128)(2,1)S(1)} %get-tuple-element.154), channel_id=1, source_target_pairs={{0,16},{2,18},{4,20},{6,22},{8,24},{10,26},{12,28},{14,30},{16,0},... | collective-permute-start | bytes 393224 | tf_op jit(solution)/shard_map/ppermute | solution.py:821
  122.6 10.6 %collective-permute-start.28 = (bf16[128,512]{1,0:T(8,128)(2,1)S(1)}, bf16[128,512]{1,0:T(8,128)(2,1)S(1)}, u32[]{:S(2)}, u32[]{:S(2)}) collective-permute-start(bf16[128,512]{1,0:T(8,128)(2,1)S(1)} %get-tuple-element.155), channel_id=1, source_target_pairs={{0,24},{2,26},{4,28},{6,30},{8,16},{10,18},{12,20},{14,22},{16,8},... | collective-permute-start | bytes 393224 | tf_op jit(solution)/shard_map/ppermute | solution.py:821
  123.2 12.1 %collective-permute-start.21 = (bf16[320,512]{1,0:T(8,128)(2,1)}, bf16[320,512]{1,0:T(8,128)(2,1)S(1)}, u32[]{:S(2)}, u32[]{:S(2)}) collective-permute-start(bf16[320,512]{1,0:T(8,128)(2,1)} %get-tuple-element.146), channel_id=1, source_target_pairs={{0,2},{2,0},{4,6},{6,4},{8,10},{10,8},{12,14},{14,12},{16,18},{18,... | collective-permute-start | bytes 983048 | tf_op jit(solution)/shard_map/ppermute | solution.py:821
  124.4 15.9 %collective-permute-start.22 = (bf16[320,512]{1,0:T(8,128)(2,1)}, bf16[320,512]{1,0:T(8,128)(2,1)S(1)}, u32[]{:S(2)}, u32[]{:S(2)}) collective-permute-start(bf16[320,512]{1,0:T(8,128)(2,1)} %get-tuple-element.147), channel_id=1, source_target_pairs={{0,4},{2,6},{4,0},{6,2},{8,12},{10,14},{12,8},{14,10},{16,20},{18,... | collective-permute-start | bytes 983048 | tf_op jit(solution)/shard_map/ppermute | solution.py:821
  126.4 15.2 %collective-permute-start.23 = (bf16[320,512]{1,0:T(8,128)(2,1)}, bf16[320,512]{1,0:T(8,128)(2,1)S(1)}, u32[]{:S(2)}, u32[]{:S(2)}) collective-permute-start(bf16[320,512]{1,0:T(8,128)(2,1)} %get-tuple-element.148), channel_id=1, source_target_pairs={{0,6},{2,4},{4,2},{6,0},{8,14},{10,12},{12,10},{14,8},{16,22},{18,... | collective-permute-start | bytes 983048 | tf_op jit(solution)/shard_map/ppermute | solution.py:821
  133.2 28.6 %collective-permute-start.7 = (bf16[512,512]{1,0:T(8,128)(2,1)S(1)}, bf16[512,512]{1,0:T(8,128)(2,1)S(1)}, u32[]{:S(2)}, u32[]{:S(2)}) collective-permute-start(bf16[512,512]{1,0:T(8,128)(2,1)S(1)} %copy-done.19), channel_id=1, source_target_pairs={{0,1},{1,0},{2,3},{3,2},{4,5},{5,4},{6,7},{7,6},{8,9},{9,8},{10,11... | collective-permute-start | bytes 1572872 | tf_op jit(solution)/shard_map/ppermute | solution.py:808
  133.2 29.5 %collective-permute-start.11 = (bf16[512,512]{1,0:T(8,128)(2,1)S(1)}, bf16[512,512]{1,0:T(8,128)(2,1)S(1)}, u32[]{:S(2)}, u32[]{:S(2)}) collective-permute-start(bf16[512,512]{1,0:T(8,128)(2,1)S(1)} %copy-done.20), channel_id=1, source_target_pairs={{0,1},{1,0},{2,3},{3,2},{4,5},{5,4},{6,7},{7,6},{8,9},{9,8},{10,11... | collective-permute-start | bytes 1572872 | tf_op jit(solution)/shard_map/ppermute | solution.py:808
  140.3 13.2 %collective-permute-start.33 = (bf16[128,512]{1,0:T(8,128)(2,1)S(1)}, bf16[128,512]{1,0:T(8,128)(2,1)S(1)}, u32[]{:S(2)}, u32[]{:S(2)}) collective-permute-start(bf16[128,512]{1,0:T(8,128)(2,1)S(1)} %shard_map.350.refs_5_.refs_1_), channel_id=1, source_target_pairs={{0,16},{2,18},{4,20},{6,22},{8,24},{10,26},{12,28},{14,30},{16,0},... | collective-permute-start | bytes 393224 | tf_op jit(solution)/shard_map/ppermute | solution.py:821
  141.6 11.8 %collective-permute-start.34 = (bf16[128,512]{1,0:T(8,128)(2,1)S(1)}, bf16[128,512]{1,0:T(8,128)(2,1)S(1)}, u32[]{:S(2)}, u32[]{:S(2)}) collective-permute-start(bf16[128,512]{1,0:T(8,128)(2,1)S(1)} %shard_map.350.refs_5_.refs_1_), channel_id=1, source_target_pairs={{0,24},{2,26},{4,28},{6,30},{8,16},{10,18},{12,20},{14,22},{16,8},... | collective-permute-start | bytes 393224 | tf_op jit(solution)/shard_map/ppermute | solution.py:821
  144.1 11.7 %collective-permute-start.29 = (bf16[80,512]{1,0:T(8,128)(2,1)S(1)}, bf16[80,512]{1,0:T(8,128)(2,1)S(1)}, u32[]{:S(2)}, u32[]{:S(2)}) collective-permute-start(bf16[80,512]{1,0:T(8,128)(2,1)S(1)} %get-tuple-element.157), channel_id=1, source_target_pairs={{0,8},{2,10},{4,12},{6,14},{8,0},{10,2},{12,4},{14,6},{16,24},{18,... | collective-permute-start | bytes 245768 | tf_op jit(solution)/shard_map/ppermute | solution.py:821
  155.9 26.5 %collective-permute-start.43 = (bf16[256,512]{1,0:T(8,128)(2,1)S(1)}, bf16[256,512]{1,0:T(8,128)(2,1)S(1)}, u32[]{:S(2)}, u32[]{:S(2)}) collective-permute-start(bf16[256,512]{1,0:T(8,128)(2,1)S(1)} %get-tuple-element.160.refs_5_.refs_1_), channel_id=1, source_target_pairs={{0,4},{2,6},{4,0},{6,2},{8,12},{10,14},{12,8},{14,10},{16,20},{18,... | collective-permute-start | bytes 786440 | tf_op jit(solution)/shard_map/ppermute | solution.py:821
  158.8 25.4 %collective-permute-start.45 = (bf16[256,512]{1,0:T(8,128)(2,1)S(1)}, bf16[256,512]{1,0:T(8,128)(2,1)S(1)}, u32[]{:S(2)}, u32[]{:S(2)}) collective-permute-start(bf16[256,512]{1,0:T(8,128)(2,1)S(1)} %get-tuple-element.163.refs_5_), channel_id=1, source_target_pairs={{0,2},{2,0},{4,6},{6,4},{8,10},{10,8},{12,14},{14,12},{16,18},{18,... | collective-permute-start | bytes 786440 | tf_op jit(solution)/shard_map/ppermute | solution.py:821
  161.8 23.4 %collective-permute-start.42 = (bf16[256,512]{1,0:T(8,128)(2,1)S(1)}, bf16[256,512]{1,0:T(8,128)(2,1)S(1)}, u32[]{:S(2)}, u32[]{:S(2)}) collective-permute-start(bf16[256,512]{1,0:T(8,128)(2,1)S(1)} %get-tuple-element.160.refs_5_.refs_1_), channel_id=1, source_target_pairs={{0,2},{2,0},{4,6},{6,4},{8,10},{10,8},{12,14},{14,12},{16,18},{18,... | collective-permute-start | bytes 786440 | tf_op jit(solution)/shard_map/ppermute | solution.py:821
  162.7 23.2 %collective-permute-start.46 = (bf16[256,512]{1,0:T(8,128)(2,1)S(1)}, bf16[256,512]{1,0:T(8,128)(2,1)S(1)}, u32[]{:S(2)}, u32[]{:S(2)}) collective-permute-start(bf16[256,512]{1,0:T(8,128)(2,1)S(1)} %get-tuple-element.163.refs_5_), channel_id=1, source_target_pairs={{0,4},{2,6},{4,0},{6,2},{8,12},{10,14},{12,8},{14,10},{16,20},{18,... | collective-permute-start | bytes 786440 | tf_op jit(solution)/shard_map/ppermute | solution.py:821
  181.7 20.8 %collective-permute-start.38 = (bf16[320,512]{1,0:T(8,128)(2,1)S(1)}, bf16[320,512]{1,0:T(8,128)(2,1)S(1)}, u32[]{:S(2)}, u32[]{:S(2)}) collective-permute-start(bf16[320,512]{1,0:T(8,128)(2,1)S(1)} %shard_map.355.refs_9_.refs_1_), channel_id=1, source_target_pairs={{0,2},{2,0},{4,6},{6,4},{8,10},{10,8},{12,14},{14,12},{16,18},{18,... | collective-permute-start | bytes 983048 | tf_op jit(solution)/shard_map/ppermute | solution.py:821
  182.4 20.1 %collective-permute-start.39 = (bf16[320,512]{1,0:T(8,128)(2,1)S(1)}, bf16[320,512]{1,0:T(8,128)(2,1)S(1)}, u32[]{:S(2)}, u32[]{:S(2)}) collective-permute-start(bf16[320,512]{1,0:T(8,128)(2,1)S(1)} %shard_map.355.refs_9_.refs_1_), channel_id=1, source_target_pairs={{0,4},{2,6},{4,0},{6,2},{8,12},{10,14},{12,8},{14,10},{16,20},{18,... | collective-permute-start | bytes 983048 | tf_op jit(solution)/shard_map/ppermute | solution.py:821
  184.2 18.3 %collective-permute-start.40 = (bf16[320,512]{1,0:T(8,128)(2,1)S(1)}, bf16[320,512]{1,0:T(8,128)(2,1)S(1)}, u32[]{:S(2)}, u32[]{:S(2)}) collective-permute-start(bf16[320,512]{1,0:T(8,128)(2,1)S(1)} %shard_map.355.refs_9_.refs_1_), channel_id=1, source_target_pairs={{0,6},{2,4},{4,2},{6,0},{8,14},{10,12},{12,10},{14,8},{16,22},{18,... | collective-permute-start | bytes 983048 | tf_op jit(solution)/shard_map/ppermute | solution.py:821
  185.2 11.4 %collective-permute-start.44 = (bf16[256,512]{1,0:T(8,128)(2,1)S(1)}, bf16[256,512]{1,0:T(8,128)(2,1)S(1)}, u32[]{:S(2)}, u32[]{:S(2)}) collective-permute-start(bf16[256,512]{1,0:T(8,128)(2,1)S(1)} %collective-permute-done.43.refs_3_), channel_id=1, source_target_pairs={{0,2},{2,0},{4,6},{6,4},{8,10},{10,8},{12,14},{14,12},{16,18},{18,... | collective-permute-start | bytes 786440 | tf_op jit(solution)/shard_map/ppermute | solution.py:821
  185.9 11.1 %collective-permute-start.47 = (bf16[256,512]{1,0:T(8,128)(2,1)S(1)}, bf16[256,512]{1,0:T(8,128)(2,1)S(1)}, u32[]{:S(2)}, u32[]{:S(2)}) collective-permute-start(bf16[256,512]{1,0:T(8,128)(2,1)S(1)} %collective-permute-done.45.refs_6_), channel_id=1, source_target_pairs={{0,4},{2,6},{4,0},{6,2},{8,12},{10,14},{12,8},{14,10},{16,20},{18,... | collective-permute-start | bytes 786440 | tf_op jit(solution)/shard_map/ppermute | solution.py:821
  (75 other events, 526.1 us)

commit v2 on v1

--- a/solution.py
+++ b/solution.py
@@ -11,6 +11,28 @@
 LANES = 128
 EPSILON = 1e-05
 LARGE_VALUE = 1e30
+TINY = 1e-30
+ORDER = (
+    "KF",
+    "S",
+    "KD",
+    "KE",
+    "p1",
+    "KG",
+    "p2",
+    "P",
+    "h1",
+    "s1",
+    "h2",
+    "s2",
+    "d1",
+    "d2",
+    "j",
+    "c",
+    "U3",
+    "UB",
+    "UA",
+)
 MEBI = 1024 * 1024
 
 low = jnp.bfloat16
@@ -109,7 +131,7 @@
         self.pairs = 2 * attn // LANES
         self.group = blocks // (rows * self.pairs)
         self.slice = HEAD_DIM // self.group
-        self.height = -(-(self.slice + 3) // 8) * 8
+        self.height = -(-(self.slice + 7) // 16) * 16
 
     def at(self, row, tile):
         return slice(row * self.block + tile.start, row * self.block + tile.stop)
@@ -122,25 +144,77 @@
     return slice(pair * LANES, (pair + 1) * LANES)
 
 
-def write_state(z, sent_ref, held_ref, row, pair, state, total, restart, extra):
-    held_ref[...] = state
+def rows_in_lanes(rows):
+    same = jnp.where(iota((LANES, LANES), 0) == iota((LANES, LANES), 1), 1.0, 0.0).astype(low)
+    return dot_nt(same, rows)
+
+
+def write_piece(z, sent_ref, index, stage_ref, body, total, centre, restart, extra):
+    k = z.slice
+    stage_ref[0:k, :] = body
+    line = k
+    for value in (total, centre):
+        for term in two_terms(value):
+            stage_ref[line : line + 1, :] = term.astype(wide)
+            line += 1
+    stage_ref[line : line + 1, :] = jnp.broadcast_to(restart, (1, LANES))
+    for term in two_terms(extra):
+        line += 1
+        stage_ref[line : line + 1, :] = term.astype(wide)
+    if z.height > k + 7:
+        stage_ref[k + 7 : z.height, :] = jnp.zeros((z.height - k - 7, LANES), wide)
+    sent_ref[index] = stage_ref[...].astype(low)
+
+
+def pair_sum(piece, line):
+    return piece[line : line + 1, :] + piece[line + 1 : line + 2, :]
+
+
+def centred(state, spread):
+    centre = column_sums(state) / jnp.maximum(column_sums(spread), TINY)
+    high, rest = two_terms(centre)
+    centre = high.astype(wide) + rest.astype(wide)
+    return state - spread * centre, centre
+
+
+def write_state(z, sent_ref, held_ref, stage_ref, row, pair, state, total, centre, restart, extra):
+    number = row * z.pairs + pair
+    if state is not None:
+        held_ref[number] = state
     for step in range(z.group):
-        index = (row * z.pairs + pair) * z.group + step
-        sent_ref[index, 0 : z.slice, :] = held_ref[step * z.slice : (step + 1) * z.slice, :]
-        sent_ref[index, z.slice : z.slice + 1, :] = total
-        sent_ref[index, z.slice + 1 : z.slice + 2, :] = jnp.broadcast_to(restart, (1, LANES))
-        sent_ref[index, z.slice + 2 : z.slice + 3, :] = extra
-        if z.height > z.slice + 3:
-            sent_ref[index, z.slice + 3 : z.height, :] = jnp.zeros(
-                (z.height - z.slice - 3, LANES), wide
+        index = number * z.group + step
+        body = held_ref[number, step * z.slice : (step + 1) * z.slice, :]
+        write_piece(z, sent_ref, index, stage_ref, body, total, centre, restart, extra)
+
+
+def read_states(z, got_ref, held_ref, backward):
+    lane = iota((1, LANES), 1)
+    place = jnp.where(lane < HEAD_DIM, lane, lane - HEAD_DIM) // z.slice
+    totals, centres = [], []
+    for number in range(z.rows * z.pairs):
+        total = jnp.zeros((1, LANES), wide)
+        centre = jnp.zeros((HEAD_DIM, LANES), wide)
+        for step in range(z.group):
+            piece = got_ref[number * z.group + step].astype(wide)
+            held_ref[number, step * z.slice : (step + 1) * z.slice, :] = piece[0 : z.slice, :]
+            total = jnp.where(place == step, pair_sum(piece, z.slice), total)
+            if not backward:
+                here = iota((HEAD_DIM, LANES), 0) // z.slice == step
+                centre = jnp.where(here, pair_sum(piece, z.slice + 2), centre)
+        totals.append(total)
+        centres.append(centre)
+    if not backward:
+        high, rest = two_terms(jnp.concatenate(totals, axis=0))
+        columns = rows_in_lanes(jnp.concatenate([high, rest], axis=0))
+        count = len(totals)
+        columns = columns[:, 0:count] + columns[:, count : 2 * count]
+        for number, centre in enumerate(centres):
+            column = columns[:, number : number + 1]
+            spread = jnp.where(
+                first_head((HEAD_DIM, LANES)), column[0:HEAD_DIM], column[HEAD_DIM:LANES]
             )
-
-
-def read_state(z, got_ref, held_ref, row, pair):
-    start = (row * z.pairs + pair) * z.group
-    for step in range(z.group):
-        held_ref[step * z.slice : (step + 1) * z.slice, :] = got_ref[start + step, 0 : z.slice, :]
-    return held_ref[...], got_ref[start, z.slice : z.slice + 1, :]
+            held_ref[number] = held_ref[number] + spread * centre
+    return totals
 
 
 def mask_of(z, cols_ref, segs_ref, row):
@@ -172,7 +246,9 @@
     cols_ref,
     segs_ref,
     sent_ref,
+    means_ref,
     held_ref,
+    stage_ref,
     pre_ref,
 ):
     mine = mine_ref[0]
@@ -226,15 +302,23 @@
         cols_ref[z.span(row), :] = cols
         for pair in range(z.pairs):
             keys = kfeat_ref[z.span(row), lanes_of(pair)].astype(wide) * last
-            product = dot_tn(keys.astype(low), vlow_ref[z.span(row), lanes_of(pair)])
+            keys_low, values = keys.astype(low), vlow_ref[z.span(row), lanes_of(pair)]
+            ones = jnp.ones((z.block, LANES), low)
+            product = dot_tn(keys_low, jnp.concatenate([values, ones], axis=1))
+            spread = compact(product[:, LANES : 2 * LANES])
+            state, centre = centred(compact(product[:, 0:LANES]), spread)
+            line = row * z.pairs + pair
+            means_ref[line : line + 1, :] = column_sums(values.astype(wide)) * (1.0 / z.block)
             write_state(
                 z,
                 sent_ref,
                 held_ref,
+                stage_ref,
                 row,
                 pair,
-                compact(product),
+                state,
                 column_sums(keys),
+                centre,
                 restart,
                 jnp.zeros((1, LANES), wide),
             )
@@ -244,16 +328,55 @@
     return jnp.maximum(values, 0.0) + jnp.log1p(jnp.exp(-jnp.abs(values)))
 
 
-def scan_kernel(z, backward, held_ref, scanned_ref, lowest_ref):
-    flag = z.slice + 1
-    running = jnp.zeros((z.height, LANES), wide)
+def scan_kernel(z, backward, mine_ref, held_ref, scanned_ref, lowest_ref, stage_ref, rows_ref, runs_ref):
+    k = z.slice
+    shift = (mine_ref[z.me] & (z.group - 1)) * k
+    picks = []
+    for head in range(2):
+        hit = iota((k, LANES), 1) == iota((k, LANES), 0) + shift + head * HEAD_DIM
+        picks.append(jnp.where(hit, 1.0, 0.0).astype(low))
+    half = iota((k, LANES), 1) < HEAD_DIM
+    lane = iota((k, LANES), 1)
+    columns = [jnp.zeros((k, LANES), wide) for _ in range(2)]
+    if not backward:
+        for block in range(z.blocks):
+            rows_ref[0, block : block + 1, :] = held_ref[block, k : k + 16, :].astype(wide)[0:1]
+            rows_ref[1, block : block + 1, :] = held_ref[block, k : k + 16, :].astype(wide)[1:2]
+        terms = [rows_ref[i].astype(low) for i in range(2)]
+        columns = [dot_nt(pick, terms[0]) + dot_nt(pick, terms[1]) for pick in picks]
+    run = jnp.zeros((k, LANES), wide)
+    run_total = jnp.zeros((1, LANES), wide)
+    run_spread = jnp.zeros((k, LANES), wide)
     least = jnp.full((1, LANES), LARGE_VALUE, wide)
+    none = jnp.zeros((1, LANES), wide)
     for step in range(z.blocks):
         block = z.blocks - 1 - step if backward else step
-        scanned_ref[block] = running
-        here = held_ref[block]
-        running = here + (1.0 - here[flag : flag + 1, :]) * running
-        least = jnp.minimum(least, here[flag + 1 : flag + 2, :])
+        here = held_ref[block].astype(wide)
+        state, total, centre = here[0:k], pair_sum(here, k), pair_sum(here, k + 2)
+        keep = 1.0 - here[k + 4 : k + 5]
+        least = jnp.minimum(least, pair_sum(here, k + 5))
+        if backward:
+            lost = (run - run.astype(low).astype(wide)) * centre
+            for head in range(2):
+                sums = jnp.sum(only_head(lost, head), axis=1, keepdims=True)
+                columns[head] = jnp.where(lane == block, sums, columns[head])
+            runs_ref[block] = run
+            rows_ref[0, block : block + 1, :] = run_total
+        else:
+            body, middle = centred(run, run_spread)
+            write_piece(z, scanned_ref, block, stage_ref, body, run_total, middle, none, none)
+            spread = jnp.where(
+                half, columns[0][:, block : block + 1], columns[1][:, block : block + 1]
+            )
+            state = state + spread * centre
+            run_spread = spread + keep * run_spread
+        run = state + keep * run
+        run_total = total + keep * run_total
+    if backward:
+        moved = dot_tn(columns[0].astype(low), picks[0]) + dot_tn(columns[1].astype(low), picks[1])
+        for block in range(z.blocks):
+            total = rows_ref[0, block : block + 1, :] + moved[block : block + 1, :]
+            write_piece(z, scanned_ref, block, stage_ref, runs_ref[block], total, none, none, none)
     lowest_ref[...] = jnp.broadcast_to(least, (8, LANES))
 
 
@@ -326,6 +449,7 @@
     wd_ref,
     wd2_ref,
     db_ref,
+    means_ref,
     layer_ref,
     act_ref,
     act2_ref,
@@ -348,6 +472,8 @@
     s_norm,
     s_min,
     held_ref,
+    stage_ref,
+    s_lost,
     s_up,
     s_gact,
 ):
@@ -356,13 +482,14 @@
 
     @pl.when(step == 0)
     def _():
+        totals = read_states(z, got_ref, held_ref, False)
         least = jnp.full((1, 1), LARGE_VALUE, wide)
         for row in range(z.rows):
             carried = cols_ref[z.span(row), 1:2]
             valid = cols_ref[z.span(row), 3:4]
             for pair in range(z.pairs):
                 here = (z.span(row), lanes_of(pair))
-                state, total = read_state(z, got_ref, held_ref, row, pair)
+                state, total = held_ref[row * z.pairs + pair], totals[row * z.pairs + pair]
                 high, rest = two_terms(two_blocks(state))
                 queries = qfeat_ref[here]
                 across = dot(
@@ -439,9 +566,9 @@
         grad_branch = gbr_ref[...]
         gnum_ref[:, 0:a] = dot_nt(grad_branch, wo_ref[...])
         gnum_ref[:, a : 2 * a] = dot_nt(grad_branch, wo2_ref[...])
+        totals, centres = [], []
         for row in range(z.rows):
             carried = cols_ref[z.span(row), 1:2]
-            restart = cols_ref[row * z.block : row * z.block + 1, 4:5]
             table = jnp.zeros((z.block, LANES), wide)
             for pair in range(z.pairs):
                 here = (z.span(row), lanes_of(pair))
@@ -461,18 +588,34 @@
                 product = dot_tn(queries, jnp.concatenate([high, rest], axis=1))
                 product = product[:, 0:LANES] + product[:, LANES : 2 * LANES]
                 total = column_sums(queries.astype(wide) * (grad_norm * carried))
+                state = compact(product)
+                number = row * z.pairs + pair
+                held_ref[number] = state
+                centre = means_ref[number : number + 1, :].astype(low).astype(wide)
+                lost = (state - state.astype(low).astype(wide)) * centre
+                s_lost[number * LANES : (number + 1) * LANES, :] = two_blocks(lost).astype(low)
+                totals.append(total)
+                centres.append(centre)
+            gnorm_ref[z.span(row), :] = table
+        lost = dot_nt(jnp.ones((8, LANES), low), s_lost[...])
+        for row in range(z.rows):
+            restart = cols_ref[row * z.block : row * z.block + 1, 4:5]
+            for pair in range(z.pairs):
+                number = row * z.pairs + pair
+                total = totals[number] + lost[0:1, lanes_of(number)]
                 write_state(
                     z,
                     sent_ref,
                     held_ref,
+                    stage_ref,
                     row,
                     pair,
-                    compact(product),
+                    None,
                     total,
+                    centres[number],
                     restart,
                     s_min[0:1, :],
                 )
-            gnorm_ref[z.span(row), :] = table
 
 
 def local_kernel(
@@ -497,13 +640,14 @@
     a = z.attn
     vec_ref[...] = jnp.zeros_like(vec_ref)
     half = z.pairs // 2
+    totals = read_states(z, got_ref, held_ref, False)
     for row in range(z.rows):
         mask = mask_of(z, cols_ref, segs_ref, row)
         carried = cols_ref[z.span(row), 1:2]
         for pair in range(z.pairs):
             here = (z.span(row), lanes_of(pair))
             queries, keys, values = qfeat_ref[here], kfeat_ref[here], vlow_ref[here]
-            state, total = read_state(z, got_ref, held_ref, row, pair)
+            state, total = held_ref[row * z.pairs + pair], totals[row * z.pairs + pair]
             high, rest = two_terms(two_blocks(state))
             grad_norm = spread_heads(gnorm_ref[z.span(row), 2 * pair : 2 * pair + 2])
             num_high, num_rest = two_terms(gnum_ref[here])
@@ -583,51 +727,95 @@
         give[...] = added(kept[half : 2 * half, :], got[half : 2 * half, :])
 
 
-def second_pair_kernel(level, mine_ref, down_ref, down_got, up_ref, up_got, *outs):
-    rows = outs[0].shape[0] // 2
-    for distance, out_ref in enumerate(outs):
-        start = jnp.bitwise_xor(mine_ref[1 + level.index], distance) * rows
-        span = pl.ds(pl.multiple_of(start, rows), rows)
-        out_ref[0:rows, :] = added(down_ref[span, :], down_got[span, :])
-        out_ref[rows : 2 * rows, :] = added(up_ref[span, :], up_got[span, :])
+def second_pair_kernel(bit, mine_ref, down_ref, down_got, up_ref, up_got, keep_ref, give_ref):
+    upper = mine_ref[bit] > 0
+    down, up = added(down_ref[...], down_got[...]), added(up_ref[...], up_got[...])
+    keep_ref[...] = jnp.where(upper, up, down)
+    give_ref[...] = jnp.where(upper, down, up)
+
+
+def halve_kernel(bit, mine_ref, kept_ref, got_ref, keep_ref, give_ref):
+    rows = keep_ref.shape[0]
+    here = pl.ds(pl.multiple_of(mine_ref[bit] * rows, rows), rows)
+    there = pl.ds(pl.multiple_of((1 - mine_ref[bit]) * rows, rows), rows)
+    keep_ref[...] = added(kept_ref[here, :], got_ref[here, :])
+    give_ref[...] = added(kept_ref[there, :], got_ref[there, :])
+
+
+def add_kernel(kept_ref, got_ref, out_ref):
+    out_ref[...] = added(kept_ref[...], got_ref[...])
+
+
+def double_kernel(bit, mine_ref, own_ref, got_ref, out_ref):
+    rows = own_ref.shape[0]
+    out_ref[pl.ds(pl.multiple_of(mine_ref[bit] * rows, rows), rows), :] = own_ref[...]
+    out_ref[pl.ds(pl.multiple_of((1 - mine_ref[bit]) * rows, rows), rows), :] = got_ref[...]
+
+
+def cut_kernel(one_ref, two_ref, first_ref, second_ref):
+    rows = first_ref.shape[0]
+    first_ref[...] = one_ref[0:rows, :]
+    second_ref[...] = two_ref[rows : 2 * rows, :]
 
 
 def sum_kernel(level, mine_ref, *refs):
-    pieces, outs = refs[: level.radix], refs[level.radix :]
-    rows = outs[0].shape[0]
-    place = mine_ref[1 + level.index + 1] if len(outs) > 1 else None
-    for distance, out_ref in enumerate(outs):
+    pieces, outs, seen = refs[: level.radix], refs[level.radix : -1], refs[-1]
+    rows = pieces[0].shape[0] - 16
+    place = mine_ref[1 + level.index]
+    for distance, piece in enumerate(pieces):
+        seen[jnp.bitwise_xor(place, distance)] = piece[rows : rows + 16, :].astype(wide)
+    vectors = seen[0]
+    for i in range(1, level.radix):
+        vectors = vectors + seen[i]
+    last = outs[-1].dtype == wide
+    parts = outs[:-1] if last else outs
+    part_rows = rows // len(parts)
+    for distance, out_ref in enumerate(parts):
         start = 0
-        if place is not None:
-            start = pl.multiple_of(jnp.bitwise_xor(place, distance) * rows, rows)
-        total = pieces[0][pl.ds(start, rows), :].astype(wide)
+        if not last:
+            start = jnp.bitwise_xor(mine_ref[1 + level.index + 1], distance) * part_rows
+            start = pl.multiple_of(start, part_rows)
+        total = pieces[0][pl.ds(start, part_rows), :].astype(wide)
         for piece in pieces[1:]:
-            total = total + piece[pl.ds(start, rows), :].astype(wide)
-        out_ref[...] = total.astype(low)
+            total = total + piece[pl.ds(start, part_rows), :].astype(wide)
+        out_ref[0:part_rows, :] = total.astype(low)
+        if not last:
+            out_ref[part_rows : part_rows + 16, :] = vectors.astype(low)
+    if last:
+        outs[-1][...] = vectors
 
 
 def join_kernel(level, mine_ref, *refs):
-    pieces, outs = refs[: level.radix], refs[level.radix :]
-    rows = pieces[0].shape[0] // len(outs)
+    pieces, out_ref = refs[: level.radix], refs[level.radix]
+    rows = pieces[0].shape[0]
     for distance, piece in enumerate(pieces):
         place = jnp.bitwise_xor(mine_ref[1 + level.index], distance)
-        for i, out_ref in enumerate(outs):
-            span = pl.ds(pl.multiple_of(place * rows, rows), rows)
-            out_ref[span, :] = piece[i * rows : (i + 1) * rows, :]
-
-
-def unpack_ffn_kernel(z, mine_ref, *refs):
-    downs, ups, (down_ref, up_ref) = refs[:4], refs[4:8], refs[8:]
-    rows = z.hidden // 4
-    fold = z.width // rows
-    tall = z.width // fold
-    for distance in range(4):
-        place = jnp.bitwise_xor(mine_ref[1], distance)
-        span = pl.ds(pl.multiple_of(place * rows, rows), rows)
-        down_ref[span, :] = downs[distance][...].astype(wide)
-        for i in range(fold):
-            lanes = slice(i * rows, (i + 1) * rows)
-            up_ref[i * tall : (i + 1) * tall, span] = ups[distance][:, lanes].astype(wide)
+        out_ref[pl.ds(pl.multiple_of(place * rows, rows), rows), :] = piece[...]
+
+
+def unpack_ffn_kernel(down_ref, up_ref, *refs):
+    down_out, up_out = refs[-2:]
+    rows = down_out.shape[0]
+    fold = up_ref.shape[1] // rows
+    down_out[...] = down_ref[...].astype(wide)
+    tall = up_out.shape[0] // fold
+    for i in range(fold):
+        lanes = slice(i * rows, (i + 1) * rows)
+        up_out[i * tall : (i + 1) * tall, :] = up_ref[:, lanes].astype(wide)
+
+
+def unpack_three_kernel(mine_ref, own_ref, x_ref, y_ref, down_out, up_out):
+    rows = down_out.shape[0]
+    for step, ref in enumerate((own_ref, x_ref, y_ref)):
+
+        @pl.when(pl.program_id(0) == step)
+        def _():
+            down, up = ref.at[0:rows, :], ref.at[rows : 2 * rows, :]
+            unpack_ffn_kernel(down, up, down_out, up_out)
+
+
+def unpack_far_kernel(mine_ref, down_ref, up_ref, down_old, up_old, down_out, up_out):
+    unpack_ffn_kernel(down_ref, up_ref, down_out, up_out)
 
 
 def final_kernel(
@@ -665,6 +853,7 @@
 ):
     a = z.attn
     half = z.pairs // 2
+    totals = read_states(z, got_ref, held_ref, True)
     keep_ref[...] = jnp.zeros_like(keep_ref)
     give_ref[...] = jnp.zeros_like(give_ref)
     for row in range(z.rows):
@@ -672,18 +861,12 @@
         for pair in range(z.pairs):
             here = (z.span(row), lanes_of(pair))
             keys, values = kfeat_ref[here], vlow_ref[here]
-            state, total = read_state(z, got_ref, held_ref, row, pair)
-            high, rest = two_terms(two_blocks(state))
+            state, total = held_ref[row * z.pairs + pair], totals[row * z.pairs + pair]
+            high = two_blocks(state).astype(low)
             grad_k = gk_ref[here].astype(wide) + last * (
-                dot_nt(
-                    jnp.concatenate([values, values], axis=1),
-                    jnp.concatenate([high, rest], axis=1),
-                )
-                + total
+                dot_nt(values, high) + total
             )
-            grad_v = gv_ref[here].astype(wide) + last * dot(
-                jnp.concatenate([keys, keys], axis=1), jnp.concatenate([high, rest], axis=0)
-            )
+            grad_v = gv_ref[here].astype(wide) + last * dot(keys, high)
             grad_k = (grad_k * kslope_ref[here].astype(wide)).astype(low)
             grad_v = grad_v.astype(low)
             out_k, out_v = (gk1_ref, gv1_ref) if pair < half else (gk2_ref, gv2_ref)
@@ -757,12 +940,14 @@
         dot_tn(att_ref[...], gbr_ref[...]) + dot_tn(att2_ref[...], gbr2_ref[...])
     ).astype(low)
     start = w + half + a
-    out_ref[start:, :] = jnp.zeros((out_ref.shape[0] - start, w), low)
-    out_ref[start : start + 16, :] = (keep_ref[...] + got_ref[...]).astype(low)
+    if out_ref.shape[0] > start:
+        out_ref[start:, :] = jnp.zeros((out_ref.shape[0] - start, w), low)
+    vectors = (keep_ref[...] + got_ref[...]).astype(low)
     for distance, out in enumerate(outs):
-        rows = out.shape[0]
+        rows = out.shape[0] - 16
         first_row = jnp.bitwise_xor(mine_ref[1], distance) * rows
-        out[...] = out_ref[pl.ds(pl.multiple_of(first_row, rows), rows), :]
+        out[0:rows, :] = out_ref[pl.ds(pl.multiple_of(first_row, rows), rows), :]
+        out[rows : rows + 16, :] = vectors
 
 
 def place_kernel(mine_ref, one_ref, one2_ref, two_ref, two2_ref, out_one_ref, out_two_ref):
@@ -781,8 +966,8 @@
 
 def unpack_attn_kernel(z, level, mine_ref, *refs):
     pieces, refs = refs[: level.radix], refs[level.radix :]
-    lowest_ref, lowest2_ref, q_ref, k_ref, v_ref, o_ref = refs[:6]
-    vecs, sums_ref = refs[6:17], refs[17]
+    vec_ref, lowest_ref, lowest2_ref, q_ref, k_ref, v_ref, o_ref = refs[:7]
+    vecs, sums_ref = refs[7:18], refs[18]
     join_kernel(level, mine_ref, *pieces, sums_ref)
     a, w = z.attn, z.width
     half = w // 2
@@ -791,8 +976,7 @@
     v_ref[0:half, :] = sums_ref[w : w + half, 0:a].astype(wide)
     v_ref[half:w, :] = sums_ref[w : w + half, a : 2 * a].astype(wide)
     o_ref[...] = sums_ref[w + half : w + half + a, :].astype(wide)
-    start = w + half + a
-    table = sums_ref[start : start + 16, :].astype(wide)
+    table = vec_ref[...]
     g1, b1, ob, g2, b2, db, qb, kb, vb, upb, least = vecs
     for row, out in enumerate((g1, b1, ob, g2, b2, db)):
         out[...] = table[row : row + 1, :]
@@ -835,6 +1019,7 @@
 
 
 HELD = pl.BlockSpec(memory_space=pltpu.VMEM)
+PLACED = pl.BlockSpec(memory_space=pl.ANY)
 
 
 def full(value):
@@ -842,7 +1027,7 @@
     return pl.BlockSpec(dims, lambda *_: (0,) * len(dims))
 
 
-def call(kernel, ins, outs, flops, mine=None, specs=None, out_specs=None, grid=(1,), scratch=(), limit=58, after=None, held=(), held_out=()):
+def call(kernel, ins, outs, flops, mine=None, specs=None, out_specs=None, grid=(1,), scratch=(), limit=58, after=None, held=(), held_out=(), mark=False, aliases=None):
     specs, out_specs = specs or {}, out_specs or {}
     in_list = [specs.get(i, full(value)) for i, value in enumerate(ins)]
     out_list = [out_specs.get(i, full(value)) for i, value in enumerate(outs)]
@@ -851,14 +1036,23 @@
     moved = sum(v.size * v.dtype.itemsize for v in list(ins) + list(outs))
     head = 0 if mine is None else 1
     ins = list(ins)
-    body = kernel
+    outs = list(outs)
+    count_in, count_out = head + len(ins), len(outs)
     if after is not None:
-        spot = head + len(ins)
-        in_list.append(pl.BlockSpec(memory_space=pl.ANY))
+        in_list.append(HELD)
         ins.append(after)
-
-        def body(*refs):
-            kernel(*refs[:spot], *refs[spot + 1 :])
+    if mark:
+        out_list.append(HELD)
+        outs.append(jax.ShapeDtypeStruct((8, LANES), wide))
+
+    def body(*refs):
+        refs = list(refs)
+        if after is not None:
+            refs.pop(count_in)
+        if mark:
+            mark_ref = refs.pop(count_in + count_out)
+            mark_ref[...] = jnp.zeros((8, LANES), wide)
+        kernel(*refs)
 
     return pl.pallas_call(
         body,
@@ -870,6 +1064,7 @@
             scratch_shapes=list(scratch),
         ),
         out_shape=list(outs),
+        input_output_aliases=aliases or {},
         compiler_params=pltpu.CompilerParams(vmem_limit_bytes=limit * MEBI),
         cost_estimate=pl.CostEstimate(flops=int(flops), bytes_accessed=int(moved), transcendentals=0),
     )(*(() if mine is None else (mine,)), *ins)
@@ -906,7 +1101,11 @@
     levels = levels_of(blocks)
     me = lax.axis_index("seq")
     places = [(me >> level.shift) & (level.radix - 1) for level in levels]
-    mine = jnp.stack([lax.axis_index("mp")] + places).astype(jnp.int32)
+    far_bits = [1 << k for k in range(2, blocks.bit_length() - 1)]
+    signs = [(me & bit) // bit for bit in far_bits]
+    mine = jnp.stack([lax.axis_index("mp")] + places + signs + [me]).astype(jnp.int32)
+    z.me = mine.shape[0] - 1
+    first_bit = 1 + len(levels)
 
     def row(vector):
         return vector.reshape(1, vector.shape[0])
@@ -923,12 +1122,13 @@
         return pl.BlockSpec((z.rows, block, width), lambda i, m: (m[0], 0, 0))
 
     part = functools.partial
-    sent_shape = shape((blocks, z.height, LANES), wide)
-    state_scratch = pltpu.VMEM((HEAD_DIM, LANES), wide)
+    sent_shape = shape((blocks, z.height, LANES), low)
+    stage = pltpu.VMEM((z.height, LANES), wide)
+    state_scratch = pltpu.VMEM((z.rows * z.pairs, HEAD_DIM, LANES), wide)
     thin = shape((t, LANES), wide)
     narrow, broad, half = shape((t, width), low), shape((t, width), wide), shape((t, a), low)
 
-    first, kslope, kfeat, vlow, cols, segs, sent = call(
+    first, kslope, kfeat, vlow, cols, segs, sent, means = call(
         part(project_kernel, z),
         (
             tokens,
@@ -952,11 +1152,12 @@
             thin,
             shape((8 * z.rows, block), wide),
             sent_shape,
+            shape((z.rows * z.pairs, LANES), wide),
         ),
         4e9,
         mine,
         specs={0: own_block()},
-        scratch=[state_scratch, pltpu.VMEM((2, t, a), wide)],
+        scratch=[state_scratch, stage, pltpu.VMEM((2, t, a), wide)],
     )
 
     def scan(held, backward, after):
@@ -965,21 +1166,28 @@
             (held,),
             (sent_shape, shape((8, LANES), wide)),
             1e8,
-            limit=8,
+            mine,
+            scratch=[
+                stage,
+                pltpu.VMEM((2, blocks, LANES), wide),
+                pltpu.VMEM((blocks, z.slice, LANES), wide),
+            ],
+            limit=10,
             after=after,
             held=(0,),
             held_out=(0, 1),
         )
 
     arriving = over_blocks(sent)
-    qslope, qfeat, weights, within, sums = call(
+    qslope, qfeat, weights, within, sums, mark = call(
         part(score_kernel, z),
         (first, query_weight, wq2, row(query_bias), other_bias, kfeat, vlow, cols, segs),
         (narrow, narrow, shape((z.rows * z.pairs * 2, block, block), low), broad, thin),
         4e9,
         scratch=[pltpu.VMEM((2, t, a), wide)],
+        mark=True,
     )
-    entering, _ = scan(arriving, False, qfeat)
+    entering, _ = scan(arriving, False, mark)
     entering = over_blocks(entering)
     steps = hidden // width
     up_block = pl.BlockSpec((width, width), lambda i, m: (0, i))
@@ -1024,6 +1232,7 @@
             down_weight,
             wd2,
             db,
+            means,
         ),
         (
             narrow,
@@ -1065,218 +1274,347 @@
             pltpu.VMEM((t, 2 * a), wide),
             pltpu.VMEM((8, LANES), wide),
             state_scratch,
+            stage,
+            pltpu.VMEM((z.rows * z.pairs * LANES, LANES), low),
             pltpu.VMEM((z.rows, block, width), wide),
             pltpu.VMEM((z.rows, block, width), wide),
         ],
     )
     act_in, gup_in, second_in = swap(act2), swap(gup2), swap(second)
-    leaving = over_blocks(sent_back)
     piece = hidden // 4
     act_block = pl.BlockSpec((t, piece), lambda i, m: (0, jnp.bitwise_xor(m[1], i)))
     two = shape((2 * piece, width), low)
     one = shape((piece, width), low)
-    down_keep, down_give, up_keep, up_give = call(
-        part(ffn_grad_kernel, z),
-        (act, act_in, cotangent, cotangent, second, second_in, gup, gup_in),
-        (two, two, two, two),
-        4e9,
-        mine,
-        specs={
-            0: act_block,
-            1: act_block,
-            2: own_block(),
-            3: own_block(True),
-            6: act_block,
-            7: act_block,
-        },
-        grid=(4,),
-    )
+    table = shape((16, width), wide)
+    height = max(2 * width, 16 * blocks)
+    radix = levels[0].radix
 
     def to(value, distance):
         return levels[0].exchange(value, distance, blocks)
 
+    def far(value, bit):
+        return lax.ppermute(value, "seq", [(i, i ^ bit) for i in range(blocks)])
+
     def spread(level, parts):
         return [parts[0]] + [level.exchange(p, d, blocks) for d, p in enumerate(parts) if d]
 
+    def small(kernel, ins, dims, after, scalars=None, scratch=()):
+        outs = [shape(dim, low) if isinstance(dim, tuple) else dim for dim in dims]
+        *outs, marks["last"] = call(
+            kernel,
+            ins,
+            outs,
+            1e6,
+            scalars,
+            limit=8,
+            after=after,
+            held=range(len(ins)),
+            held_out=range(len(outs)),
+            mark=True,
+            scratch=scratch,
+        )
+        return outs
+
+    marks = {}
+
     def summed(number, parts, after):
         level = levels[number]
-        following = levels[number + 1].radix if number + 1 < len(levels) else 1
-        rows = parts[0].shape[0] // following
-        return call(
-            part(sum_kernel, level),
-            parts,
-            [shape((rows, width), low)] * following,
+        rows = parts[0].shape[0] - 16
+        outs = [shape((rows, width), low), shape((16, width), wide)]
+        if number + 1 < len(levels):
+            following = levels[number + 1].radix
+            outs = [shape((rows // following + 16, width), low)] * following
+        seen = [pltpu.VMEM((level.radix, 16, width), wide)]
+        return small(part(sum_kernel, level), parts, outs, after, mine, seen)
+
+    def joined(number, value, after):
+        level = levels[number]
+        dims = [(level.radix * value.shape[0], width)]
+        parts = spread(level, [value] * level.radix)
+        return small(part(join_kernel, level), parts, dims, after, mine)[0]
+
+    v = {"leaving": over_blocks(sent_back)}
+
+    def ffn_gradients(after):
+        down_keep, down_give, up_keep, up_give, mark = call(
+            part(ffn_grad_kernel, z),
+            (act, act_in, cotangent, cotangent, second, second_in, gup, gup_in),
+            (two, two, two, two),
+            4e9,
+            mine,
+            specs={
+                0: act_block,
+                1: act_block,
+                2: own_block(),
+                3: own_block(True),
+                6: act_block,
+                7: act_block,
+            },
+            grid=(4,),
+            after=after,
+            mark=True,
+        )
+        v["down"], v["up"] = (down_keep, to(down_give, 1)), (up_keep, to(up_give, 2))
+        return mark
+
+    def backward_scan(after):
+        leaving, v["lowest"] = scan(v["leaving"], True, after)
+        v["leaving"] = over_blocks(leaving)
+        return v["lowest"]
+
+    def local_gradients(after):
+        *v["local"], mark = call(
+            part(local_kernel, z),
+            (entering, weights, qfeat, kfeat, vlow, gnum, gnorm, qslope, cols, segs),
+            (half, half, narrow, narrow, shape((8, 2 * a), wide)),
+            6e9,
+            scratch=[state_scratch],
+            after=after,
+            mark=True,
+        )
+        return mark
+
+    def final_gradients(after):
+        gq, gq2, gk_local, gv_local, vec_loc = v["local"]
+        *v["final"], mark = call(
+            part(final_kernel, z),
+            (
+                v["leaving"],
+                kfeat,
+                vlow,
+                kslope,
+                gk_local,
+                gv_local,
+                cols,
+                gq,
+                gq2,
+                query_weight,
+                wq2,
+                key_weight,
+                wk2,
+                value_weight,
+                wv2,
+                tokens,
+                g1,
+                gbr,
+                vec_mid,
+                vec_loc,
+            ),
+            (half, half, half, half, narrow, table, table),
+            4e9,
+            mine,
+            specs={15: own_block()},
+            scratch=[state_scratch, pltpu.VMEM((t, width), wide)],
+            held=(0,),
+            after=after,
+            mark=True,
+        )
+        return mark
+
+    def first_pair(after):
+        dims = [(piece, width)] * 4
+        ins = v["down"] + v["up"]
+        down_keep, down_give, up_keep, up_give = small(first_pair_kernel, ins, dims, after)
+        v["down"], v["up"] = (down_keep, to(down_give, 2)), (up_keep, to(up_give, 1))
+        return marks["last"]
+
+    def attn_gradients(after):
+        gq, gq2 = v["local"][:2]
+        gk, gk2, gv, gv2, _, keep, give = v["final"]
+        *v["rest"], mark = call(
+            part(attn_grad_kernel, z, radix),
+            (
+                first,
+                swap(first),
+                gq,
+                swap(gq2),
+                gk,
+                swap(gk2),
+                gv,
+                swap(gv2),
+                att,
+                swap(att2),
+                gbr,
+                swap(gbr),
+                keep,
+                swap(give),
+            ),
+            [shape((height // radix + 16, width), low)] * radix,
+            2e9,
+            mine,
+            scratch=[pltpu.VMEM((height, width), low)],
+            after=after,
+            mark=True,
+        )
+        v["rest"] = spread(levels[0], v["rest"])
+        return mark
+
+    def second_pair(after):
+        dims = [(piece, width)] * 2
+        ins = v["down"] + v["up"]
+        keep, give = small(part(second_pair_kernel, first_bit), ins, dims, after, mine)
+        v["ffn"] = (keep, far(give, far_bits[0]))
+        return marks["last"]
+
+    def first_half(after):
+        dims = [(v["ffn"][0].shape[0] // 2, width)] * 2
+        kernel = part(halve_kernel, first_bit + 1)
+        keep, give = small(kernel, v["ffn"], dims, after, mine)
+        v["ffn"] = (keep, far(give, far_bits[1]))
+        return marks["last"]
+
+    def last_half(after):
+        for number in range(2, len(far_bits)):
+            dims = [(v["ffn"][0].shape[0] // 2, width)] * 2
+            kernel = part(halve_kernel, first_bit + number)
+            keep, give = small(kernel, v["ffn"], dims, after, mine)
+            v["ffn"] = (keep, far(give, far_bits[number]))
+        (out,) = small(add_kernel, v["ffn"], [v["ffn"][0].shape], after)
+        v["ffn"] = (out, far(out, far_bits[-1]))
+        return marks["last"]
+
+    def first_double(after):
+        for number in reversed(range(1, len(far_bits))):
+            dims = [(2 * v["ffn"][0].shape[0], width)]
+            (out,) = small(part(double_kernel, first_bit + number), v["ffn"], dims, after, mine)
+            v["ffn"] = (out, far(out, far_bits[number - 1]))
+        return marks["last"]
+
+    def last_double(after):
+        dims = [(2 * v["ffn"][0].shape[0], width)]
+        (out,) = small(part(double_kernel, first_bit), v["ffn"], dims, after, mine)
+        v["ffn"] = (out, to(out, 1), to(out, 2))
+        return marks["last"]
+
+    def cut(after):
+        out, out_x, out_y = v["ffn"]
+        far_down, far_up = small(cut_kernel, (out_y, out_x), [(piece, width)] * 2, after)
+        v["ffn"] = (out, out_x, out_y, to(far_down, 1), to(far_up, 2))
+        return marks["last"]
+
+    def first_sum(after):
+        v["rest"] = summed(0, v["rest"], after)
+        out = v["rest"][0]
+        v["rest"] = spread(levels[1], v["rest"])
+        return marks["last"]
+
+    def last_sum(after):
+        for number in range(1, len(levels)):
+            v["rest"] = summed(number, v["rest"], after)
+            if number + 1 < len(levels):
+                v["rest"] = spread(levels[number + 1], v["rest"])
+        return marks["last"]
+
+    def join(after):
+        out, v["vectors"] = v["rest"]
+        for number in range(len(levels) - 1, 0, -1):
+            out = joined(number, out, after)
+        v["rest"] = spread(levels[0], [out] * radix)
+        return marks["last"]
+
+    def place(after):
+        placed = pl.BlockSpec(
+            (z.rows, block, width), lambda i, m: (jnp.where(i == 0, m[0], 1 - m[0]), 0, 0)
+        )
+        gtok = v["final"][4]
+        *v["out"], mark = call(
+            place_kernel,
+            (layer, swap(layer), gtok, swap(gtok)),
+            (shape(tokens.shape, low), shape(tokens.shape, wide)),
             1e6,
             mine,
-            limit=8,
+            out_specs={0: placed, 1: placed},
+            grid=(2,),
             after=after,
-            held=range(len(parts)),
-            held_out=range(following),
+            mark=True,
         )
-
-    def joined(number, value, count, after):
-        level = levels[number]
-        rows = level.radix * value.shape[0] // count
-        return call(
-            part(join_kernel, level),
-            spread(level, [value] * level.radix),
-            [shape((rows, width), low)] * count,
+        return mark
+
+    def piece_blocks(step):
+        return [
+            pl.BlockSpec((piece, width), lambda i, m: (jnp.bitwise_xor(m[1], i + step), 0)),
+            pl.BlockSpec((width, piece), lambda i, m: (0, jnp.bitwise_xor(m[1], i + step))),
+        ]
+
+    def unpack_three(after):
+        outs = (shape((hidden, width), wide), shape((width, hidden), wide))
+        *v["grads"], mark = call(
+            unpack_three_kernel,
+            v["ffn"][:3],
+            outs,
             1e6,
             mine,
-            limit=8,
+            out_specs=dict(enumerate(piece_blocks(0))),
+            grid=(3,),
             after=after,
-            held=range(level.radix),
-            held_out=range(count),
+            mark=True,
         )
-
-    leaving, lowest = scan(leaving, True, down_keep)
-    scanned = lowest
-    leaving = over_blocks(leaving)
-    down_got, up_got = to(down_give, 1), to(up_give, 2)
-    gq, gq2, gk_local, gv_local, vec_loc = call(
-        part(local_kernel, z),
-        (entering, weights, qfeat, kfeat, vlow, gnum, gnorm, qslope, cols, segs),
-        (half, half, narrow, narrow, shape((8, 2 * a), wide)),
-        6e9,
-        scratch=[state_scratch],
-        after=scanned,
+        return mark
+
+    def unpack_far(after):
+        outs = (shape((hidden, width), wide), shape((width, hidden), wide))
+        *v["ffn"], mark = call(
+            unpack_far_kernel,
+            (*v["ffn"][3:], *v["grads"]),
+            outs,
+            1e6,
+            mine,
+            specs={2: PLACED, 3: PLACED},
+            out_specs=dict(enumerate(piece_blocks(3))),
+            after=after,
+            mark=True,
+            aliases={3: 0, 4: 1},
+        )
+        return mark
+
+    def unpack_attn(after):
+        *v["rest"], mark = call(
+            part(unpack_attn_kernel, z, levels[0]),
+            (*v["rest"], v["vectors"], v["lowest"], swap(v["lowest"])),
+            (
+                shape((width, a), wide),
+                shape((width, a), wide),
+                shape((width, a), wide),
+                shape((a, width), wide),
+            )
+            + tuple(shape((1, width), wide) for _ in range(6))
+            + tuple(shape((1, a), wide) for _ in range(3))
+            + (shape((1, hidden), wide), shape((1, 1), wide)),
+            1e6,
+            mine,
+            scratch=[pltpu.VMEM((height, width), low)],
+            after=after,
+            mark=True,
+        )
+        return mark
+
+    steps = dict(
+        KF=ffn_gradients,
+        S=backward_scan,
+        KD=local_gradients,
+        KE=final_gradients,
+        KG=attn_gradients,
+        p1=first_pair,
+        p2=second_pair,
+        h1=first_half,
+        h2=last_half,
+        d1=first_double,
+        d2=last_double,
+        c=cut,
+        s1=first_sum,
+        s2=last_sum,
+        j=join,
+        P=place,
+        U3=unpack_three,
+        UA=unpack_far,
+        UB=unpack_attn,
     )
-    table = shape((16, width), wide)
-    gk, gk2, gv, gv2, gtok, keep, give = call(
-        part(final_kernel, z),
-        (
-            leaving,
-            kfeat,
-            vlow,
-            kslope,
-            gk_local,
-            gv_local,
-            cols,
-            gq,
-            gq2,
-            query_weight,
-            wq2,
-            key_weight,
-            wk2,
-            value_weight,
-            wv2,
-            tokens,
-            g1,
-            gbr,
-            vec_mid,
-            vec_loc,
-        ),
-        (half, half, half, half, narrow, table, table),
-        4e9,
-        mine,
-        specs={15: own_block()},
-        scratch=[state_scratch, pltpu.VMEM((t, width), wide)],
-        held=(0,),
-    )
-    down_keep, down_give, up_keep, up_give = call(
-        first_pair_kernel,
-        (down_keep, down_got, up_keep, up_got),
-        (one, one, one, one),
-        1e6,
-        limit=8,
-        after=keep,
-        held=range(4),
-        held_out=range(4),
-    )
-    down_got, up_got = to(down_give, 2), to(up_give, 1)
-    unit = 16 * blocks
-    height = -(-(2 * width + 16) // unit) * unit
-    radix = levels[0].radix
-    rest = call(
-        part(attn_grad_kernel, z, radix),
-        (
-            first,
-            swap(first),
-            gq,
-            swap(gq2),
-            gk,
-            swap(gk2),
-            gv,
-            swap(gv2),
-            att,
-            swap(att2),
-            gbr,
-            swap(gbr),
-            keep,
-            swap(give),
-        ),
-        [shape((height // radix, width), low)] * radix,
-        2e9,
-        mine,
-        scratch=[pltpu.VMEM((height, width), low)],
-        after=down_keep,
-    )
-    rest_done = rest[0]
-    radix = levels[1].radix
-    parts = call(
-        part(second_pair_kernel, levels[1]),
-        (down_keep, down_got, up_keep, up_got),
-        [shape((2 * piece // radix, width), low)] * radix,
-        1e6,
-        mine,
-        limit=8,
-        after=rest_done,
-        held=range(4),
-        held_out=range(radix),
-    )
-    for number in range(1, len(levels)):
-        parts = summed(number, spread(levels[number], parts), rest_done)
-    (ffn,) = parts
-    rest = summed(0, spread(levels[0], rest), ffn)
-    for number in range(len(levels) - 1, 1, -1):
-        (ffn,) = joined(number, ffn, 1, rest[0])
-    down, up = joined(1, ffn, 2, rest[0])
-    for number in range(1, len(levels)):
-        rest = summed(number, spread(levels[number], rest), down)
-    (rest,) = rest
-    down_x, down_y, up_x, up_y = to(down, 1), to(down, 2), to(up, 1), to(up, 2)
-    ffn_pieces = (down, down_x, down_y, to(down_y, 1), up, up_x, up_y, to(up_x, 2))
-    placed = pl.BlockSpec(
-        (z.rows, block, width), lambda i, m: (jnp.where(i == 0, m[0], 1 - m[0]), 0, 0)
-    )
-    layer_out, grad_tokens = call(
-        place_kernel,
-        (layer, swap(layer), gtok, swap(gtok)),
-        (shape(tokens.shape, low), shape(tokens.shape, wide)),
-        1e6,
-        mine,
-        out_specs={0: placed, 1: placed},
-        grid=(2,),
-        after=rest,
-    )
-    for number in range(len(levels) - 1, 0, -1):
-        (rest,) = joined(number, rest, 1, grad_tokens)
-    rest_pieces = spread(levels[0], [rest] * levels[0].radix)
-    grad_down, grad_up = call(
-        part(unpack_ffn_kernel, z),
-        ffn_pieces,
-        (shape((hidden, width), wide), shape((width, hidden), wide)),
-        1e6,
-        mine,
-        after=rest,
-    )
-    (grad_q, grad_k, grad_v, grad_o, g1, b1, ob, g2, b2, db, qb, kb, vb, upb, least) = call(
-        part(unpack_attn_kernel, z, levels[0]),
-        (*rest_pieces, lowest, swap(lowest)),
-        (
-            shape((width, a), wide),
-            shape((width, a), wide),
-            shape((width, a), wide),
-            shape((a, width), wide),
-        )
-        + tuple(shape((1, width), wide) for _ in range(6))
-        + tuple(shape((1, a), wide) for _ in range(3))
-        + (shape((1, hidden), wide), shape((1, 1), wide)),
-        1e6,
-        mine,
-        scratch=[pltpu.VMEM((height, width), low)],
-        after=grad_down,
-    )
+    after = None
+    for name in ORDER:
+        after = steps[name](after)
+    layer_out, grad_tokens = v["out"]
+    grad_down, grad_up = v["ffn"]
+    grad_q, grad_k, grad_v, grad_o, g1, b1, ob, g2, b2, db, qb, kb, vb, upb, least = v["rest"]
 
     def flat(table):
         return table.reshape(table.shape[1])

time: 208 us -> 192 us (0.923)
  waiting for transfers between devices: 54.6 us -> 37.4 us
  Pallas kernels: 73.6 us -> 79.1 us
  local copies, waits for them, and re-layouts: 16.5 us -> 14 us
    ppermute x28 -> x20, waiting for transfers between devices: 36.6 us -> 19.4 us  [exchange(): return lax.ppermute(value, 'seq', [(i, i ^ other) for i in range(count)])]
    ppermute x28 -> x20, starting transfers between devices: 35.3 us -> 24.4 us  [exchange(): return lax.ppermute(value, 'seq', [(i, i ^ other) for i in range(count)])]
    ppermute x0 -> x4, waiting for transfers between devices: none -> 7.01 us  [far(): return lax.ppermute(value, 'seq', [(i, i ^ bit) for i in range(blocks)])]
    ppermute x0 -> x4, starting transfers between devices: none -> 6.5 us  [far(): return lax.ppermute(value, 'seq', [(i, i ^ bit) for i in range(blocks)])]
    all_to_all x4, waiting for transfers between devices: 14.5 us -> 8.68 us  [over_blocks(): return lax.all_to_all(value, 'seq', 0, 0)]
    pallas_call x19 -> x23, Pallas kernels: 73.6 us -> 79.1 us  [call(): pl.pallas_call(body, grid_spec=pltpu.PrefetchScalarGridSpec(num_scalar_pr...]
    all_to_all x4, starting transfers between devices: 20 us -> 23.1 us  [over_blocks(): return lax.all_to_all(value, 'seq', 0, 0)]
    unnamed x110 -> x102, local copies, waits for them, and re-layouts: 15.9 us -> 12.8 us
  transfers between devices with their start and end apart: 52 -> 48, of which waited for: 18 -> 18; matrix products, arithmetic and copies ran while one was open for 1% -> 1% of each run, Pallas kernels for 25% -> 30%
where the time goes in v2:
time: 192 us; the launch traced here: 191 us
  Pallas kernels  79.1 us (41%)
  starting transfers between devices  58.3 us (30%)
  waiting for transfers between devices  37.4 us (19%)
  local copies, waits for them, and re-layouts  14 us (7%)
    pallas_call x23, Pallas kernels, call(): pl.pallas_call(body, grid_spec=pltpu.PrefetchScalarGridSpec(num_scalar_pr...  79.1 us
    ppermute x20, starting transfers between devices, exchange(): return lax.ppermute(value, 'seq', [(i, i ^ other) for i in range(count)])  24.4 us
    all_to_all x4, starting transfers between devices, over_blocks(): return lax.all_to_all(value, 'seq', 0, 0)  23.1 us
    ppermute x20, waiting for transfers between devices, exchange(): return lax.ppermute(value, 'seq', [(i, i ^ other) for i in range(count)])  19.4 us
    unnamed x102, local copies, waits for them, and re-layouts  12.8 us
    all_to_all x4, waiting for transfers between devices, over_blocks(): return lax.all_to_all(value, 'seq', 0, 0)  8.68 us
    ppermute x4, waiting for transfers between devices, far(): return lax.ppermute(value, 'seq', [(i, i ^ bit) for i in range(blocks)])  7.01 us
    ppermute x4, starting transfers between devices, far(): return lax.ppermute(value, 'seq', [(i, i ^ bit) for i in range(blocks)])  6.5 us
  transfers between devices with their start and end apart: 48, of which 18 were waited for; matrix products, arithmetic and copies ran while one was open for 1% of the time, Pallas kernels for 30%

profile of v2, /device:TPU:0, one launch (start us, length us, event | category | flops | bytes accessed | tf_op | source)
XLA Modules:
  0.0 190.8 jit_solution(15723557371921028760)
XLA Ops:
  4.5 5.1 %shard_map.339 = (bf16[512,512]{1,0:T(8,128)(2,1)}, bf16[512,512]{1,0:T(8,128)(2,1)}, bf16[512,512]{1,0:T(8,128)(2,1)}, bf16[512,512]{1,0:T(8,128)(2,1)}, f32[51...) custom-call(s32[6]{0:T(128)} %stack.27.refs_0_, ...), custom_call_target="tpu_custom_call" | custom-call | flops 4000000000 | bytes 4695040 | tf_op jit(solution)/shard_map/pallas_call | solution.py:1057
  9.6 8.3 %all-to-all-start = ((bf16[16,48,128]{2,1,0:T(8,128)(2,1)}), bf16[16,48,128]{2,1,0:T(8,128)(2,1)S(1)}, u32[]{:S(2)}, u32[]{:S(2)}) async-start(bf16[16,48,128]{2,1,0:T(8,128)(2,1)} %get-tuple-element.127), calls=%async_computation | async-start | bytes 393216 | tf_op jit(solution)/shard_map/all_to_all | solution.py:996
  18.6 6.1 %shard_map.340 = (bf16[512,512]{1,0:T(8,128)(2,1)}, bf16[512,512]{1,0:T(8,128)(2,1)}, bf16[16,256,256]{2,1,0:T(8,128)(2,1)}, f32[512,512]{1,0:T(8,128)}, f32[512,128]{1,0:T(8,128)}, /*index=5*/f32[8,128]{1,0:T(8,128)}) custom-call(bf16[512,512]{1,0:T(8,128)(2,1)} %get-tuple-element.128.refs_0_.refs_1_, bf16[512,256]{1,0:T(8,128)(2,1)} %refs_10_.1, ...), custom_call_target="tpu_custom_call" | custom-call | flops 4000000000 | bytes 6840320 | tf_op jit(solution)/shard_map/pallas_call | solution.py:1057
  24.7 2.1 %all-to-all-done.refs_1_ = bf16[16,48,128]{2,1,0:T(8,128)(2,1)S(1)} async-done(((bf16[16,48,128]{2,1,0:T(8,128)(2,1)}), bf16[16,48,128]{2,1,0:T(8,128)(2,1)S(1)}, u32[]{:S(2)}, u32[]{:S(2)}) %all-to-all-start) | async-done | bytes 196640 | tf_op jit(solution)/shard_map/all_to_all | solution.py:996
  27.5 1.7 shard_map.341
  29.2 4.8 %all-to-all-start.1 = ((bf16[16,48,128]{2,1,0:T(8,128)(2,1)}), bf16[16,48,128]{2,1,0:T(8,128)(2,1)S(1)}, u32[]{:S(2)}, u32[]{:S(2)}) async-start(bf16[16,48,128]{2,1,0:T(8,128)(2,1)} %get-tuple-element.134), calls=%async_computation.1 | async-start | bytes 393216 | tf_op jit(solution)/shard_map/all_to_all | solution.py:996
  35.6 6.5 %all-to-all-done.1.refs_1_.refs_0_ = bf16[16,48,128]{2,1,0:T(8,128)(2,1)S(1)} async-done(((bf16[16,48,128]{2,1,0:T(8,128)(2,1)}), bf16[16,48,128]{2,1,0:T(8,128)(2,1)S(1)}, u32[]{:S(2)}, u32[]{:S(2)}) %all-to-all-start.1) | async-done | bytes 196640 | tf_op jit(solution)/shard_map/all_to_all | solution.py:996
  43.5 18.2 %shard_map.342 = (bf16[512,512]{1,0:T(8,128)(2,1)}, bf16[512,1024]{1,0:T(8,128)(2,1)}, bf16[512,1024]{1,0:T(8,128)(2,1)}, bf16[512,1024]{1,0:T(8,128)(2,1)}, bf1...) custom-call(s32[6]{0:T(128)} %stack.27.refs_0_, ...), custom_call_target="tpu_custom_call" | custom-call | flops 12000000000 | bytes 16961536 | tf_op jit(solution)/shard_map/pallas_call | solution.py:1057
  62.8 3.5 %all-to-all-start.2 = ((bf16[16,48,128]{2,1,0:T(8,128)(2,1)}), bf16[16,48,128]{2,1,0:T(8,128)(2,1)S(1)}, u32[]{:S(2)}, u32[]{:S(2)}) async-start(bf16[16,48,128]{2,1,0:T(8,128)(2,1)} %get-tuple-element.140), calls=%async_computation.2 | async-start | bytes 393216 | tf_op jit(solution)/shard_map/all_to_all | solution.py:996
  68.6 7.9 %shard_map.343 = (bf16[512,512]{1,0:T(8,128)(2,1)}, bf16[512,512]{1,0:T(8,128)(2,1)}, bf16[512,512]{1,0:T(8,128)(2,1)}, bf16[512,512]{1,0:T(8,128)(2,1)}, f32[8,128]{1,0:T(8,128)}) custom-call(s32[6]{0:T(128)} %stack.27.refs_0_, bf16[512,1024]{1,0:T(8,128)(2,1)} %get-tuple-element.141.refs_1_, bf16[512,1024]{1,0:T(8,128)(2,1)} %copy-done.39, ...), custom_call_target="tpu_custom_call" | custom-call | flops 4000000000 | bytes 9437184 | tf_op jit(solution)/shard_map/pallas_call | solution.py:1057
  77.2 1.7 shard_map.344
  79.5 6.5 %all-to-all-start.3 = ((bf16[16,48,128]{2,1,0:T(8,128)(2,1)}), bf16[16,48,128]{2,1,0:T(8,128)(2,1)S(1)}, u32[]{:S(2)}, u32[]{:S(2)}) async-start(bf16[16,48,128]{2,1,0:T(8,128)(2,1)} %get-tuple-element.147), calls=%async_computation.3 | async-start | bytes 393216 | tf_op jit(solution)/shard_map/all_to_all | solution.py:996
  86.0 2.0 %collective-permute-start.12 = (bf16[512,512]{1,0:T(8,128)(2,1)}, bf16[512,512]{1,0:T(8,128)(2,1)S(1)}, u32[]{:S(2)}, u32[]{:S(2)}) collective-permute-start(bf16[512,512]{1,0:T(8,128)(2,1)} %get-tuple-element.164), channel_id=1, source_target_pairs={{0,2},{2,0},{4,6},{6,4},{8,10},{10,8},{12,14},{14,12},{16,18},{18,... | collective-permute-start | bytes 1572872 | tf_op jit(solution)/shard_map/ppermute | solution.py:1005
  89.4 8.0 %shard_map.345 = (bf16[512,256]{1,0:T(8,128)(2,1)}, bf16[512,256]{1,0:T(8,128)(2,1)}, bf16[512,512]{1,0:T(8,128)(2,1)}, bf16[512,512]{1,0:T(8,128)(2,1)}, f32[8,512]{1,0:T(8,128)}, /*index=5*/f32[8,128]{1,0:T(8,128)}) custom-call(bf16[16,48,128]{2,1,0:T(8,128)(2,1)} %copy-done.31, bf16[16,256,256]{2,1,0:T(8,128)(2,1)} %get-tuple-element.149.refs_1_, ...), custom_call_target="tpu_custom_call" | custom-call | flops 6000000000 | bytes 7569408 | tf_op jit(solution)/shard_map/pallas_call | solution.py:1057
  98.4 6.3 %shard_map.346 = (bf16[512,256]{1,0:T(8,128)(2,1)}, bf16[512,256]{1,0:T(8,128)(2,1)}, bf16[512,256]{1,0:T(8,128)(2,1)}, bf16[512,256]{1,0:T(8,128)(2,1)}, bf16[5...) custom-call(s32[6]{0:T(128)} %stack.27.refs_0_, ...), custom_call_target="tpu_custom_call" | custom-call | flops 4000000000 | bytes 8439808 | tf_op jit(solution)/shard_map/pallas_call | solution.py:1057
  109.0 5.3 %shard_map.348 = (bf16[272,512]{1,0:T(8,128)(2,1)}, bf16[272,512]{1,0:T(8,128)(2,1)}, bf16[272,512]{1,0:T(8,128)(2,1)}, bf16[272,512]{1,0:T(8,128)(2,1)}, f32[8,128]{1,0:T(8,128)}) custom-call(s32[6]{0:T(128)} %stack.27.refs_0_, bf16[512,512]{1,0:T(8,128)(2,1)} %get-tuple-element.128.refs_0_.refs_1_, bf16[512,512]{1,0:T(8,128)(2,1)} %copy-done.41, ...), custom_call_target="tpu_custom_call" | custom-call | flops 2000000000 | bytes 5373952 | tf_op jit(solution)/shard_map/pallas_call | solution.py:1057
  121.2 1.8 collective-permute-start.25
  123.8 4.1 %shard_map.350 = (bf16[4,256,512]{2,1,0:T(8,128)(2,1)}, f32[4,256,512]{2,1,0:T(8,128)}, f32[8,128]{1,0:T(8,128)}) custom-call(s32[6]{0:T(128)} %stack.27.refs_0_, bf16[512,512]{1,0:T(8,128)(2,1)} %get-tuple-element.139.refs_1_, bf16[512,512]{1,0:T(8,128)(2,1)} %copy-done.24, bf16[512,512]{1,0:T(8,128)(2,1)} %get-tuple-element.162.refs_3_, ...), custom_call_target="tpu_custom_call" | custom-call | flops 1000000 | bytes 5242880 | tf_op jit(solution)/shard_map/pallas_call | solution.py:1057
  129.2 2.4 %collective-permute-start.30 = (bf16[128,512]{1,0:T(8,128)(2,1)S(1)}, bf16[128,512]{1,0:T(8,128)(2,1)S(1)}, u32[]{:S(2)}, u32[]{:S(2)}) collective-permute-start(bf16[128,512]{1,0:T(8,128)(2,1)S(1)} %get-tuple-element.198), channel_id=1, source_target_pairs={{0,16},{2,18},{4,20},{6,22},{8,24},{10,26},{12,28},{14,30},{16,0},... | collective-permute-start | bytes 393224 | tf_op jit(solution)/shard_map/ppermute | solution.py:1296
  131.6 2.3 %collective-permute-done.24.refs_3_ = bf16[272,512]{1,0:T(8,128)(2,1)S(1)} collective-permute-done((bf16[272,512]{1,0:T(8,128)(2,1)}, bf16[272,512]{1,0:T(8,128)(2,1)S(1)}, u32[]{:S(2)}, u32[]{:S(2)}) %collective-permute-start.24) | collective-permute-done | bytes 278560 | tf_op jit(solution)/shard_map/ppermute | solution.py:1005
  134.7 1.9 collective-permute-done.30.refs_1_
  137.7 1.9 collective-permute-start.27
  139.7 2.4 %collective-permute-start.29 = (bf16[80,512]{1,0:T(8,128)(2,1)S(1)}, bf16[80,512]{1,0:T(8,128)(2,1)S(1)}, u32[]{:S(2)}, u32[]{:S(2)}) collective-permute-start(bf16[80,512]{1,0:T(8,128)(2,1)S(1)} %get-tuple-element.196), channel_id=1, source_target_pairs={{0,24},{2,26},{4,28},{6,30},{8,16},{10,18},{12,20},{14,22},{16,8},... | collective-permute-start | bytes 245768 | tf_op jit(solution)/shard_map/ppermute | solution.py:1005
  142.8 6.2 %collective-permute-done.28.refs_3_ = bf16[80,512]{1,0:T(8,128)(2,1)S(1)} collective-permute-done((bf16[80,512]{1,0:T(8,128)(2,1)S(1)}, bf16[80,512]{1,0:T(8,128)(2,1)S(1)}, u32[]{:S(2)}, u32[]{:S(2)}) %collective-permute-start.28) | collective-permute-done | bytes 81952 | tf_op jit(solution)/shard_map/ppermute | solution.py:1005
  151.7 5.1 %collective-permute-done.35.refs_2_ = bf16[256,512]{1,0:T(8,128)(2,1)S(1)} collective-permute-done((bf16[256,512]{1,0:T(8,128)(2,1)S(1)}, bf16[256,512]{1,0:T(8,128)(2,1)S(1)}, u32[]{:S(2)}, u32[]{:S(2)}) %collective-permute-start.35) | collective-permute-done | bytes 262176 | tf_op jit(solution)/shard_map/ppermute | solution.py:1296
  165.1 2.4 %collective-permute-done.32.refs_3_ = bf16[64,512]{1,0:T(8,128)(2,1)S(1)} collective-permute-done((bf16[64,512]{1,0:T(8,128)(2,1)S(1)}, bf16[64,512]{1,0:T(8,128)(2,1)S(1)}, u32[]{:S(2)}, u32[]{:S(2)}) %collective-permute-start.32) | collective-permute-done | bytes 65568 | tf_op jit(solution)/shard_map/ppermute | solution.py:1005
  170.9 2.3 %collective-permute-start.38 = (bf16[256,512]{1,0:T(8,128)(2,1)S(1)}, bf16[256,512]{1,0:T(8,128)(2,1)S(1)}, u32[]{:S(2)}, u32[]{:S(2)}) collective-permute-start(bf16[256,512]{1,0:T(8,128)(2,1)S(1)} %get-tuple-element.207.refs_1_), channel_id=1, source_target_pairs={{0,6},{2,4},{4,2},{6,0},{8,14},{10,12},{12,10},{14,8},{16,22},{18,... | collective-permute-start | bytes 786440 | tf_op jit(solution)/shard_map/ppermute | solution.py:1005
  175.1 4.2 %shard_map.359 = (f32[1024,512]{1,0:T(8,128)}, f32[512,1024]{1,0:T(8,128)}, f32[8,128]{1,0:T(8,128)}) custom-call(s32[6]{0:T(128)} %stack.27.refs_0_, bf16[512,512]{1,0:T(8,128)(2,1)} %copy-done.2, bf16[512,512]{1,0:T(8,128)(2,1)} %copy-done, bf16[512,512]{1,0:T(8,128)(2,1)} %copy-done.1, f32[8,128]{1,0:T(8,128)} %copy-done.17), custom_call_target="tpu_custom_call" | custom-call | flops 1000000 | bytes 5767168 | tf_op jit(solution)/shard_map/pallas_call | solution.py:1057
  179.3 2.2 %collective-permute-done.37.refs_3_ = bf16[256,512]{1,0:T(8,128)(2,1)S(1)} collective-permute-done((bf16[256,512]{1,0:T(8,128)(2,1)S(1)}, bf16[256,512]{1,0:T(8,128)(2,1)S(1)}, u32[]{:S(2)}, u32[]{:S(2)}) %collective-permute-start.37) | collective-permute-done | bytes 262176 | tf_op jit(solution)/shard_map/ppermute | solution.py:1005
  181.5 1.8 collective-permute-done.38.refs_4_
  184.0 3.3 %shard_map.360 = (f32[512,256]{1,0:T(8,128)}, f32[512,256]{1,0:T(8,128)}, f32[512,256]{1,0:T(8,128)}, f32[256,512]{1,0:T(8,128)}, f32[1,512]{1,0:T(1,128)}, /*in...) custom-call(s32[6]{0:T(128)} %stack.27.refs_0_, ...), custom_call_target="tpu_custom_call" | custom-call | flops 1000000 | bytes 3206148 | tf_op jit(solution)/shard_map/pallas_call | solution.py:1057
  188.1 2.7 %shard_map.361 = (f32[1024,512]{1,0:T(8,128)}, f32[512,1024]{1,0:T(8,128)}, f32[8,128]{1,0:T(8,128)}) custom-call(s32[6]{0:T(128)} %stack.27.refs_0_, bf16[256,512]{1,0:T(8,128)(2,1)} %copy-done.26, bf16[256,512]{1,0:T(8,128)(2,1)} %copy-done.27, f32[1024,512]{1,0:T(8,128)} %get-tuple-element.228.refs_3_, ...), custom_call_target="tpu_custom_call", output_to_operand_aliasing={{0}: (3, {}), {1}: (4, {})} | custom-call | flops 1000000 | bytes 8912896 | tf_op jit(solution)/shard_map/pallas_call | solution.py:1057
  (193 shorter events, 48.6 us)
Async XLA Ops:
  2.5 15.4 %collective-permute-start.3 = (bf16[512,256]{1,0:T(8,128)(2,1)}, bf16[512,256]{1,0:T(8,128)(2,1)S(1)}, u32[]{:S(2)}, u32[]{:S(2)}) collective-permute-start(bf16[512,256]{1,0:T(8,128)(2,1)} %refs_10_.1), channel_id=1, source_target_pairs={{0,1},{1,0},{2,3},{3,2},{4,5},{5,4},{6,7},{7,6},{8,9},{9,8},{10,11... | collective-permute-start | bytes 786440 | tf_op jit(solution)/shard_map/ppermute | solution.py:992
  2.6 39.6 %collective-permute-start.5 = (bf16[512,1024]{1,0:T(8,128)(2,1)}, bf16[512,1024]{1,0:T(8,128)(2,1)S(1)}, u32[]{:S(2)}, u32[]{:S(2)}) collective-permute-start(bf16[512,1024]{1,0:T(8,128)(2,1)} %refs_13_.1), channel_id=1, source_target_pairs={{0,1},{1,0},{2,3},{3,2},{4,5},{5,4},{6,7},{7,6},{8,9},{9,8},{10,11... | collective-permute-start | bytes 3145736 | tf_op jit(solution)/shard_map/ppermute | solution.py:992
  3.6 38.5 %collective-permute-start.6 = (bf16[1024,512]{1,0:T(8,128)(2,1)}, bf16[1024,512]{1,0:T(8,128)(2,1)S(1)}, u32[]{:S(2)}, u32[]{:S(2)}) collective-permute-start(bf16[1024,512]{1,0:T(8,128)(2,1)} %refs_17_.1), channel_id=1, source_target_pairs={{0,1},{1,0},{2,3},{3,2},{4,5},{5,4},{6,7},{7,6},{8,9},{9,8},{10,11... | collective-permute-start | bytes 3145736 | tf_op jit(solution)/shard_map/ppermute | solution.py:992
  9.6 17.2 %all-to-all-start = ((bf16[16,48,128]{2,1,0:T(8,128)(2,1)}), bf16[16,48,128]{2,1,0:T(8,128)(2,1)S(1)}, u32[]{:S(2)}, u32[]{:S(2)}) async-start(bf16[16,48,128]{2,1,0:T(8,128)(2,1)} %get-tuple-element.127), calls=%async_computation | async-start | bytes 393216 | tf_op jit(solution)/shard_map/all_to_all | solution.py:996
  29.2 13.0 %all-to-all-start.1 = ((bf16[16,48,128]{2,1,0:T(8,128)(2,1)}), bf16[16,48,128]{2,1,0:T(8,128)(2,1)S(1)}, u32[]{:S(2)}, u32[]{:S(2)}) async-start(bf16[16,48,128]{2,1,0:T(8,128)(2,1)} %get-tuple-element.134), calls=%async_computation.1 | async-start | bytes 393216 | tf_op jit(solution)/shard_map/all_to_all | solution.py:996
  62.4 35.1 %collective-permute-start.16 = (bf16[512,512]{1,0:T(8,128)(2,1)S(1)}, bf16[512,512]{1,0:T(8,128)(2,1)S(1)}, u32[]{:S(2)}, u32[]{:S(2)}) collective-permute-start(bf16[512,512]{1,0:T(8,128)(2,1)S(1)} %copy-done.40), channel_id=1, source_target_pairs={{0,1},{1,0},{2,3},{3,2},{4,5},{5,4},{6,7},{7,6},{8,9},{9,8},{10,11... | collective-permute-start | bytes 1572872 | tf_op jit(solution)/shard_map/ppermute | solution.py:992
  62.8 13.7 %all-to-all-start.2 = ((bf16[16,48,128]{2,1,0:T(8,128)(2,1)}), bf16[16,48,128]{2,1,0:T(8,128)(2,1)S(1)}, u32[]{:S(2)}, u32[]{:S(2)}) async-start(bf16[16,48,128]{2,1,0:T(8,128)(2,1)} %get-tuple-element.140), calls=%async_computation.2 | async-start | bytes 393216 | tf_op jit(solution)/shard_map/all_to_all | solution.py:996
  66.3 38.8 %collective-permute-start.21 = (bf16[512,512]{1,0:T(8,128)(2,1)}, bf16[512,512]{1,0:T(8,128)(2,1)}, u32[]{:S(2)}, u32[]{:S(2)}) collective-permute-start(bf16[512,512]{1,0:T(8,128)(2,1)} %get-tuple-element.158.refs_18_.refs_11_), channel_id=1, source_target_pairs={{0,1},{1,0},{2,3},{3,2},{4,5},{5,4},{6,7},{7,6},{8,9},{9,8},{10,11... | collective-permute-start | bytes 1572872 | tf_op jit(solution)/shard_map/ppermute | solution.py:992
  67.0 37.6 %collective-permute-start.20 = (bf16[512,256]{1,0:T(8,128)(2,1)}, bf16[512,256]{1,0:T(8,128)(2,1)}, u32[]{:S(2)}, u32[]{:S(2)}) collective-permute-start(bf16[512,256]{1,0:T(8,128)(2,1)} %get-tuple-element.177), channel_id=1, source_target_pairs={{0,1},{1,0},{2,3},{3,2},{4,5},{5,4},{6,7},{7,6},{8,9},{9,8},{10,11... | collective-permute-start | bytes 786440 | tf_op jit(solution)/shard_map/ppermute | solution.py:992
  79.5 18.0 %all-to-all-start.3 = ((bf16[16,48,128]{2,1,0:T(8,128)(2,1)}), bf16[16,48,128]{2,1,0:T(8,128)(2,1)S(1)}, u32[]{:S(2)}, u32[]{:S(2)}) async-start(bf16[16,48,128]{2,1,0:T(8,128)(2,1)} %get-tuple-element.147), calls=%async_computation.3 | async-start | bytes 393216 | tf_op jit(solution)/shard_map/all_to_all | solution.py:996
  86.0 19.3 %collective-permute-start.12 = (bf16[512,512]{1,0:T(8,128)(2,1)}, bf16[512,512]{1,0:T(8,128)(2,1)S(1)}, u32[]{:S(2)}, u32[]{:S(2)}) collective-permute-start(bf16[512,512]{1,0:T(8,128)(2,1)} %get-tuple-element.164), channel_id=1, source_target_pairs={{0,2},{2,0},{4,6},{6,4},{8,10},{10,8},{12,14},{14,12},{16,18},{18,... | collective-permute-start | bytes 1572872 | tf_op jit(solution)/shard_map/ppermute | solution.py:1005
  88.0 17.7 %collective-permute-start.13 = (bf16[512,512]{1,0:T(8,128)(2,1)}, bf16[512,512]{1,0:T(8,128)(2,1)S(1)}, u32[]{:S(2)}, u32[]{:S(2)}) collective-permute-start(bf16[512,512]{1,0:T(8,128)(2,1)} %get-tuple-element.166), channel_id=1, source_target_pairs={{0,4},{2,6},{4,0},{6,2},{8,12},{10,14},{12,8},{14,10},{16,20},{18,... | collective-permute-start | bytes 1572872 | tf_op jit(solution)/shard_map/ppermute | solution.py:1005
  97.5 9.2 %collective-permute-start.17 = (bf16[512,256]{1,0:T(8,128)(2,1)}, bf16[512,256]{1,0:T(8,128)(2,1)S(1)}, u32[]{:S(2)}, u32[]{:S(2)}) collective-permute-start(bf16[512,256]{1,0:T(8,128)(2,1)} %get-tuple-element.157.refs_9_), channel_id=1, source_target_pairs={{0,1},{1,0},{2,3},{3,2},{4,5},{5,4},{6,7},{7,6},{8,9},{9,8},{10,11... | collective-permute-start | bytes 786440 | tf_op jit(solution)/shard_map/ppermute | solution.py:992
  105.3 15.9 %collective-permute-start.7 = (bf16[512,512]{1,0:T(8,128)(2,1)S(1)}, bf16[512,512]{1,0:T(8,128)(2,1)S(1)}, u32[]{:S(2)}, u32[]{:S(2)}) collective-permute-start(bf16[512,512]{1,0:T(8,128)(2,1)S(1)} %copy-done.22), channel_id=1, source_target_pairs={{0,1},{1,0},{2,3},{3,2},{4,5},{5,4},{6,7},{7,6},{8,9},{9,8},{10,11... | collective-permute-start | bytes 1572872 | tf_op jit(solution)/shard_map/ppermute | solution.py:992
  106.7 8.6 %collective-permute-start.14 = (bf16[256,512]{1,0:T(8,128)(2,1)S(1)}, bf16[256,512]{1,0:T(8,128)(2,1)S(1)}, u32[]{:S(2)}, u32[]{:S(2)}) collective-permute-start(bf16[256,512]{1,0:T(8,128)(2,1)S(1)} %get-tuple-element.169), channel_id=1, source_target_pairs={{0,4},{2,6},{4,0},{6,2},{8,12},{10,14},{12,8},{14,10},{16,20},{18,... | collective-permute-start | bytes 786440 | tf_op jit(solution)/shard_map/ppermute | solution.py:1005
  107.7 8.3 %collective-permute-start.15 = (bf16[256,512]{1,0:T(8,128)(2,1)S(1)}, bf16[256,512]{1,0:T(8,128)(2,1)S(1)}, u32[]{:S(2)}, u32[]{:S(2)}) collective-permute-start(bf16[256,512]{1,0:T(8,128)(2,1)S(1)} %get-tuple-element.171), channel_id=1, source_target_pairs={{0,2},{2,0},{4,6},{6,4},{8,10},{10,8},{12,14},{14,12},{16,18},{18,... | collective-permute-start | bytes 786440 | tf_op jit(solution)/shard_map/ppermute | solution.py:1005
  108.2 14.7 %collective-permute-start.11 = (bf16[512,512]{1,0:T(8,128)(2,1)S(1)}, bf16[512,512]{1,0:T(8,128)(2,1)S(1)}, u32[]{:S(2)}, u32[]{:S(2)}) collective-permute-start(bf16[512,512]{1,0:T(8,128)(2,1)S(1)} %copy-done.23), channel_id=1, source_target_pairs={{0,1},{1,0},{2,3},{3,2},{4,5},{5,4},{6,7},{7,6},{8,9},{9,8},{10,11... | collective-permute-start | bytes 1572872 | tf_op jit(solution)/shard_map/ppermute | solution.py:992
  118.0 9.9 %collective-permute-start.26 = (bf16[256,512]{1,0:T(8,128)(2,1)S(1)}, bf16[256,512]{1,0:T(8,128)(2,1)S(1)}, u32[]{:S(2)}, u32[]{:S(2)}) collective-permute-start(bf16[256,512]{1,0:T(8,128)(2,1)S(1)} %get-tuple-element.190), channel_id=1, source_target_pairs={{0,8},{2,10},{4,12},{6,14},{8,0},{10,2},{12,4},{14,6},{16,24},{18,... | collective-permute-start | bytes 786440 | tf_op jit(solution)/shard_map/ppermute | solution.py:1296
  119.5 12.2 %collective-permute-start.23 = (bf16[272,512]{1,0:T(8,128)(2,1)}, bf16[272,512]{1,0:T(8,128)(2,1)S(1)}, u32[]{:S(2)}, u32[]{:S(2)}) collective-permute-start(bf16[272,512]{1,0:T(8,128)(2,1)} %get-tuple-element.186), channel_id=1, source_target_pairs={{0,2},{2,0},{4,6},{6,4},{8,10},{10,8},{12,14},{14,12},{16,18},{18,... | collective-permute-start | bytes 835592 | tf_op jit(solution)/shard_map/ppermute | solution.py:1005
  120.0 13.9 %collective-permute-start.24 = (bf16[272,512]{1,0:T(8,128)(2,1)}, bf16[272,512]{1,0:T(8,128)(2,1)S(1)}, u32[]{:S(2)}, u32[]{:S(2)}) collective-permute-start(bf16[272,512]{1,0:T(8,128)(2,1)} %get-tuple-element.187), channel_id=1, source_target_pairs={{0,4},{2,6},{4,0},{6,2},{8,12},{10,14},{12,8},{14,10},{16,20},{18,... | collective-permute-start | bytes 835592 | tf_op jit(solution)/shard_map/ppermute | solution.py:1005
  121.2 12.8 %collective-permute-start.25 = (bf16[272,512]{1,0:T(8,128)(2,1)}, bf16[272,512]{1,0:T(8,128)(2,1)S(1)}, u32[]{:S(2)}, u32[]{:S(2)}) collective-permute-start(bf16[272,512]{1,0:T(8,128)(2,1)} %get-tuple-element.188), channel_id=1, source_target_pairs={{0,6},{2,4},{4,2},{6,0},{8,14},{10,12},{12,10},{14,8},{16,22},{18,... | collective-permute-start | bytes 835592 | tf_op jit(solution)/shard_map/ppermute | solution.py:1005
  136.6 13.0 %collective-permute-start.34 = (bf16[128,512]{1,0:T(8,128)(2,1)S(1)}, bf16[128,512]{1,0:T(8,128)(2,1)S(1)}, u32[]{:S(2)}, u32[]{:S(2)}) collective-permute-start(bf16[128,512]{1,0:T(8,128)(2,1)S(1)} %get-tuple-element.202.refs_1_), channel_id=1, source_target_pairs={{0,16},{2,18},{4,20},{6,22},{8,24},{10,26},{12,28},{14,30},{16,0},... | collective-permute-start | bytes 393224 | tf_op jit(solution)/shard_map/ppermute | solution.py:1296
  139.6 9.4 %collective-permute-start.28 = (bf16[80,512]{1,0:T(8,128)(2,1)S(1)}, bf16[80,512]{1,0:T(8,128)(2,1)S(1)}, u32[]{:S(2)}, u32[]{:S(2)}) collective-permute-start(bf16[80,512]{1,0:T(8,128)(2,1)S(1)} %get-tuple-element.195), channel_id=1, source_target_pairs={{0,16},{2,18},{4,20},{6,22},{8,24},{10,26},{12,28},{14,30},{16,0},... | collective-permute-start | bytes 245768 | tf_op jit(solution)/shard_map/ppermute | solution.py:1005
  139.7 9.3 %collective-permute-start.29 = (bf16[80,512]{1,0:T(8,128)(2,1)S(1)}, bf16[80,512]{1,0:T(8,128)(2,1)S(1)}, u32[]{:S(2)}, u32[]{:S(2)}) collective-permute-start(bf16[80,512]{1,0:T(8,128)(2,1)S(1)} %get-tuple-element.196), channel_id=1, source_target_pairs={{0,24},{2,26},{4,28},{6,30},{8,16},{10,18},{12,20},{14,22},{16,8},... | collective-permute-start | bytes 245768 | tf_op jit(solution)/shard_map/ppermute | solution.py:1005
  157.4 13.5 %collective-permute-start.40 = (bf16[512,512]{1,0:T(8,128)(2,1)S(1)}, bf16[512,512]{1,0:T(8,128)(2,1)S(1)}, u32[]{:S(2)}, u32[]{:S(2)}) collective-permute-start(bf16[512,512]{1,0:T(8,128)(2,1)S(1)} %get-tuple-element.209.refs_1_), channel_id=1, source_target_pairs={{0,2},{2,0},{4,6},{6,4},{8,10},{10,8},{12,14},{14,12},{16,18},{18,... | collective-permute-start | bytes 1572872 | tf_op jit(solution)/shard_map/ppermute | solution.py:1005
  158.9 14.3 %collective-permute-start.41 = (bf16[512,512]{1,0:T(8,128)(2,1)S(1)}, bf16[512,512]{1,0:T(8,128)(2,1)S(1)}, u32[]{:S(2)}, u32[]{:S(2)}) collective-permute-start(bf16[512,512]{1,0:T(8,128)(2,1)S(1)} %get-tuple-element.209.refs_1_), channel_id=1, source_target_pairs={{0,4},{2,6},{4,0},{6,2},{8,12},{10,14},{12,8},{14,10},{16,20},{18,... | collective-permute-start | bytes 1572872 | tf_op jit(solution)/shard_map/ppermute | solution.py:1005
  165.1 9.0 %collective-permute-start.39 = (f32[8,128]{1,0:T(8,128)S(1)}, f32[8,128]{1,0:T(8,128)S(1)}, u32[]{:S(2)}, u32[]{:S(2)}) collective-permute-start(f32[8,128]{1,0:T(8,128)S(1)} %copy-done.13), channel_id=1, source_target_pairs={{0,1},{1,0},{2,3},{3,2},{4,5},{5,4},{6,7},{7,6},{8,9},{9,8},{10,11... | collective-permute-start | bytes 12296 | tf_op jit(solution)/shard_map/ppermute | solution.py:992
  169.6 9.6 %collective-permute-start.36 = (bf16[256,512]{1,0:T(8,128)(2,1)S(1)}, bf16[256,512]{1,0:T(8,128)(2,1)S(1)}, u32[]{:S(2)}, u32[]{:S(2)}) collective-permute-start(bf16[256,512]{1,0:T(8,128)(2,1)S(1)} %get-tuple-element.207.refs_1_), channel_id=1, source_target_pairs={{0,2},{2,0},{4,6},{6,4},{8,10},{10,8},{12,14},{14,12},{16,18},{18,... | collective-permute-start | bytes 786440 | tf_op jit(solution)/shard_map/ppermute | solution.py:1005
  169.9 11.6 %collective-permute-start.37 = (bf16[256,512]{1,0:T(8,128)(2,1)S(1)}, bf16[256,512]{1,0:T(8,128)(2,1)S(1)}, u32[]{:S(2)}, u32[]{:S(2)}) collective-permute-start(bf16[256,512]{1,0:T(8,128)(2,1)S(1)} %get-tuple-element.207.refs_1_), channel_id=1, source_target_pairs={{0,4},{2,6},{4,0},{6,2},{8,12},{10,14},{12,8},{14,10},{16,20},{18,... | collective-permute-start | bytes 786440 | tf_op jit(solution)/shard_map/ppermute | solution.py:1005
  170.9 12.4 %collective-permute-start.38 = (bf16[256,512]{1,0:T(8,128)(2,1)S(1)}, bf16[256,512]{1,0:T(8,128)(2,1)S(1)}, u32[]{:S(2)}, u32[]{:S(2)}) collective-permute-start(bf16[256,512]{1,0:T(8,128)(2,1)S(1)} %get-tuple-element.207.refs_1_), channel_id=1, source_target_pairs={{0,6},{2,4},{4,2},{6,0},{8,14},{10,12},{12,10},{14,8},{16,22},{18,... | collective-permute-start | bytes 786440 | tf_op jit(solution)/shard_map/ppermute | solution.py:1005
  173.9 13.4 %collective-permute-start.42 = (bf16[256,512]{1,0:T(8,128)(2,1)S(1)}, bf16[256,512]{1,0:T(8,128)(2,1)S(1)}, u32[]{:S(2)}, u32[]{:S(2)}) collective-permute-start(bf16[256,512]{1,0:T(8,128)(2,1)S(1)} %get-tuple-element.226), channel_id=1, source_target_pairs={{0,2},{2,0},{4,6},{6,4},{8,10},{10,8},{12,14},{14,12},{16,18},{18,... | collective-permute-start | bytes 786440 | tf_op jit(solution)/shard_map/ppermute | solution.py:1005
  174.1 13.2 %collective-permute-start.43 = (bf16[256,512]{1,0:T(8,128)(2,1)S(1)}, bf16[256,512]{1,0:T(8,128)(2,1)S(1)}, u32[]{:S(2)}, u32[]{:S(2)}) collective-permute-start(bf16[256,512]{1,0:T(8,128)(2,1)S(1)} %get-tuple-element.227), channel_id=1, source_target_pairs={{0,4},{2,6},{4,0},{6,2},{8,12},{10,14},{12,8},{14,10},{16,20},{18,... | collective-permute-start | bytes 786440 | tf_op jit(solution)/shard_map/ppermute | solution.py:1005
  (67 other events, 331.4 us)

commit v3 on v2

--- a/solution.py
+++ b/solution.py
@@ -22,8 +22,8 @@
     "p2",
     "P",
     "h1",
+    "h2",
     "s1",
-    "h2",
     "s2",
     "d1",
     "d2",
@@ -1187,7 +1187,7 @@
         scratch=[pltpu.VMEM((2, t, a), wide)],
         mark=True,
     )
-    entering, _ = scan(arriving, False, mark)
+    entering, _ = scan(arriving, False, None)
     entering = over_blocks(entering)
     steps = hidden // width
     up_block = pl.BlockSpec((width, width), lambda i, m: (0, i))
@@ -1443,6 +1443,8 @@
             2e9,
             mine,
             scratch=[pltpu.VMEM((height, width), low)],
+            held=range(1, 14, 2),
+            limit=30,
             after=after,
             mark=True,
         )
@@ -1525,6 +1527,8 @@
             mine,
             out_specs={0: placed, 1: placed},
             grid=(2,),
+            held=(1, 3),
+            limit=30,
             after=after,
             mark=True,
         )
@@ -1546,6 +1550,8 @@
             mine,
             out_specs=dict(enumerate(piece_blocks(0))),
             grid=(3,),
+            held=(0, 1, 2),
+            limit=24,
             after=after,
             mark=True,
         )
@@ -1561,6 +1567,8 @@
             mine,
             specs={2: PLACED, 3: PLACED},
             out_specs=dict(enumerate(piece_blocks(3))),
+            held=(0, 1),
+            limit=16,
             after=after,
             mark=True,
             aliases={3: 0, 4: 1},
@@ -1583,6 +1591,8 @@
             1e6,
             mine,
             scratch=[pltpu.VMEM((height, width), low)],
+            held=range(radix),
+            limit=24,
             after=after,
             mark=True,
         )

time: 192 us -> 184 us (0.958)
  Pallas kernels: 79.1 us -> 70.1 us
  local copies, waits for them, and re-layouts: 14 us -> 8.32 us
  starting transfers between devices: 58.3 us -> 62.2 us
  waiting for transfers between devices: 37.4 us -> 41 us
    pallas_call x23, Pallas kernels: 79.1 us -> 70.1 us  [call(): pl.pallas_call(body, grid_spec=pltpu.PrefetchScalarGridSpec(num_scalar_pr...]
    unnamed x102 -> x58, local copies, waits for them, and re-layouts: 12.8 us -> 6.43 us
    ppermute x4, waiting for transfers between devices: 7.01 us -> 10.5 us  [far(): return lax.ppermute(value, 'seq', [(i, i ^ bit) for i in range(blocks)])]
    ppermute x20, starting transfers between devices: 24.4 us -> 27.2 us  [exchange(): return lax.ppermute(value, 'seq', [(i, i ^ other) for i in range(count)])]
  transfers between devices with their start and end apart: 48 -> 48, of which waited for: 18 -> 19; matrix products, arithmetic and copies ran while one was open for 1% -> 1% of each run, Pallas kernels for 30% -> 27%
where the time goes in v3:
time: 184 us
  Pallas kernels  70.1 us (38%)
  starting transfers between devices  62.2 us (34%)
  waiting for transfers between devices  41 us (22%)
  local copies, waits for them, and re-layouts  8.32 us (5%)
    pallas_call x23, Pallas kernels, call(): pl.pallas_call(body, grid_spec=pltpu.PrefetchScalarGridSpec(num_scalar_pr...  70.1 us
    ppermute x20, starting transfers between devices, exchange(): return lax.ppermute(value, 'seq', [(i, i ^ other) for i in range(count)])  27.2 us
    all_to_all x4, starting transfers between devices, over_blocks(): return lax.all_to_all(value, 'seq', 0, 0)  23.7 us
    ppermute x20, waiting for transfers between devices, exchange(): return lax.ppermute(value, 'seq', [(i, i ^ other) for i in range(count)])  21.3 us
    ppermute x4, waiting for transfers between devices, far(): return lax.ppermute(value, 'seq', [(i, i ^ bit) for i in range(blocks)])  10.5 us
    all_to_all x4, waiting for transfers between devices, over_blocks(): return lax.all_to_all(value, 'seq', 0, 0)  8.85 us
    unnamed x58, local copies, waits for them, and re-layouts  6.43 us
    ppermute x4, starting transfers between devices, far(): return lax.ppermute(value, 'seq', [(i, i ^ bit) for i in range(blocks)])  6.37 us
  transfers between devices with their start and end apart: 48, of which 19 were waited for; matrix products, arithmetic and copies ran while one was open for 1% of the time, Pallas kernels for 27%

profile of v3, /device:TPU:0, one launch (start us, length us, event | category | flops | bytes accessed | tf_op | source)
XLA Modules:
  0.0 183.6 jit_solution(5419583561346206416)
XLA Ops:
  4.4 5.2 %shard_map.339 = (bf16[512,512]{1,0:T(8,128)(2,1)}, bf16[512,512]{1,0:T(8,128)(2,1)}, bf16[512,512]{1,0:T(8,128)(2,1)}, bf16[512,512]{1,0:T(8,128)(2,1)}, f32[51...) custom-call(s32[6]{0:T(128)} %stack.27.refs_0_, ...), custom_call_target="tpu_custom_call" | custom-call | flops 4000000000 | bytes 4695040 | tf_op jit(solution)/shard_map/pallas_call | solution.py:1057
  9.7 7.9 %all-to-all-start = ((bf16[16,48,128]{2,1,0:T(8,128)(2,1)}), bf16[16,48,128]{2,1,0:T(8,128)(2,1)S(1)}, u32[]{:S(2)}, u32[]{:S(2)}) async-start(bf16[16,48,128]{2,1,0:T(8,128)(2,1)} %get-tuple-element.126), calls=%async_computation | async-start | bytes 393216 | tf_op jit(solution)/shard_map/all_to_all | solution.py:996
  19.5 7.1 %all-to-all-done.refs_1_ = bf16[16,48,128]{2,1,0:T(8,128)(2,1)S(1)} async-done(((bf16[16,48,128]{2,1,0:T(8,128)(2,1)}), bf16[16,48,128]{2,1,0:T(8,128)(2,1)S(1)}, u32[]{:S(2)}, u32[]{:S(2)}) %all-to-all-start) | async-done | bytes 196640 | tf_op jit(solution)/shard_map/all_to_all | solution.py:996
  26.5 1.7 shard_map.340
  28.2 3.7 %all-to-all-start.1 = ((bf16[16,48,128]{2,1,0:T(8,128)(2,1)}), bf16[16,48,128]{2,1,0:T(8,128)(2,1)S(1)}, u32[]{:S(2)}, u32[]{:S(2)}) async-start(bf16[16,48,128]{2,1,0:T(8,128)(2,1)} %get-tuple-element.127), calls=%async_computation.1 | async-start | bytes 393216 | tf_op jit(solution)/shard_map/all_to_all | solution.py:996
  32.7 6.0 %shard_map.341 = (bf16[512,512]{1,0:T(8,128)(2,1)}, bf16[512,512]{1,0:T(8,128)(2,1)}, bf16[16,256,256]{2,1,0:T(8,128)(2,1)}, f32[512,512]{1,0:T(8,128)}, f32[512,128]{1,0:T(8,128)}, /*index=5*/f32[8,128]{1,0:T(8,128)}) custom-call(bf16[512,512]{1,0:T(8,128)(2,1)} %get-tuple-element.128.refs_0_.refs_1_, bf16[512,256]{1,0:T(8,128)(2,1)} %refs_10_.1, ...), custom_call_target="tpu_custom_call" | custom-call | flops 4000000000 | bytes 6840320 | tf_op jit(solution)/shard_map/pallas_call | solution.py:1057
  38.7 1.6 all-to-all-done.1.refs_1_.refs_0_
  41.4 18.1 %shard_map.342 = (bf16[512,512]{1,0:T(8,128)(2,1)}, bf16[512,1024]{1,0:T(8,128)(2,1)}, bf16[512,1024]{1,0:T(8,128)(2,1)}, bf16[512,1024]{1,0:T(8,128)(2,1)}, bf1...) custom-call(s32[6]{0:T(128)} %stack.27.refs_0_, ...), custom_call_target="tpu_custom_call" | custom-call | flops 12000000000 | bytes 16961536 | tf_op jit(solution)/shard_map/pallas_call | solution.py:1057
  60.7 5.3 %all-to-all-start.2 = ((bf16[16,48,128]{2,1,0:T(8,128)(2,1)}), bf16[16,48,128]{2,1,0:T(8,128)(2,1)S(1)}, u32[]{:S(2)}, u32[]{:S(2)}) async-start(bf16[16,48,128]{2,1,0:T(8,128)(2,1)} %get-tuple-element.138), calls=%async_computation.2 | async-start | bytes 393216 | tf_op jit(solution)/shard_map/all_to_all | solution.py:996
  66.8 7.9 %shard_map.343 = (bf16[512,512]{1,0:T(8,128)(2,1)}, bf16[512,512]{1,0:T(8,128)(2,1)}, bf16[512,512]{1,0:T(8,128)(2,1)}, bf16[512,512]{1,0:T(8,128)(2,1)}, f32[8,128]{1,0:T(8,128)}) custom-call(s32[6]{0:T(128)} %stack.27.refs_0_, bf16[512,1024]{1,0:T(8,128)(2,1)} %get-tuple-element.139.refs_1_, bf16[512,1024]{1,0:T(8,128)(2,1)} %collective-permute-done.8.refs_2_, ...), custom_call_target="tpu_custom_call" | custom-call | flops 4000000000 | bytes 9437184 | tf_op jit(solution)/shard_map/pallas_call | solution.py:1057
  75.5 1.7 shard_map.344
  77.8 6.7 %all-to-all-start.3 = ((bf16[16,48,128]{2,1,0:T(8,128)(2,1)}), bf16[16,48,128]{2,1,0:T(8,128)(2,1)S(1)}, u32[]{:S(2)}, u32[]{:S(2)}) async-start(bf16[16,48,128]{2,1,0:T(8,128)(2,1)} %get-tuple-element.145), calls=%async_computation.3 | async-start | bytes 393216 | tf_op jit(solution)/shard_map/all_to_all | solution.py:996
  84.5 2.0 %collective-permute-start.12 = (bf16[512,512]{1,0:T(8,128)(2,1)}, bf16[512,512]{1,0:T(8,128)(2,1)S(1)}, u32[]{:S(2)}, u32[]{:S(2)}) collective-permute-start(bf16[512,512]{1,0:T(8,128)(2,1)} %get-tuple-element.162), channel_id=1, source_target_pairs={{0,2},{2,0},{4,6},{6,4},{8,10},{10,8},{12,14},{14,12},{16,18},{18,... | collective-permute-start | bytes 1572872 | tf_op jit(solution)/shard_map/ppermute | solution.py:1005
  88.0 8.0 %shard_map.345 = (bf16[512,256]{1,0:T(8,128)(2,1)}, bf16[512,256]{1,0:T(8,128)(2,1)}, bf16[512,512]{1,0:T(8,128)(2,1)}, bf16[512,512]{1,0:T(8,128)(2,1)}, f32[8,512]{1,0:T(8,128)}, /*index=5*/f32[8,128]{1,0:T(8,128)}) custom-call(bf16[16,48,128]{2,1,0:T(8,128)(2,1)} %copy-done.18, bf16[16,256,256]{2,1,0:T(8,128)(2,1)} %get-tuple-element.147.refs_1_, ...), custom_call_target="tpu_custom_call" | custom-call | flops 6000000000 | bytes 7569408 | tf_op jit(solution)/shard_map/pallas_call | solution.py:1057
  96.8 6.3 %shard_map.346 = (bf16[512,256]{1,0:T(8,128)(2,1)}, bf16[512,256]{1,0:T(8,128)(2,1)}, bf16[512,256]{1,0:T(8,128)(2,1)}, bf16[512,256]{1,0:T(8,128)(2,1)}, bf16[5...) custom-call(s32[6]{0:T(128)} %stack.27.refs_0_, ...), custom_call_target="tpu_custom_call" | custom-call | flops 4000000000 | bytes 8439808 | tf_op jit(solution)/shard_map/pallas_call | solution.py:1057
  107.9 1.9 %shard_map.348 = (bf16[272,512]{1,0:T(8,128)(2,1)S(1)}, bf16[272,512]{1,0:T(8,128)(2,1)S(1)}, bf16[272,512]{1,0:T(8,128)(2,1)S(1)}, bf16[272,512]{1,0:T(8,128)(2,1)S(1)}, f32[8,128]{1,0:T(8,128)S(1)}) custom-call(s32[6]{0:T(128)S(1)} %copy-done.6, bf16[512,512]{1,0:T(8,128)(2,1)S(1)} %copy-done.10, bf16[512,512]{1,0:T(8,128)(2,1)S(1)} %collective-permute-done.16.refs_2_, ...), custom_call_target="tpu_custom_call" | custom-call | flops 2000000000 | bytes 5373952 | tf_op jit(solution)/shard_map/pallas_call | solution.py:1057
  109.8 4.2 %collective-permute-done.14.refs_2_ = bf16[256,512]{1,0:T(8,128)(2,1)S(1)} collective-permute-done((bf16[256,512]{1,0:T(8,128)(2,1)S(1)}, bf16[256,512]{1,0:T(8,128)(2,1)S(1)}, u32[]{:S(2)}, u32[]{:S(2)}) %collective-permute-start.14) | collective-permute-done | bytes 262176 | tf_op jit(solution)/shard_map/ppermute | solution.py:1005
  118.6 1.8 collective-permute-start.25
  120.4 2.4 %shard_map.350 = (bf16[4,256,512]{2,1,0:T(8,128)(2,1)}, f32[4,256,512]{2,1,0:T(8,128)}, f32[8,128]{1,0:T(8,128)S(1)}) custom-call(s32[6]{0:T(128)S(1)} %copy-done.6, bf16[512,512]{1,0:T(8,128)(2,1)S(1)} %copy-done, bf16[512,512]{1,0:T(8,128)(2,1)S(1)} %collective-permute-done.7.refs_2_, bf16[512,512]{1,0:T(8,128)(2,1)S(1)} %copy-done.1, ...), custom_call_target="tpu_custom_call" | custom-call | flops 1000000 | bytes 5242880 | tf_op jit(solution)/shard_map/pallas_call | solution.py:1057
  123.6 2.4 %collective-permute-start.27 = (bf16[128,512]{1,0:T(8,128)(2,1)S(1)}, bf16[128,512]{1,0:T(8,128)(2,1)S(1)}, u32[]{:S(2)}, u32[]{:S(2)}) collective-permute-start(bf16[128,512]{1,0:T(8,128)(2,1)S(1)} %get-tuple-element.191), channel_id=1, source_target_pairs={{0,16},{2,18},{4,20},{6,22},{8,24},{10,26},{12,28},{14,30},{16,0},... | collective-permute-start | bytes 393224 | tf_op jit(solution)/shard_map/ppermute | solution.py:1296
  126.0 5.1 %collective-permute-done.27.refs_1_ = bf16[128,512]{1,0:T(8,128)(2,1)S(1)} collective-permute-done((bf16[128,512]{1,0:T(8,128)(2,1)S(1)}, bf16[128,512]{1,0:T(8,128)(2,1)S(1)}, u32[]{:S(2)}, u32[]{:S(2)}) %collective-permute-start.27) | collective-permute-done | bytes 131104 | tf_op jit(solution)/shard_map/ppermute | solution.py:1296
  132.8 4.5 %collective-permute-start.28 = (bf16[80,512]{1,0:T(8,128)(2,1)S(1)}, bf16[80,512]{1,0:T(8,128)(2,1)S(1)}, u32[]{:S(2)}, u32[]{:S(2)}) collective-permute-start(bf16[80,512]{1,0:T(8,128)(2,1)S(1)} %get-tuple-element.195), channel_id=1, source_target_pairs={{0,8},{2,10},{4,12},{6,14},{8,0},{10,2},{12,4},{14,6},{16,24},{18,... | collective-permute-start | bytes 245768 | tf_op jit(solution)/shard_map/ppermute | solution.py:1005
  137.3 2.4 %collective-permute-start.30 = (bf16[80,512]{1,0:T(8,128)(2,1)S(1)}, bf16[80,512]{1,0:T(8,128)(2,1)S(1)}, u32[]{:S(2)}, u32[]{:S(2)}) collective-permute-start(bf16[80,512]{1,0:T(8,128)(2,1)S(1)} %get-tuple-element.197), channel_id=1, source_target_pairs={{0,24},{2,26},{4,28},{6,30},{8,16},{10,18},{12,20},{14,22},{16,8},... | collective-permute-start | bytes 245768 | tf_op jit(solution)/shard_map/ppermute | solution.py:1005
  140.0 4.9 %collective-permute-done.29.refs_3_ = bf16[80,512]{1,0:T(8,128)(2,1)S(1)} collective-permute-done((bf16[80,512]{1,0:T(8,128)(2,1)S(1)}, bf16[80,512]{1,0:T(8,128)(2,1)S(1)}, u32[]{:S(2)}, u32[]{:S(2)}) %collective-permute-start.29) | collective-permute-done | bytes 81952 | tf_op jit(solution)/shard_map/ppermute | solution.py:1005
  147.7 5.2 %collective-permute-done.35.refs_2_ = bf16[256,512]{1,0:T(8,128)(2,1)S(1)} collective-permute-done((bf16[256,512]{1,0:T(8,128)(2,1)S(1)}, bf16[256,512]{1,0:T(8,128)(2,1)S(1)}, u32[]{:S(2)}, u32[]{:S(2)}) %collective-permute-start.35) | collective-permute-done | bytes 262176 | tf_op jit(solution)/shard_map/ppermute | solution.py:1296
  155.3 1.7 collective-permute-start.31
  157.9 1.8 collective-permute-start.33
  160.0 2.6 %collective-permute-done.32.refs_3_ = bf16[64,512]{1,0:T(8,128)(2,1)S(1)} collective-permute-done((bf16[64,512]{1,0:T(8,128)(2,1)S(1)}, bf16[64,512]{1,0:T(8,128)(2,1)S(1)}, u32[]{:S(2)}, u32[]{:S(2)}) %collective-permute-start.32) | collective-permute-done | bytes 65568 | tf_op jit(solution)/shard_map/ppermute | solution.py:1005
  170.6 2.7 %shard_map.359 = (f32[1024,512]{1,0:T(8,128)}, f32[512,1024]{1,0:T(8,128)}, f32[8,128]{1,0:T(8,128)S(1)}) custom-call(s32[6]{0:T(128)S(1)} %copy-done.6, bf16[512,512]{1,0:T(8,128)(2,1)S(1)} %get-tuple-element.207.refs_1_, bf16[512,512]{1,0:T(8,128)(2,1)S(1)} %collective-permute-done.40.refs_1_.refs_2_, ...), custom_call_target="tpu_custom_call" | custom-call | flops 1000000 | bytes 5767168 | tf_op jit(solution)/shard_map/pallas_call | solution.py:1057
  173.9 4.7 %collective-permute-done.37.refs_3_ = bf16[256,512]{1,0:T(8,128)(2,1)S(1)} collective-permute-done((bf16[256,512]{1,0:T(8,128)(2,1)S(1)}, bf16[256,512]{1,0:T(8,128)(2,1)S(1)}, u32[]{:S(2)}, u32[]{:S(2)}) %collective-permute-start.37) | collective-permute-done | bytes 262176 | tf_op jit(solution)/shard_map/ppermute | solution.py:1005
  179.6 2.0 %shard_map.360 = (f32[512,256]{1,0:T(8,128)}, f32[512,256]{1,0:T(8,128)}, f32[512,256]{1,0:T(8,128)}, f32[256,512]{1,0:T(8,128)}, f32[1,512]{1,0:T(1,128)}, /*in...) custom-call(s32[6]{0:T(128)S(1)} %copy-done.6, ...), custom_call_target="tpu_custom_call" | custom-call | flops 1000000 | bytes 3206148 | tf_op jit(solution)/shard_map/pallas_call | solution.py:1057
  182.0 1.6 shard_map.361
  (149 shorter events, 41.1 us)
Async XLA Ops:
  2.5 37.9 %collective-permute-start.5 = (bf16[512,1024]{1,0:T(8,128)(2,1)}, bf16[512,1024]{1,0:T(8,128)(2,1)S(1)}, u32[]{:S(2)}, u32[]{:S(2)}) collective-permute-start(bf16[512,1024]{1,0:T(8,128)(2,1)} %refs_13_.1), channel_id=1, source_target_pairs={{0,1},{1,0},{2,3},{3,2},{4,5},{5,4},{6,7},{7,6},{8,9},{9,8},{10,11... | collective-permute-start | bytes 3145736 | tf_op jit(solution)/shard_map/ppermute | solution.py:992
  2.6 37.8 %collective-permute-start.6 = (bf16[1024,512]{1,0:T(8,128)(2,1)}, bf16[1024,512]{1,0:T(8,128)(2,1)}, u32[]{:S(2)}, u32[]{:S(2)}) collective-permute-start(bf16[1024,512]{1,0:T(8,128)(2,1)} %refs_17_.1), channel_id=1, source_target_pairs={{0,1},{1,0},{2,3},{3,2},{4,5},{5,4},{6,7},{7,6},{8,9},{9,8},{10,11... | collective-permute-start | bytes 3145736 | tf_op jit(solution)/shard_map/ppermute | solution.py:992
  9.7 16.9 %all-to-all-start = ((bf16[16,48,128]{2,1,0:T(8,128)(2,1)}), bf16[16,48,128]{2,1,0:T(8,128)(2,1)S(1)}, u32[]{:S(2)}, u32[]{:S(2)}) async-start(bf16[16,48,128]{2,1,0:T(8,128)(2,1)} %get-tuple-element.126), calls=%async_computation | async-start | bytes 393216 | tf_op jit(solution)/shard_map/all_to_all | solution.py:996
  17.6 14.4 %collective-permute-start.3 = (bf16[512,256]{1,0:T(8,128)(2,1)S(1)}, bf16[512,256]{1,0:T(8,128)(2,1)S(1)}, u32[]{:S(2)}, u32[]{:S(2)}) collective-permute-start(bf16[512,256]{1,0:T(8,128)(2,1)S(1)} %copy-done.24), channel_id=1, source_target_pairs={{0,1},{1,0},{2,3},{3,2},{4,5},{5,4},{6,7},{7,6},{8,9},{9,8},{10,11... | collective-permute-start | bytes 786440 | tf_op jit(solution)/shard_map/ppermute | solution.py:992
  17.8 20.9 %collective-permute-start.4 = (bf16[256,512]{1,0:T(8,128)(2,1)S(1)}, bf16[256,512]{1,0:T(8,128)(2,1)S(1)}, u32[]{:S(2)}, u32[]{:S(2)}) collective-permute-start(bf16[256,512]{1,0:T(8,128)(2,1)S(1)} %copy-done.23), channel_id=1, source_target_pairs={{0,1},{1,0},{2,3},{3,2},{4,5},{5,4},{6,7},{7,6},{8,9},{9,8},{10,11... | collective-permute-start | bytes 786440 | tf_op jit(solution)/shard_map/ppermute | solution.py:992
  28.2 12.2 %all-to-all-start.1 = ((bf16[16,48,128]{2,1,0:T(8,128)(2,1)}), bf16[16,48,128]{2,1,0:T(8,128)(2,1)S(1)}, u32[]{:S(2)}, u32[]{:S(2)}) async-start(bf16[16,48,128]{2,1,0:T(8,128)(2,1)} %get-tuple-element.127), calls=%async_computation.1 | async-start | bytes 393216 | tf_op jit(solution)/shard_map/all_to_all | solution.py:996
  60.2 35.8 %collective-permute-start.16 = (bf16[512,512]{1,0:T(8,128)(2,1)S(1)}, bf16[512,512]{1,0:T(8,128)(2,1)S(1)}, u32[]{:S(2)}, u32[]{:S(2)}) collective-permute-start(bf16[512,512]{1,0:T(8,128)(2,1)S(1)} %copy-done.10), channel_id=1, source_target_pairs={{0,1},{1,0},{2,3},{3,2},{4,5},{5,4},{6,7},{7,6},{8,9},{9,8},{10,11... | collective-permute-start | bytes 1572872 | tf_op jit(solution)/shard_map/ppermute | solution.py:992
  60.7 14.2 %all-to-all-start.2 = ((bf16[16,48,128]{2,1,0:T(8,128)(2,1)}), bf16[16,48,128]{2,1,0:T(8,128)(2,1)S(1)}, u32[]{:S(2)}, u32[]{:S(2)}) async-start(bf16[16,48,128]{2,1,0:T(8,128)(2,1)} %get-tuple-element.138), calls=%async_computation.2 | async-start | bytes 393216 | tf_op jit(solution)/shard_map/all_to_all | solution.py:996
  65.9 37.8 %collective-permute-start.21 = (bf16[512,512]{1,0:T(8,128)(2,1)}, bf16[512,512]{1,0:T(8,128)(2,1)S(1)}, u32[]{:S(2)}, u32[]{:S(2)}) collective-permute-start(bf16[512,512]{1,0:T(8,128)(2,1)} %get-tuple-element.156.refs_18_.refs_11_), channel_id=1, source_target_pairs={{0,1},{1,0},{2,3},{3,2},{4,5},{5,4},{6,7},{7,6},{8,9},{9,8},{10,11... | collective-permute-start | bytes 1572872 | tf_op jit(solution)/shard_map/ppermute | solution.py:992
  66.0 37.2 %collective-permute-start.20 = (bf16[512,256]{1,0:T(8,128)(2,1)}, bf16[512,256]{1,0:T(8,128)(2,1)S(1)}, u32[]{:S(2)}, u32[]{:S(2)}) collective-permute-start(bf16[512,256]{1,0:T(8,128)(2,1)} %get-tuple-element.175), channel_id=1, source_target_pairs={{0,1},{1,0},{2,3},{3,2},{4,5},{5,4},{6,7},{7,6},{8,9},{9,8},{10,11... | collective-permute-start | bytes 786440 | tf_op jit(solution)/shard_map/ppermute | solution.py:992
  77.8 18.3 %all-to-all-start.3 = ((bf16[16,48,128]{2,1,0:T(8,128)(2,1)}), bf16[16,48,128]{2,1,0:T(8,128)(2,1)S(1)}, u32[]{:S(2)}, u32[]{:S(2)}) async-start(bf16[16,48,128]{2,1,0:T(8,128)(2,1)} %get-tuple-element.145), calls=%async_computation.3 | async-start | bytes 393216 | tf_op jit(solution)/shard_map/all_to_all | solution.py:996
  84.5 19.3 %collective-permute-start.12 = (bf16[512,512]{1,0:T(8,128)(2,1)}, bf16[512,512]{1,0:T(8,128)(2,1)S(1)}, u32[]{:S(2)}, u32[]{:S(2)}) collective-permute-start(bf16[512,512]{1,0:T(8,128)(2,1)} %get-tuple-element.162), channel_id=1, source_target_pairs={{0,2},{2,0},{4,6},{6,4},{8,10},{10,8},{12,14},{14,12},{16,18},{18,... | collective-permute-start | bytes 1572872 | tf_op jit(solution)/shard_map/ppermute | solution.py:1005
  86.6 17.7 %collective-permute-start.13 = (bf16[512,512]{1,0:T(8,128)(2,1)}, bf16[512,512]{1,0:T(8,128)(2,1)S(1)}, u32[]{:S(2)}, u32[]{:S(2)}) collective-permute-start(bf16[512,512]{1,0:T(8,128)(2,1)} %get-tuple-element.164), channel_id=1, source_target_pairs={{0,4},{2,6},{4,0},{6,2},{8,12},{10,14},{12,8},{14,10},{16,20},{18,... | collective-permute-start | bytes 1572872 | tf_op jit(solution)/shard_map/ppermute | solution.py:1005
  96.0 9.3 %collective-permute-start.17 = (bf16[512,256]{1,0:T(8,128)(2,1)}, bf16[512,256]{1,0:T(8,128)(2,1)S(1)}, u32[]{:S(2)}, u32[]{:S(2)}) collective-permute-start(bf16[512,256]{1,0:T(8,128)(2,1)} %get-tuple-element.155.refs_9_), channel_id=1, source_target_pairs={{0,1},{1,0},{2,3},{3,2},{4,5},{5,4},{6,7},{7,6},{8,9},{9,8},{10,11... | collective-permute-start | bytes 786440 | tf_op jit(solution)/shard_map/ppermute | solution.py:992
  103.9 14.7 %collective-permute-start.7 = (bf16[512,512]{1,0:T(8,128)(2,1)S(1)}, bf16[512,512]{1,0:T(8,128)(2,1)S(1)}, u32[]{:S(2)}, u32[]{:S(2)}) collective-permute-start(bf16[512,512]{1,0:T(8,128)(2,1)S(1)} %copy-done), channel_id=1, source_target_pairs={{0,1},{1,0},{2,3},{3,2},{4,5},{5,4},{6,7},{7,6},{8,9},{9,8},{10,11... | collective-permute-start | bytes 1572872 | tf_op jit(solution)/shard_map/ppermute | solution.py:992
  105.3 8.7 %collective-permute-start.14 = (bf16[256,512]{1,0:T(8,128)(2,1)S(1)}, bf16[256,512]{1,0:T(8,128)(2,1)S(1)}, u32[]{:S(2)}, u32[]{:S(2)}) collective-permute-start(bf16[256,512]{1,0:T(8,128)(2,1)S(1)} %get-tuple-element.167), channel_id=1, source_target_pairs={{0,4},{2,6},{4,0},{6,2},{8,12},{10,14},{12,8},{14,10},{16,20},{18,... | collective-permute-start | bytes 786440 | tf_op jit(solution)/shard_map/ppermute | solution.py:1005
  106.3 8.3 %collective-permute-start.15 = (bf16[256,512]{1,0:T(8,128)(2,1)S(1)}, bf16[256,512]{1,0:T(8,128)(2,1)S(1)}, u32[]{:S(2)}, u32[]{:S(2)}) collective-permute-start(bf16[256,512]{1,0:T(8,128)(2,1)S(1)} %get-tuple-element.169), channel_id=1, source_target_pairs={{0,2},{2,0},{4,6},{6,4},{8,10},{10,8},{12,14},{14,12},{16,18},{18,... | collective-permute-start | bytes 786440 | tf_op jit(solution)/shard_map/ppermute | solution.py:1005
  106.9 13.5 %collective-permute-start.11 = (bf16[512,512]{1,0:T(8,128)(2,1)S(1)}, bf16[512,512]{1,0:T(8,128)(2,1)S(1)}, u32[]{:S(2)}, u32[]{:S(2)}) collective-permute-start(bf16[512,512]{1,0:T(8,128)(2,1)S(1)} %copy-done.1), channel_id=1, source_target_pairs={{0,1},{1,0},{2,3},{3,2},{4,5},{5,4},{6,7},{7,6},{8,9},{9,8},{10,11... | collective-permute-start | bytes 1572872 | tf_op jit(solution)/shard_map/ppermute | solution.py:992
  116.9 15.2 %collective-permute-start.23 = (bf16[272,512]{1,0:T(8,128)(2,1)S(1)}, bf16[272,512]{1,0:T(8,128)(2,1)S(1)}, u32[]{:S(2)}, u32[]{:S(2)}) collective-permute-start(bf16[272,512]{1,0:T(8,128)(2,1)S(1)} %get-tuple-element.184), channel_id=1, source_target_pairs={{0,2},{2,0},{4,6},{6,4},{8,10},{10,8},{12,14},{14,12},{16,18},{18,... | collective-permute-start | bytes 835592 | tf_op jit(solution)/shard_map/ppermute | solution.py:1005
  117.5 14.6 %collective-permute-start.24 = (bf16[272,512]{1,0:T(8,128)(2,1)S(1)}, bf16[272,512]{1,0:T(8,128)(2,1)S(1)}, u32[]{:S(2)}, u32[]{:S(2)}) collective-permute-start(bf16[272,512]{1,0:T(8,128)(2,1)S(1)} %get-tuple-element.185), channel_id=1, source_target_pairs={{0,4},{2,6},{4,0},{6,2},{8,12},{10,14},{12,8},{14,10},{16,20},{18,... | collective-permute-start | bytes 835592 | tf_op jit(solution)/shard_map/ppermute | solution.py:1005
  118.6 13.5 %collective-permute-start.25 = (bf16[272,512]{1,0:T(8,128)(2,1)S(1)}, bf16[272,512]{1,0:T(8,128)(2,1)S(1)}, u32[]{:S(2)}, u32[]{:S(2)}) collective-permute-start(bf16[272,512]{1,0:T(8,128)(2,1)S(1)} %get-tuple-element.186), channel_id=1, source_target_pairs={{0,6},{2,4},{4,2},{6,0},{8,14},{10,12},{12,10},{14,8},{16,22},{18,... | collective-permute-start | bytes 835592 | tf_op jit(solution)/shard_map/ppermute | solution.py:1005
  131.2 14.4 %collective-permute-start.34 = (bf16[128,512]{1,0:T(8,128)(2,1)S(1)}, bf16[128,512]{1,0:T(8,128)(2,1)S(1)}, u32[]{:S(2)}, u32[]{:S(2)}) collective-permute-start(bf16[128,512]{1,0:T(8,128)(2,1)S(1)} %get-tuple-element.200.refs_1_), channel_id=1, source_target_pairs={{0,16},{2,18},{4,20},{6,22},{8,24},{10,26},{12,28},{14,30},{16,0},... | collective-permute-start | bytes 393224 | tf_op jit(solution)/shard_map/ppermute | solution.py:1296
  137.3 7.7 %collective-permute-start.29 = (bf16[80,512]{1,0:T(8,128)(2,1)S(1)}, bf16[80,512]{1,0:T(8,128)(2,1)S(1)}, u32[]{:S(2)}, u32[]{:S(2)}) collective-permute-start(bf16[80,512]{1,0:T(8,128)(2,1)S(1)} %get-tuple-element.196), channel_id=1, source_target_pairs={{0,16},{2,18},{4,20},{6,22},{8,24},{10,26},{12,28},{14,30},{16,0},... | collective-permute-start | bytes 245768 | tf_op jit(solution)/shard_map/ppermute | solution.py:1005
  137.3 7.7 %collective-permute-start.30 = (bf16[80,512]{1,0:T(8,128)(2,1)S(1)}, bf16[80,512]{1,0:T(8,128)(2,1)S(1)}, u32[]{:S(2)}, u32[]{:S(2)}) collective-permute-start(bf16[80,512]{1,0:T(8,128)(2,1)S(1)} %get-tuple-element.197), channel_id=1, source_target_pairs={{0,24},{2,26},{4,28},{6,30},{8,16},{10,18},{12,20},{14,22},{16,8},... | collective-permute-start | bytes 245768 | tf_op jit(solution)/shard_map/ppermute | solution.py:1005
  153.5 13.5 %collective-permute-start.40 = (bf16[512,512]{1,0:T(8,128)(2,1)S(1)}, bf16[512,512]{1,0:T(8,128)(2,1)S(1)}, u32[]{:S(2)}, u32[]{:S(2)}) collective-permute-start(bf16[512,512]{1,0:T(8,128)(2,1)S(1)} %get-tuple-element.207.refs_1_), channel_id=1, source_target_pairs={{0,2},{2,0},{4,6},{6,4},{8,10},{10,8},{12,14},{14,12},{16,18},{18,... | collective-permute-start | bytes 1572872 | tf_op jit(solution)/shard_map/ppermute | solution.py:1005
  154.1 14.0 %collective-permute-start.41 = (bf16[512,512]{1,0:T(8,128)(2,1)S(1)}, bf16[512,512]{1,0:T(8,128)(2,1)S(1)}, u32[]{:S(2)}, u32[]{:S(2)}) collective-permute-start(bf16[512,512]{1,0:T(8,128)(2,1)S(1)} %get-tuple-element.207.refs_1_), channel_id=1, source_target_pairs={{0,4},{2,6},{4,0},{6,2},{8,12},{10,14},{12,8},{14,10},{16,20},{18,... | collective-permute-start | bytes 1572872 | tf_op jit(solution)/shard_map/ppermute | solution.py:1005
  160.0 9.7 %collective-permute-start.39 = (f32[8,128]{1,0:T(8,128)S(1)}, f32[8,128]{1,0:T(8,128)S(1)}, u32[]{:S(2)}, u32[]{:S(2)}) collective-permute-start(f32[8,128]{1,0:T(8,128)S(1)} %copy-done.8), channel_id=1, source_target_pairs={{0,1},{1,0},{2,3},{3,2},{4,5},{5,4},{6,7},{7,6},{8,9},{9,8},{10,11... | collective-permute-start | bytes 12296 | tf_op jit(solution)/shard_map/ppermute | solution.py:992
  164.6 9.3 %collective-permute-start.36 = (bf16[256,512]{1,0:T(8,128)(2,1)S(1)}, bf16[256,512]{1,0:T(8,128)(2,1)S(1)}, u32[]{:S(2)}, u32[]{:S(2)}) collective-permute-start(bf16[256,512]{1,0:T(8,128)(2,1)S(1)} %get-tuple-element.205.refs_1_), channel_id=1, source_target_pairs={{0,2},{2,0},{4,6},{6,4},{8,10},{10,8},{12,14},{14,12},{16,18},{18,... | collective-permute-start | bytes 786440 | tf_op jit(solution)/shard_map/ppermute | solution.py:1005
  166.1 12.5 %collective-permute-start.37 = (bf16[256,512]{1,0:T(8,128)(2,1)S(1)}, bf16[256,512]{1,0:T(8,128)(2,1)S(1)}, u32[]{:S(2)}, u32[]{:S(2)}) collective-permute-start(bf16[256,512]{1,0:T(8,128)(2,1)S(1)} %get-tuple-element.205.refs_1_), channel_id=1, source_target_pairs={{0,4},{2,6},{4,0},{6,2},{8,12},{10,14},{12,8},{14,10},{16,20},{18,... | collective-permute-start | bytes 786440 | tf_op jit(solution)/shard_map/ppermute | solution.py:1005
  167.0 12.7 %collective-permute-start.38 = (bf16[256,512]{1,0:T(8,128)(2,1)S(1)}, bf16[256,512]{1,0:T(8,128)(2,1)S(1)}, u32[]{:S(2)}, u32[]{:S(2)}) collective-permute-start(bf16[256,512]{1,0:T(8,128)(2,1)S(1)} %get-tuple-element.205.refs_1_), channel_id=1, source_target_pairs={{0,6},{2,4},{4,2},{6,0},{8,14},{10,12},{12,10},{14,8},{16,22},{18,... | collective-permute-start | bytes 786440 | tf_op jit(solution)/shard_map/ppermute | solution.py:1005
  168.2 13.6 %collective-permute-start.42 = (bf16[256,512]{1,0:T(8,128)(2,1)S(1)}, bf16[256,512]{1,0:T(8,128)(2,1)S(1)}, u32[]{:S(2)}, u32[]{:S(2)}) collective-permute-start(bf16[256,512]{1,0:T(8,128)(2,1)S(1)} %get-tuple-element.224), channel_id=1, source_target_pairs={{0,2},{2,0},{4,6},{6,4},{8,10},{10,8},{12,14},{14,12},{16,18},{18,... | collective-permute-start | bytes 786440 | tf_op jit(solution)/shard_map/ppermute | solution.py:1005
  169.7 12.3 %collective-permute-start.43 = (bf16[256,512]{1,0:T(8,128)(2,1)S(1)}, bf16[256,512]{1,0:T(8,128)(2,1)S(1)}, u32[]{:S(2)}, u32[]{:S(2)}) collective-permute-start(bf16[256,512]{1,0:T(8,128)(2,1)S(1)} %get-tuple-element.225), channel_id=1, source_target_pairs={{0,4},{2,6},{4,0},{6,2},{8,12},{10,14},{12,8},{14,10},{16,20},{18,... | collective-permute-start | bytes 786440 | tf_op jit(solution)/shard_map/ppermute | solution.py:1005
  (45 other events, 262.2 us)

commit v4 on v3

--- a/solution.py
+++ b/solution.py
@@ -340,8 +340,8 @@
     columns = [jnp.zeros((k, LANES), wide) for _ in range(2)]
     if not backward:
         for block in range(z.blocks):
-            rows_ref[0, block : block + 1, :] = held_ref[block, k : k + 16, :].astype(wide)[0:1]
-            rows_ref[1, block : block + 1, :] = held_ref[block, k : k + 16, :].astype(wide)[1:2]
+            rows_ref[0, block : block + 1, :] = held_ref[block].astype(wide)[k : k + 1]
+            rows_ref[1, block : block + 1, :] = held_ref[block].astype(wide)[k + 1 : k + 2]
         terms = [rows_ref[i].astype(low) for i in range(2)]
         columns = [dot_nt(pick, terms[0]) + dot_nt(pick, terms[1]) for pick in picks]
     run = jnp.zeros((k, LANES), wide)
@@ -1175,7 +1175,7 @@
             limit=10,
             after=after,
             held=(0,),
-            held_out=(0, 1),
+            held_out=(0,),
         )
 
     arriving = over_blocks(sent)

time: 184 us -> 184 us (level)
  no operation moved by 1% of the time
where the time goes in v4:
time: 184 us
  Pallas kernels  70.1 us (38%)
  starting transfers between devices  62.2 us (34%)
  waiting for transfers between devices  41 us (22%)
  local copies, waits for them, and re-layouts  8.32 us (5%)
    pallas_call x23, Pallas kernels, call(): pl.pallas_call(body, grid_spec=pltpu.PrefetchScalarGridSpec(num_scalar_pr...  70.1 us
    ppermute x20, starting transfers between devices, exchange(): return lax.ppermute(value, 'seq', [(i, i ^ other) for i in range(count)])  27.2 us
    all_to_all x4, starting transfers between devices, over_blocks(): return lax.all_to_all(value, 'seq', 0, 0)  23.7 us
    ppermute x20, waiting for transfers between devices, exchange(): return lax.ppermute(value, 'seq', [(i, i ^ other) for i in range(count)])  21.3 us
    ppermute x4, waiting for transfers between devices, far(): return lax.ppermute(value, 'seq', [(i, i ^ bit) for i in range(blocks)])  10.5 us
    all_to_all x4, waiting for transfers between devices, over_blocks(): return lax.all_to_all(value, 'seq', 0, 0)  8.85 us
    unnamed x58, local copies, waits for them, and re-layouts  6.43 us
    ppermute x4, starting transfers between devices, far(): return lax.ppermute(value, 'seq', [(i, i ^ bit) for i in range(blocks)])  6.37 us
  transfers between devices with their start and end apart: 48, of which 19 were waited for; matrix products, arithmetic and copies ran while one was open for 1% of the time, Pallas kernels for 27%

profile of v4, /device:TPU:0, one launch (start us, length us, event | category | flops | bytes accessed | tf_op | source)
XLA Modules:
  0.0 183.6 jit_solution(5419583561346206416)
XLA Ops:
  4.4 5.2 %shard_map.339 = (bf16[512,512]{1,0:T(8,128)(2,1)}, bf16[512,512]{1,0:T(8,128)(2,1)}, bf16[512,512]{1,0:T(8,128)(2,1)}, bf16[512,512]{1,0:T(8,128)(2,1)}, f32[51...) custom-call(s32[6]{0:T(128)} %stack.27.refs_0_, ...), custom_call_target="tpu_custom_call" | custom-call | flops 4000000000 | bytes 4695040 | tf_op jit(solution)/shard_map/pallas_call | solution.py:1057
  9.7 7.9 %all-to-all-start = ((bf16[16,48,128]{2,1,0:T(8,128)(2,1)}), bf16[16,48,128]{2,1,0:T(8,128)(2,1)S(1)}, u32[]{:S(2)}, u32[]{:S(2)}) async-start(bf16[16,48,128]{2,1,0:T(8,128)(2,1)} %get-tuple-element.126), calls=%async_computation | async-start | bytes 393216 | tf_op jit(solution)/shard_map/all_to_all | solution.py:996
  19.5 7.1 %all-to-all-done.refs_1_ = bf16[16,48,128]{2,1,0:T(8,128)(2,1)S(1)} async-done(((bf16[16,48,128]{2,1,0:T(8,128)(2,1)}), bf16[16,48,128]{2,1,0:T(8,128)(2,1)S(1)}, u32[]{:S(2)}, u32[]{:S(2)}) %all-to-all-start) | async-done | bytes 196640 | tf_op jit(solution)/shard_map/all_to_all | solution.py:996
  26.5 1.7 shard_map.340
  28.2 3.7 %all-to-all-start.1 = ((bf16[16,48,128]{2,1,0:T(8,128)(2,1)}), bf16[16,48,128]{2,1,0:T(8,128)(2,1)S(1)}, u32[]{:S(2)}, u32[]{:S(2)}) async-start(bf16[16,48,128]{2,1,0:T(8,128)(2,1)} %get-tuple-element.127), calls=%async_computation.1 | async-start | bytes 393216 | tf_op jit(solution)/shard_map/all_to_all | solution.py:996
  32.7 6.0 %shard_map.341 = (bf16[512,512]{1,0:T(8,128)(2,1)}, bf16[512,512]{1,0:T(8,128)(2,1)}, bf16[16,256,256]{2,1,0:T(8,128)(2,1)}, f32[512,512]{1,0:T(8,128)}, f32[512,128]{1,0:T(8,128)}, /*index=5*/f32[8,128]{1,0:T(8,128)}) custom-call(bf16[512,512]{1,0:T(8,128)(2,1)} %get-tuple-element.128.refs_0_.refs_1_, bf16[512,256]{1,0:T(8,128)(2,1)} %refs_10_.1, ...), custom_call_target="tpu_custom_call" | custom-call | flops 4000000000 | bytes 6840320 | tf_op jit(solution)/shard_map/pallas_call | solution.py:1057
  38.7 1.6 all-to-all-done.1.refs_1_.refs_0_
  41.4 18.1 %shard_map.342 = (bf16[512,512]{1,0:T(8,128)(2,1)}, bf16[512,1024]{1,0:T(8,128)(2,1)}, bf16[512,1024]{1,0:T(8,128)(2,1)}, bf16[512,1024]{1,0:T(8,128)(2,1)}, bf1...) custom-call(s32[6]{0:T(128)} %stack.27.refs_0_, ...), custom_call_target="tpu_custom_call" | custom-call | flops 12000000000 | bytes 16961536 | tf_op jit(solution)/shard_map/pallas_call | solution.py:1057
  60.7 5.3 %all-to-all-start.2 = ((bf16[16,48,128]{2,1,0:T(8,128)(2,1)}), bf16[16,48,128]{2,1,0:T(8,128)(2,1)S(1)}, u32[]{:S(2)}, u32[]{:S(2)}) async-start(bf16[16,48,128]{2,1,0:T(8,128)(2,1)} %get-tuple-element.138), calls=%async_computation.2 | async-start | bytes 393216 | tf_op jit(solution)/shard_map/all_to_all | solution.py:996
  66.8 7.9 %shard_map.343 = (bf16[512,512]{1,0:T(8,128)(2,1)}, bf16[512,512]{1,0:T(8,128)(2,1)}, bf16[512,512]{1,0:T(8,128)(2,1)}, bf16[512,512]{1,0:T(8,128)(2,1)}, f32[8,128]{1,0:T(8,128)}) custom-call(s32[6]{0:T(128)} %stack.27.refs_0_, bf16[512,1024]{1,0:T(8,128)(2,1)} %get-tuple-element.139.refs_1_, bf16[512,1024]{1,0:T(8,128)(2,1)} %collective-permute-done.8.refs_2_, ...), custom_call_target="tpu_custom_call" | custom-call | flops 4000000000 | bytes 9437184 | tf_op jit(solution)/shard_map/pallas_call | solution.py:1057
  75.5 1.7 shard_map.344
  77.8 6.7 %all-to-all-start.3 = ((bf16[16,48,128]{2,1,0:T(8,128)(2,1)}), bf16[16,48,128]{2,1,0:T(8,128)(2,1)S(1)}, u32[]{:S(2)}, u32[]{:S(2)}) async-start(bf16[16,48,128]{2,1,0:T(8,128)(2,1)} %get-tuple-element.145), calls=%async_computation.3 | async-start | bytes 393216 | tf_op jit(solution)/shard_map/all_to_all | solution.py:996
  84.5 2.0 %collective-permute-start.12 = (bf16[512,512]{1,0:T(8,128)(2,1)}, bf16[512,512]{1,0:T(8,128)(2,1)S(1)}, u32[]{:S(2)}, u32[]{:S(2)}) collective-permute-start(bf16[512,512]{1,0:T(8,128)(2,1)} %get-tuple-element.162), channel_id=1, source_target_pairs={{0,2},{2,0},{4,6},{6,4},{8,10},{10,8},{12,14},{14,12},{16,18},{18,... | collective-permute-start | bytes 1572872 | tf_op jit(solution)/shard_map/ppermute | solution.py:1005
  88.0 8.0 %shard_map.345 = (bf16[512,256]{1,0:T(8,128)(2,1)}, bf16[512,256]{1,0:T(8,128)(2,1)}, bf16[512,512]{1,0:T(8,128)(2,1)}, bf16[512,512]{1,0:T(8,128)(2,1)}, f32[8,512]{1,0:T(8,128)}, /*index=5*/f32[8,128]{1,0:T(8,128)}) custom-call(bf16[16,48,128]{2,1,0:T(8,128)(2,1)} %copy-done.18, bf16[16,256,256]{2,1,0:T(8,128)(2,1)} %get-tuple-element.147.refs_1_, ...), custom_call_target="tpu_custom_call" | custom-call | flops 6000000000 | bytes 7569408 | tf_op jit(solution)/shard_map/pallas_call | solution.py:1057
  96.8 6.3 %shard_map.346 = (bf16[512,256]{1,0:T(8,128)(2,1)}, bf16[512,256]{1,0:T(8,128)(2,1)}, bf16[512,256]{1,0:T(8,128)(2,1)}, bf16[512,256]{1,0:T(8,128)(2,1)}, bf16[5...) custom-call(s32[6]{0:T(128)} %stack.27.refs_0_, ...), custom_call_target="tpu_custom_call" | custom-call | flops 4000000000 | bytes 8439808 | tf_op jit(solution)/shard_map/pallas_call | solution.py:1057
  107.9 1.9 %shard_map.348 = (bf16[272,512]{1,0:T(8,128)(2,1)S(1)}, bf16[272,512]{1,0:T(8,128)(2,1)S(1)}, bf16[272,512]{1,0:T(8,128)(2,1)S(1)}, bf16[272,512]{1,0:T(8,128)(2,1)S(1)}, f32[8,128]{1,0:T(8,128)S(1)}) custom-call(s32[6]{0:T(128)S(1)} %copy-done.6, bf16[512,512]{1,0:T(8,128)(2,1)S(1)} %copy-done.10, bf16[512,512]{1,0:T(8,128)(2,1)S(1)} %collective-permute-done.16.refs_2_, ...), custom_call_target="tpu_custom_call" | custom-call | flops 2000000000 | bytes 5373952 | tf_op jit(solution)/shard_map/pallas_call | solution.py:1057
  109.8 4.2 %collective-permute-done.14.refs_2_ = bf16[256,512]{1,0:T(8,128)(2,1)S(1)} collective-permute-done((bf16[256,512]{1,0:T(8,128)(2,1)S(1)}, bf16[256,512]{1,0:T(8,128)(2,1)S(1)}, u32[]{:S(2)}, u32[]{:S(2)}) %collective-permute-start.14) | collective-permute-done | bytes 262176 | tf_op jit(solution)/shard_map/ppermute | solution.py:1005
  118.6 1.8 collective-permute-start.25
  120.4 2.4 %shard_map.350 = (bf16[4,256,512]{2,1,0:T(8,128)(2,1)}, f32[4,256,512]{2,1,0:T(8,128)}, f32[8,128]{1,0:T(8,128)S(1)}) custom-call(s32[6]{0:T(128)S(1)} %copy-done.6, bf16[512,512]{1,0:T(8,128)(2,1)S(1)} %copy-done, bf16[512,512]{1,0:T(8,128)(2,1)S(1)} %collective-permute-done.7.refs_2_, bf16[512,512]{1,0:T(8,128)(2,1)S(1)} %copy-done.1, ...), custom_call_target="tpu_custom_call" | custom-call | flops 1000000 | bytes 5242880 | tf_op jit(solution)/shard_map/pallas_call | solution.py:1057
  123.6 2.4 %collective-permute-start.27 = (bf16[128,512]{1,0:T(8,128)(2,1)S(1)}, bf16[128,512]{1,0:T(8,128)(2,1)S(1)}, u32[]{:S(2)}, u32[]{:S(2)}) collective-permute-start(bf16[128,512]{1,0:T(8,128)(2,1)S(1)} %get-tuple-element.191), channel_id=1, source_target_pairs={{0,16},{2,18},{4,20},{6,22},{8,24},{10,26},{12,28},{14,30},{16,0},... | collective-permute-start | bytes 393224 | tf_op jit(solution)/shard_map/ppermute | solution.py:1296
  126.0 5.1 %collective-permute-done.27.refs_1_ = bf16[128,512]{1,0:T(8,128)(2,1)S(1)} collective-permute-done((bf16[128,512]{1,0:T(8,128)(2,1)S(1)}, bf16[128,512]{1,0:T(8,128)(2,1)S(1)}, u32[]{:S(2)}, u32[]{:S(2)}) %collective-permute-start.27) | collective-permute-done | bytes 131104 | tf_op jit(solution)/shard_map/ppermute | solution.py:1296
  132.8 4.5 %collective-permute-start.28 = (bf16[80,512]{1,0:T(8,128)(2,1)S(1)}, bf16[80,512]{1,0:T(8,128)(2,1)S(1)}, u32[]{:S(2)}, u32[]{:S(2)}) collective-permute-start(bf16[80,512]{1,0:T(8,128)(2,1)S(1)} %get-tuple-element.195), channel_id=1, source_target_pairs={{0,8},{2,10},{4,12},{6,14},{8,0},{10,2},{12,4},{14,6},{16,24},{18,... | collective-permute-start | bytes 245768 | tf_op jit(solution)/shard_map/ppermute | solution.py:1005
  137.3 2.4 %collective-permute-start.30 = (bf16[80,512]{1,0:T(8,128)(2,1)S(1)}, bf16[80,512]{1,0:T(8,128)(2,1)S(1)}, u32[]{:S(2)}, u32[]{:S(2)}) collective-permute-start(bf16[80,512]{1,0:T(8,128)(2,1)S(1)} %get-tuple-element.197), channel_id=1, source_target_pairs={{0,24},{2,26},{4,28},{6,30},{8,16},{10,18},{12,20},{14,22},{16,8},... | collective-permute-start | bytes 245768 | tf_op jit(solution)/shard_map/ppermute | solution.py:1005
  140.0 4.9 %collective-permute-done.29.refs_3_ = bf16[80,512]{1,0:T(8,128)(2,1)S(1)} collective-permute-done((bf16[80,512]{1,0:T(8,128)(2,1)S(1)}, bf16[80,512]{1,0:T(8,128)(2,1)S(1)}, u32[]{:S(2)}, u32[]{:S(2)}) %collective-permute-start.29) | collective-permute-done | bytes 81952 | tf_op jit(solution)/shard_map/ppermute | solution.py:1005
  147.7 5.2 %collective-permute-done.35.refs_2_ = bf16[256,512]{1,0:T(8,128)(2,1)S(1)} collective-permute-done((bf16[256,512]{1,0:T(8,128)(2,1)S(1)}, bf16[256,512]{1,0:T(8,128)(2,1)S(1)}, u32[]{:S(2)}, u32[]{:S(2)}) %collective-permute-start.35) | collective-permute-done | bytes 262176 | tf_op jit(solution)/shard_map/ppermute | solution.py:1296
  155.3 1.7 collective-permute-start.31
  157.9 1.8 collective-permute-start.33
  160.0 2.6 %collective-permute-done.32.refs_3_ = bf16[64,512]{1,0:T(8,128)(2,1)S(1)} collective-permute-done((bf16[64,512]{1,0:T(8,128)(2,1)S(1)}, bf16[64,512]{1,0:T(8,128)(2,1)S(1)}, u32[]{:S(2)}, u32[]{:S(2)}) %collective-permute-start.32) | collective-permute-done | bytes 65568 | tf_op jit(solution)/shard_map/ppermute | solution.py:1005
  170.6 2.7 %shard_map.359 = (f32[1024,512]{1,0:T(8,128)}, f32[512,1024]{1,0:T(8,128)}, f32[8,128]{1,0:T(8,128)S(1)}) custom-call(s32[6]{0:T(128)S(1)} %copy-done.6, bf16[512,512]{1,0:T(8,128)(2,1)S(1)} %get-tuple-element.207.refs_1_, bf16[512,512]{1,0:T(8,128)(2,1)S(1)} %collective-permute-done.40.refs_1_.refs_2_, ...), custom_call_target="tpu_custom_call" | custom-call | flops 1000000 | bytes 5767168 | tf_op jit(solution)/shard_map/pallas_call | solution.py:1057
  173.9 4.7 %collective-permute-done.37.refs_3_ = bf16[256,512]{1,0:T(8,128)(2,1)S(1)} collective-permute-done((bf16[256,512]{1,0:T(8,128)(2,1)S(1)}, bf16[256,512]{1,0:T(8,128)(2,1)S(1)}, u32[]{:S(2)}, u32[]{:S(2)}) %collective-permute-start.37) | collective-permute-done | bytes 262176 | tf_op jit(solution)/shard_map/ppermute | solution.py:1005
  179.6 2.0 %shard_map.360 = (f32[512,256]{1,0:T(8,128)}, f32[512,256]{1,0:T(8,128)}, f32[512,256]{1,0:T(8,128)}, f32[256,512]{1,0:T(8,128)}, f32[1,512]{1,0:T(1,128)}, /*in...) custom-call(s32[6]{0:T(128)S(1)} %copy-done.6, ...), custom_call_target="tpu_custom_call" | custom-call | flops 1000000 | bytes 3206148 | tf_op jit(solution)/shard_map/pallas_call | solution.py:1057
  182.0 1.6 shard_map.361
  (149 shorter events, 41.1 us)
Async XLA Ops:
  2.5 37.9 %collective-permute-start.5 = (bf16[512,1024]{1,0:T(8,128)(2,1)}, bf16[512,1024]{1,0:T(8,128)(2,1)S(1)}, u32[]{:S(2)}, u32[]{:S(2)}) collective-permute-start(bf16[512,1024]{1,0:T(8,128)(2,1)} %refs_13_.1), channel_id=1, source_target_pairs={{0,1},{1,0},{2,3},{3,2},{4,5},{5,4},{6,7},{7,6},{8,9},{9,8},{10,11... | collective-permute-start | bytes 3145736 | tf_op jit(solution)/shard_map/ppermute | solution.py:992
  2.6 37.8 %collective-permute-start.6 = (bf16[1024,512]{1,0:T(8,128)(2,1)}, bf16[1024,512]{1,0:T(8,128)(2,1)}, u32[]{:S(2)}, u32[]{:S(2)}) collective-permute-start(bf16[1024,512]{1,0:T(8,128)(2,1)} %refs_17_.1), channel_id=1, source_target_pairs={{0,1},{1,0},{2,3},{3,2},{4,5},{5,4},{6,7},{7,6},{8,9},{9,8},{10,11... | collective-permute-start | bytes 3145736 | tf_op jit(solution)/shard_map/ppermute | solution.py:992
  9.7 16.9 %all-to-all-start = ((bf16[16,48,128]{2,1,0:T(8,128)(2,1)}), bf16[16,48,128]{2,1,0:T(8,128)(2,1)S(1)}, u32[]{:S(2)}, u32[]{:S(2)}) async-start(bf16[16,48,128]{2,1,0:T(8,128)(2,1)} %get-tuple-element.126), calls=%async_computation | async-start | bytes 393216 | tf_op jit(solution)/shard_map/all_to_all | solution.py:996
  17.6 14.4 %collective-permute-start.3 = (bf16[512,256]{1,0:T(8,128)(2,1)S(1)}, bf16[512,256]{1,0:T(8,128)(2,1)S(1)}, u32[]{:S(2)}, u32[]{:S(2)}) collective-permute-start(bf16[512,256]{1,0:T(8,128)(2,1)S(1)} %copy-done.24), channel_id=1, source_target_pairs={{0,1},{1,0},{2,3},{3,2},{4,5},{5,4},{6,7},{7,6},{8,9},{9,8},{10,11... | collective-permute-start | bytes 786440 | tf_op jit(solution)/shard_map/ppermute | solution.py:992
  17.8 20.9 %collective-permute-start.4 = (bf16[256,512]{1,0:T(8,128)(2,1)S(1)}, bf16[256,512]{1,0:T(8,128)(2,1)S(1)}, u32[]{:S(2)}, u32[]{:S(2)}) collective-permute-start(bf16[256,512]{1,0:T(8,128)(2,1)S(1)} %copy-done.23), channel_id=1, source_target_pairs={{0,1},{1,0},{2,3},{3,2},{4,5},{5,4},{6,7},{7,6},{8,9},{9,8},{10,11... | collective-permute-start | bytes 786440 | tf_op jit(solution)/shard_map/ppermute | solution.py:992
  28.2 12.2 %all-to-all-start.1 = ((bf16[16,48,128]{2,1,0:T(8,128)(2,1)}), bf16[16,48,128]{2,1,0:T(8,128)(2,1)S(1)}, u32[]{:S(2)}, u32[]{:S(2)}) async-start(bf16[16,48,128]{2,1,0:T(8,128)(2,1)} %get-tuple-element.127), calls=%async_computation.1 | async-start | bytes 393216 | tf_op jit(solution)/shard_map/all_to_all | solution.py:996
  60.2 35.8 %collective-permute-start.16 = (bf16[512,512]{1,0:T(8,128)(2,1)S(1)}, bf16[512,512]{1,0:T(8,128)(2,1)S(1)}, u32[]{:S(2)}, u32[]{:S(2)}) collective-permute-start(bf16[512,512]{1,0:T(8,128)(2,1)S(1)} %copy-done.10), channel_id=1, source_target_pairs={{0,1},{1,0},{2,3},{3,2},{4,5},{5,4},{6,7},{7,6},{8,9},{9,8},{10,11... | collective-permute-start | bytes 1572872 | tf_op jit(solution)/shard_map/ppermute | solution.py:992
  60.7 14.2 %all-to-all-start.2 = ((bf16[16,48,128]{2,1,0:T(8,128)(2,1)}), bf16[16,48,128]{2,1,0:T(8,128)(2,1)S(1)}, u32[]{:S(2)}, u32[]{:S(2)}) async-start(bf16[16,48,128]{2,1,0:T(8,128)(2,1)} %get-tuple-element.138), calls=%async_computation.2 | async-start | bytes 393216 | tf_op jit(solution)/shard_map/all_to_all | solution.py:996
  65.9 37.8 %collective-permute-start.21 = (bf16[512,512]{1,0:T(8,128)(2,1)}, bf16[512,512]{1,0:T(8,128)(2,1)S(1)}, u32[]{:S(2)}, u32[]{:S(2)}) collective-permute-start(bf16[512,512]{1,0:T(8,128)(2,1)} %get-tuple-element.156.refs_18_.refs_11_), channel_id=1, source_target_pairs={{0,1},{1,0},{2,3},{3,2},{4,5},{5,4},{6,7},{7,6},{8,9},{9,8},{10,11... | collective-permute-start | bytes 1572872 | tf_op jit(solution)/shard_map/ppermute | solution.py:992
  66.0 37.2 %collective-permute-start.20 = (bf16[512,256]{1,0:T(8,128)(2,1)}, bf16[512,256]{1,0:T(8,128)(2,1)S(1)}, u32[]{:S(2)}, u32[]{:S(2)}) collective-permute-start(bf16[512,256]{1,0:T(8,128)(2,1)} %get-tuple-element.175), channel_id=1, source_target_pairs={{0,1},{1,0},{2,3},{3,2},{4,5},{5,4},{6,7},{7,6},{8,9},{9,8},{10,11... | collective-permute-start | bytes 786440 | tf_op jit(solution)/shard_map/ppermute | solution.py:992
  77.8 18.3 %all-to-all-start.3 = ((bf16[16,48,128]{2,1,0:T(8,128)(2,1)}), bf16[16,48,128]{2,1,0:T(8,128)(2,1)S(1)}, u32[]{:S(2)}, u32[]{:S(2)}) async-start(bf16[16,48,128]{2,1,0:T(8,128)(2,1)} %get-tuple-element.145), calls=%async_computation.3 | async-start | bytes 393216 | tf_op jit(solution)/shard_map/all_to_all | solution.py:996
  84.5 19.3 %collective-permute-start.12 = (bf16[512,512]{1,0:T(8,128)(2,1)}, bf16[512,512]{1,0:T(8,128)(2,1)S(1)}, u32[]{:S(2)}, u32[]{:S(2)}) collective-permute-start(bf16[512,512]{1,0:T(8,128)(2,1)} %get-tuple-element.162), channel_id=1, source_target_pairs={{0,2},{2,0},{4,6},{6,4},{8,10},{10,8},{12,14},{14,12},{16,18},{18,... | collective-permute-start | bytes 1572872 | tf_op jit(solution)/shard_map/ppermute | solution.py:1005
  86.6 17.7 %collective-permute-start.13 = (bf16[512,512]{1,0:T(8,128)(2,1)}, bf16[512,512]{1,0:T(8,128)(2,1)S(1)}, u32[]{:S(2)}, u32[]{:S(2)}) collective-permute-start(bf16[512,512]{1,0:T(8,128)(2,1)} %get-tuple-element.164), channel_id=1, source_target_pairs={{0,4},{2,6},{4,0},{6,2},{8,12},{10,14},{12,8},{14,10},{16,20},{18,... | collective-permute-start | bytes 1572872 | tf_op jit(solution)/shard_map/ppermute | solution.py:1005
  96.0 9.3 %collective-permute-start.17 = (bf16[512,256]{1,0:T(8,128)(2,1)}, bf16[512,256]{1,0:T(8,128)(2,1)S(1)}, u32[]{:S(2)}, u32[]{:S(2)}) collective-permute-start(bf16[512,256]{1,0:T(8,128)(2,1)} %get-tuple-element.155.refs_9_), channel_id=1, source_target_pairs={{0,1},{1,0},{2,3},{3,2},{4,5},{5,4},{6,7},{7,6},{8,9},{9,8},{10,11... | collective-permute-start | bytes 786440 | tf_op jit(solution)/shard_map/ppermute | solution.py:992
  103.9 14.7 %collective-permute-start.7 = (bf16[512,512]{1,0:T(8,128)(2,1)S(1)}, bf16[512,512]{1,0:T(8,128)(2,1)S(1)}, u32[]{:S(2)}, u32[]{:S(2)}) collective-permute-start(bf16[512,512]{1,0:T(8,128)(2,1)S(1)} %copy-done), channel_id=1, source_target_pairs={{0,1},{1,0},{2,3},{3,2},{4,5},{5,4},{6,7},{7,6},{8,9},{9,8},{10,11... | collective-permute-start | bytes 1572872 | tf_op jit(solution)/shard_map/ppermute | solution.py:992
  105.3 8.7 %collective-permute-start.14 = (bf16[256,512]{1,0:T(8,128)(2,1)S(1)}, bf16[256,512]{1,0:T(8,128)(2,1)S(1)}, u32[]{:S(2)}, u32[]{:S(2)}) collective-permute-start(bf16[256,512]{1,0:T(8,128)(2,1)S(1)} %get-tuple-element.167), channel_id=1, source_target_pairs={{0,4},{2,6},{4,0},{6,2},{8,12},{10,14},{12,8},{14,10},{16,20},{18,... | collective-permute-start | bytes 786440 | tf_op jit(solution)/shard_map/ppermute | solution.py:1005
  106.3 8.3 %collective-permute-start.15 = (bf16[256,512]{1,0:T(8,128)(2,1)S(1)}, bf16[256,512]{1,0:T(8,128)(2,1)S(1)}, u32[]{:S(2)}, u32[]{:S(2)}) collective-permute-start(bf16[256,512]{1,0:T(8,128)(2,1)S(1)} %get-tuple-element.169), channel_id=1, source_target_pairs={{0,2},{2,0},{4,6},{6,4},{8,10},{10,8},{12,14},{14,12},{16,18},{18,... | collective-permute-start | bytes 786440 | tf_op jit(solution)/shard_map/ppermute | solution.py:1005
  106.9 13.5 %collective-permute-start.11 = (bf16[512,512]{1,0:T(8,128)(2,1)S(1)}, bf16[512,512]{1,0:T(8,128)(2,1)S(1)}, u32[]{:S(2)}, u32[]{:S(2)}) collective-permute-start(bf16[512,512]{1,0:T(8,128)(2,1)S(1)} %copy-done.1), channel_id=1, source_target_pairs={{0,1},{1,0},{2,3},{3,2},{4,5},{5,4},{6,7},{7,6},{8,9},{9,8},{10,11... | collective-permute-start | bytes 1572872 | tf_op jit(solution)/shard_map/ppermute | solution.py:992
  116.9 15.2 %collective-permute-start.23 = (bf16[272,512]{1,0:T(8,128)(2,1)S(1)}, bf16[272,512]{1,0:T(8,128)(2,1)S(1)}, u32[]{:S(2)}, u32[]{:S(2)}) collective-permute-start(bf16[272,512]{1,0:T(8,128)(2,1)S(1)} %get-tuple-element.184), channel_id=1, source_target_pairs={{0,2},{2,0},{4,6},{6,4},{8,10},{10,8},{12,14},{14,12},{16,18},{18,... | collective-permute-start | bytes 835592 | tf_op jit(solution)/shard_map/ppermute | solution.py:1005
  117.5 14.6 %collective-permute-start.24 = (bf16[272,512]{1,0:T(8,128)(2,1)S(1)}, bf16[272,512]{1,0:T(8,128)(2,1)S(1)}, u32[]{:S(2)}, u32[]{:S(2)}) collective-permute-start(bf16[272,512]{1,0:T(8,128)(2,1)S(1)} %get-tuple-element.185), channel_id=1, source_target_pairs={{0,4},{2,6},{4,0},{6,2},{8,12},{10,14},{12,8},{14,10},{16,20},{18,... | collective-permute-start | bytes 835592 | tf_op jit(solution)/shard_map/ppermute | solution.py:1005
  118.6 13.5 %collective-permute-start.25 = (bf16[272,512]{1,0:T(8,128)(2,1)S(1)}, bf16[272,512]{1,0:T(8,128)(2,1)S(1)}, u32[]{:S(2)}, u32[]{:S(2)}) collective-permute-start(bf16[272,512]{1,0:T(8,128)(2,1)S(1)} %get-tuple-element.186), channel_id=1, source_target_pairs={{0,6},{2,4},{4,2},{6,0},{8,14},{10,12},{12,10},{14,8},{16,22},{18,... | collective-permute-start | bytes 835592 | tf_op jit(solution)/shard_map/ppermute | solution.py:1005
  131.2 14.4 %collective-permute-start.34 = (bf16[128,512]{1,0:T(8,128)(2,1)S(1)}, bf16[128,512]{1,0:T(8,128)(2,1)S(1)}, u32[]{:S(2)}, u32[]{:S(2)}) collective-permute-start(bf16[128,512]{1,0:T(8,128)(2,1)S(1)} %get-tuple-element.200.refs_1_), channel_id=1, source_target_pairs={{0,16},{2,18},{4,20},{6,22},{8,24},{10,26},{12,28},{14,30},{16,0},... | collective-permute-start | bytes 393224 | tf_op jit(solution)/shard_map/ppermute | solution.py:1296
  137.3 7.7 %collective-permute-start.29 = (bf16[80,512]{1,0:T(8,128)(2,1)S(1)}, bf16[80,512]{1,0:T(8,128)(2,1)S(1)}, u32[]{:S(2)}, u32[]{:S(2)}) collective-permute-start(bf16[80,512]{1,0:T(8,128)(2,1)S(1)} %get-tuple-element.196), channel_id=1, source_target_pairs={{0,16},{2,18},{4,20},{6,22},{8,24},{10,26},{12,28},{14,30},{16,0},... | collective-permute-start | bytes 245768 | tf_op jit(solution)/shard_map/ppermute | solution.py:1005
  137.3 7.7 %collective-permute-start.30 = (bf16[80,512]{1,0:T(8,128)(2,1)S(1)}, bf16[80,512]{1,0:T(8,128)(2,1)S(1)}, u32[]{:S(2)}, u32[]{:S(2)}) collective-permute-start(bf16[80,512]{1,0:T(8,128)(2,1)S(1)} %get-tuple-element.197), channel_id=1, source_target_pairs={{0,24},{2,26},{4,28},{6,30},{8,16},{10,18},{12,20},{14,22},{16,8},... | collective-permute-start | bytes 245768 | tf_op jit(solution)/shard_map/ppermute | solution.py:1005
  153.5 13.5 %collective-permute-start.40 = (bf16[512,512]{1,0:T(8,128)(2,1)S(1)}, bf16[512,512]{1,0:T(8,128)(2,1)S(1)}, u32[]{:S(2)}, u32[]{:S(2)}) collective-permute-start(bf16[512,512]{1,0:T(8,128)(2,1)S(1)} %get-tuple-element.207.refs_1_), channel_id=1, source_target_pairs={{0,2},{2,0},{4,6},{6,4},{8,10},{10,8},{12,14},{14,12},{16,18},{18,... | collective-permute-start | bytes 1572872 | tf_op jit(solution)/shard_map/ppermute | solution.py:1005
  154.1 14.0 %collective-permute-start.41 = (bf16[512,512]{1,0:T(8,128)(2,1)S(1)}, bf16[512,512]{1,0:T(8,128)(2,1)S(1)}, u32[]{:S(2)}, u32[]{:S(2)}) collective-permute-start(bf16[512,512]{1,0:T(8,128)(2,1)S(1)} %get-tuple-element.207.refs_1_), channel_id=1, source_target_pairs={{0,4},{2,6},{4,0},{6,2},{8,12},{10,14},{12,8},{14,10},{16,20},{18,... | collective-permute-start | bytes 1572872 | tf_op jit(solution)/shard_map/ppermute | solution.py:1005
  160.0 9.7 %collective-permute-start.39 = (f32[8,128]{1,0:T(8,128)S(1)}, f32[8,128]{1,0:T(8,128)S(1)}, u32[]{:S(2)}, u32[]{:S(2)}) collective-permute-start(f32[8,128]{1,0:T(8,128)S(1)} %copy-done.8), channel_id=1, source_target_pairs={{0,1},{1,0},{2,3},{3,2},{4,5},{5,4},{6,7},{7,6},{8,9},{9,8},{10,11... | collective-permute-start | bytes 12296 | tf_op jit(solution)/shard_map/ppermute | solution.py:992
  164.6 9.3 %collective-permute-start.36 = (bf16[256,512]{1,0:T(8,128)(2,1)S(1)}, bf16[256,512]{1,0:T(8,128)(2,1)S(1)}, u32[]{:S(2)}, u32[]{:S(2)}) collective-permute-start(bf16[256,512]{1,0:T(8,128)(2,1)S(1)} %get-tuple-element.205.refs_1_), channel_id=1, source_target_pairs={{0,2},{2,0},{4,6},{6,4},{8,10},{10,8},{12,14},{14,12},{16,18},{18,... | collective-permute-start | bytes 786440 | tf_op jit(solution)/shard_map/ppermute | solution.py:1005
  166.1 12.5 %collective-permute-start.37 = (bf16[256,512]{1,0:T(8,128)(2,1)S(1)}, bf16[256,512]{1,0:T(8,128)(2,1)S(1)}, u32[]{:S(2)}, u32[]{:S(2)}) collective-permute-start(bf16[256,512]{1,0:T(8,128)(2,1)S(1)} %get-tuple-element.205.refs_1_), channel_id=1, source_target_pairs={{0,4},{2,6},{4,0},{6,2},{8,12},{10,14},{12,8},{14,10},{16,20},{18,... | collective-permute-start | bytes 786440 | tf_op jit(solution)/shard_map/ppermute | solution.py:1005
  167.0 12.7 %collective-permute-start.38 = (bf16[256,512]{1,0:T(8,128)(2,1)S(1)}, bf16[256,512]{1,0:T(8,128)(2,1)S(1)}, u32[]{:S(2)}, u32[]{:S(2)}) collective-permute-start(bf16[256,512]{1,0:T(8,128)(2,1)S(1)} %get-tuple-element.205.refs_1_), channel_id=1, source_target_pairs={{0,6},{2,4},{4,2},{6,0},{8,14},{10,12},{12,10},{14,8},{16,22},{18,... | collective-permute-start | bytes 786440 | tf_op jit(solution)/shard_map/ppermute | solution.py:1005
  168.2 13.6 %collective-permute-start.42 = (bf16[256,512]{1,0:T(8,128)(2,1)S(1)}, bf16[256,512]{1,0:T(8,128)(2,1)S(1)}, u32[]{:S(2)}, u32[]{:S(2)}) collective-permute-start(bf16[256,512]{1,0:T(8,128)(2,1)S(1)} %get-tuple-element.224), channel_id=1, source_target_pairs={{0,2},{2,0},{4,6},{6,4},{8,10},{10,8},{12,14},{14,12},{16,18},{18,... | collective-permute-start | bytes 786440 | tf_op jit(solution)/shard_map/ppermute | solution.py:1005
  169.7 12.3 %collective-permute-start.43 = (bf16[256,512]{1,0:T(8,128)(2,1)S(1)}, bf16[256,512]{1,0:T(8,128)(2,1)S(1)}, u32[]{:S(2)}, u32[]{:S(2)}) collective-permute-start(bf16[256,512]{1,0:T(8,128)(2,1)S(1)} %get-tuple-element.225), channel_id=1, source_target_pairs={{0,4},{2,6},{4,0},{6,2},{8,12},{10,14},{12,8},{14,10},{16,20},{18,... | collective-permute-start | bytes 786440 | tf_op jit(solution)/shard_map/ppermute | solution.py:1005
  (45 other events, 262.2 us)
